TPU v7x, 32 devices: a whole 2x2x4 slice. The times are simulated.
32 devices in a mesh: dp: 8 (over y, x, core), tensor: 4 (over z).
Axes of the slice: x: 2, y: 2, z: 4, core: 2. Of those that a mesh axis runs over, the one named last changes fastest.
Arguments:
- inputs: bfloat16 [8192, 2048], P(('dp', 'tensor')), may hold values from -6 to 6
- cotangent: bfloat16 [8192, 2048], P(('dp', 'tensor')), may hold values from -6 to 6
- doc_lengths: int32 [8, 3], P('dp'), may hold values from 1 to 896, 1024 in all within a row
- norm_gains: float32 [2, 2048], replicated, may hold values from 0.5 to 1.5
- attn_weight: float32 [4, 2048, 2048], P(None, 'dp', 'tensor'), may hold values from -0.26516504 to 0.26516504
- mlp_weight: float32 [3, 2048, 8192], P(None, 'dp', 'tensor'), may hold values from -0.125 to 0.125
- gain_first: float32 [2, 2048], replicated, may hold values from -80 to 80
- attn_first: float32 [4, 2048, 2048], P(None, 'dp', 'tensor'), may hold values from -28 to 28
- mlp_first: float32 [3, 2048, 8192], P(None, 'dp', 'tensor'), may hold values from -32 to 32
- gain_second: float32 [2, 2048], replicated, may hold values from 737.28 to 2949.12
- attn_second: float32 [4, 2048, 2048], P(None, 'dp', 'tensor'), may hold values from 90.112 to 360.448
- mlp_second: float32 [3, 2048, 8192], P(None, 'dp', 'tensor'), may hold values from 131.072 to 524.288
Outputs:
- layer_out: bfloat16 [8192, 2048], P(('dp', 'tensor'))
- grad_in: float32 [8192, 2048], P(('dp', 'tensor'))
- gain_grad: float32 [2, 2048], replicated
- attn_grad: float32 [4, 2048, 2048], P(None, 'dp', 'tensor')
- mlp_grad: float32 [3, 2048, 8192], P(None, 'dp', 'tensor')
- gain_first_new: float32 [2, 2048], replicated
- attn_first_new: float32 [4, 2048, 2048], P(None, 'dp', 'tensor')
- mlp_first_new: float32 [3, 2048, 8192], P(None, 'dp', 'tensor')
- gain_second_new: float32 [2, 2048], replicated
- attn_second_new: float32 [4, 2048, 2048], P(None, 'dp', 'tensor')
- mlp_second_new: float32 [3, 2048, 8192], P(None, 'dp', 'tensor')
- gain_new: float32 [2, 2048], replicated
- attn_new: float32 [4, 2048, 2048], P(None, 'dp', 'tensor')
- mlp_new: float32 [3, 2048, 8192], P(None, 'dp', 'tensor')
Inputs may be any that keep to these rules, and one draw needn't show every extreme that they name: `doc_lengths`: each row sums to 1024, and its longest document has exactly 896 tokens.
All inputs are finite; a program needn't handle non-finite values.
Results may differ from a plain program's by a relative error of at most 0.015.
Values may be sent and summed in bfloat16 or wider, within the bound.
A program may use at most 320 MiB of HBM per device.

v0:
```python
import jax
import jax.numpy as jnp
from jax import lax
from jax.sharding import PartitionSpec as P

D = 2048
HEAD_DIM = 64
STEP = 10


EPS_NORM = 1e-05
ROPE_BASE = 130000.0
BETA_ONE = 0.9
BETA_TWO = 0.95
EPS_ADAM = 1e-08
WEIGHT_DECAY = 0.1
GAIN_RATE = 0.3
MASKED = -1e30


def doc_layout(lengths, seq_length):
    doc_ends = jnp.cumsum(lengths)
    starts = doc_ends - lengths
    places = jnp.arange(seq_length, dtype=jnp.int32)
    segment = jnp.sum((places[:, None] >= doc_ends[None, :]).astype(jnp.int32), axis=1)
    owners = segment[:, None] == jnp.arange(lengths.shape[0], dtype=jnp.int32)[None, :]
    position = places - jnp.sum(jnp.where(owners, starts[None, :], 0), axis=1)
    return (segment, position)


def rope_tables(position):
    half_dim = HEAD_DIM // 2
    frequencies = jnp.power(
        jnp.float32(ROPE_BASE), -2.0 * jnp.arange(half_dim, dtype=jnp.float32) / HEAD_DIM
    )
    angles = position.astype(jnp.float32)[:, None] * frequencies[None, :]
    return (jnp.cos(angles)[:, None, :], jnp.sin(angles)[:, None, :])


def rotate(field, cos_table, sine_table):
    half_dim = field.shape[-1] // 2
    first_half = field[..., :half_dim]
    second_half = field[..., half_dim:]
    return jnp.concatenate(
        [
            first_half * cos_table - second_half * sine_table,
            second_half * cos_table + first_half * sine_table,
        ],
        axis=-1,
    )


def rotate_back(gradient, cos_table, sine_table):
    half_dim = gradient.shape[-1] // 2
    first_half = gradient[..., :half_dim]
    second_half = gradient[..., half_dim:]
    return jnp.concatenate(
        [
            first_half * cos_table + second_half * sine_table,
            second_half * cos_table - first_half * sine_table,
        ],
        axis=-1,
    )


def norm_forward(field):
    inv_scale = lax.rsqrt(jnp.mean(field * field, axis=-1, keepdims=True) + EPS_NORM)
    return (field * inv_scale, inv_scale)


def norm_backward(gradient, normed, inv_scale, gain_row):
    scaled = gradient * gain_row
    field_grad = inv_scale * (scaled - normed * jnp.mean(scaled * normed, axis=-1, keepdims=True))
    return (field_grad, jnp.sum(gradient * normed, axis=0))


def dot_transposed(left, right):
    return lax.dot_general(
        left, right, (((1,), (1,)), ((), ())), preferred_element_type=jnp.float32
    )


def dot_over_rows(left, right):
    return lax.dot_general(
        left, right, (((0,), (0,)), ((), ())), preferred_element_type=jnp.float32
    )


def allowed_keys(seg_rows, pos_rows, segment, position):
    return (seg_rows[:, None] == segment[None, :]) & (position[None, :] <= pos_rows[:, None])


def attend_forward(
    query_block, seg_rows, pos_rows, key_rows, values, segment, position, score_scale
):
    raw_score = (
        jnp.einsum("bhd,khd->hbk", query_block, key_rows, preferred_element_type=jnp.float32)
        * score_scale
    )
    allowed = allowed_keys(seg_rows, pos_rows, segment, position)
    masked_score = jnp.where(allowed[None], raw_score, MASKED)
    row_peak = jnp.max(masked_score, axis=-1, keepdims=True)
    exp_score = jnp.exp(masked_score - row_peak)
    exp_total = jnp.sum(exp_score, axis=-1, keepdims=True)
    prob_low = (exp_score / exp_total).astype(jnp.bfloat16)
    result = jnp.einsum(
        "hbk,khd->bhd", prob_low, values, preferred_element_type=jnp.float32
    ).astype(jnp.bfloat16)
    return (result, (row_peak + jnp.log(exp_total))[..., 0])


def attend_backward(carry_sums, pieces, key_rows, values, segment, position, score_scale):
    key_sum, value_sum = carry_sums
    query_block, grad_block, log_total, seg_rows, pos_rows = pieces
    raw_score = (
        jnp.einsum("bhd,khd->hbk", query_block, key_rows, preferred_element_type=jnp.float32)
        * score_scale
    )
    allowed = allowed_keys(seg_rows, pos_rows, segment, position)
    probs = jnp.where(allowed[None], jnp.exp(raw_score - log_total[:, :, None]), 0.0)
    value_sum = value_sum + jnp.einsum(
        "hbk,bhd->khd", probs.astype(jnp.bfloat16), grad_block, preferred_element_type=jnp.float32
    )
    prob_grad = jnp.einsum("bhd,khd->hbk", grad_block, values, preferred_element_type=jnp.float32)
    score_grad = (probs * (prob_grad - jnp.sum(prob_grad * probs, axis=-1, keepdims=True))).astype(
        jnp.bfloat16
    )
    query_grad = (
        jnp.einsum("hbk,khd->bhd", score_grad, key_rows, preferred_element_type=jnp.float32)
        * score_scale
    )
    key_sum = (
        key_sum
        + jnp.einsum("hbk,bhd->khd", score_grad, query_block, preferred_element_type=jnp.float32)
        * score_scale
    )
    return ((key_sum, value_sum), query_grad)


def attn_rates():
    return jnp.array([1.0, 1.0, 1.0, 8.0**0.5], jnp.float32).reshape(4, 1, 1) * (0.5 * D ** (-0.5))


def adam_update(weight, gradient, moment_one, moment_two, step_rate):
    first_new = BETA_ONE * moment_one + (1.0 - BETA_ONE) * gradient
    second_new = BETA_TWO * moment_two + (1.0 - BETA_TWO) * gradient * gradient
    fix_one = 1.0 - BETA_ONE**STEP
    fix_two = 1.0 - BETA_TWO**STEP
    weight_new = weight - step_rate * (
        first_new / fix_one / (jnp.sqrt(second_new / fix_two) + EPS_ADAM) + WEIGHT_DECAY * weight
    )
    return (first_new, second_new, weight_new)


def local(
    inputs,
    cotangent,
    doc_lengths,
    norm_gains,
    attn_weight,
    mlp_weight,
    gain_first,
    attn_first,
    mlp_first,
    gain_second,
    attn_second,
    mlp_second,
):
    row_count = inputs.shape[0]
    seq_length = row_count * lax.axis_size("tensor")
    head_width = attn_weight.shape[2]
    head_count = head_width // HEAD_DIM
    segment, position = doc_layout(doc_lengths[0], seq_length)
    cos_table, sine_table = rope_tables(position)
    block_rows = min(512, seq_length)
    block_count = seq_length // block_rows
    seg_blocks = segment.reshape(block_count, block_rows)
    pos_blocks = position.reshape(block_count, block_rows)
    score_scale = HEAD_DIM ** (-0.5)
    layer_in = inputs.astype(jnp.float32)
    normed_one, inv_one = norm_forward(layer_in)
    first_in = lax.all_gather(
        (normed_one * norm_gains[0]).astype(jnp.bfloat16), "tensor", axis=0, tiled=True
    )
    attn_low = lax.all_gather(attn_weight.astype(jnp.bfloat16), "dp", axis=1, tiled=True)

    def project(matrix):
        return jnp.dot(first_in, matrix, preferred_element_type=jnp.float32).reshape(
            seq_length, head_count, HEAD_DIM
        )

    queries = rotate(project(attn_low[0]), cos_table, sine_table).astype(jnp.bfloat16)
    key_rows = rotate(project(attn_low[1]), cos_table, sine_table).astype(jnp.bfloat16)
    values = project(attn_low[2]).astype(jnp.bfloat16)
    query_blocks = queries.reshape(block_count, block_rows, head_count, HEAD_DIM)

    def forward_block(pieces):
        return attend_forward(
            pieces[0], pieces[1], pieces[2], key_rows, values, segment, position, score_scale
        )

    attended, log_totals = lax.map(forward_block, (query_blocks, seg_blocks, pos_blocks))
    attended = attended.reshape(seq_length, head_width)
    middle = layer_in + lax.psum_scatter(
        dot_transposed(attended, attn_low[3]), "tensor", scatter_dimension=0, tiled=True
    )
    normed_two, inv_two = norm_forward(middle)
    second_in = lax.all_gather(
        (normed_two * norm_gains[1]).astype(jnp.bfloat16), "tensor", axis=0, tiled=True
    )
    mlp_low = lax.all_gather(mlp_weight.astype(jnp.bfloat16), "dp", axis=1, tiled=True)
    gate_proj = jnp.dot(second_in, mlp_low[0], preferred_element_type=jnp.float32)
    up_proj = jnp.dot(second_in, mlp_low[1], preferred_element_type=jnp.float32)
    sigmoid_gate = jax.nn.sigmoid(gate_proj)
    hidden = (gate_proj * sigmoid_gate * up_proj).astype(jnp.bfloat16)
    layer_out = middle + lax.psum_scatter(
        dot_transposed(hidden, mlp_low[2]), "tensor", scatter_dimension=0, tiled=True
    )
    attn_back, mlp_back = (
        lax.all_gather(attn_weight.astype(jnp.bfloat16), "dp", axis=1, tiled=True),
        lax.all_gather(mlp_weight.astype(jnp.bfloat16), "dp", axis=1, tiled=True),
    )
    grad_out = lax.all_gather(cotangent, "tensor", axis=0, tiled=True)
    d_hidden = jnp.dot(grad_out, mlp_back[2], preferred_element_type=jnp.float32)
    down_grad = dot_over_rows(grad_out, hidden)
    d_gate = (
        d_hidden * up_proj * (sigmoid_gate * (1.0 + gate_proj * (1.0 - sigmoid_gate)))
    ).astype(jnp.bfloat16)
    d_up = (d_hidden * (gate_proj * sigmoid_gate)).astype(jnp.bfloat16)
    mlp_stack = jnp.stack(
        [dot_over_rows(second_in, d_gate), dot_over_rows(second_in, d_up), down_grad]
    )
    mlp_grad = lax.psum_scatter(mlp_stack, "dp", scatter_dimension=1, tiled=True)
    d_second = lax.psum_scatter(
        dot_transposed(d_gate, mlp_back[0]) + dot_transposed(d_up, mlp_back[1]),
        "tensor",
        scatter_dimension=0,
        tiled=True,
    )
    d_middle, gain_two = norm_backward(d_second, normed_two, inv_two, norm_gains[1])
    d_middle = d_middle + cotangent.astype(jnp.float32)
    d_attn = lax.all_gather(d_middle.astype(jnp.bfloat16), "tensor", axis=0, tiled=True)
    out_proj_grad = dot_over_rows(d_attn, attended)
    d_attended = jnp.dot(d_attn, attn_back[3], preferred_element_type=jnp.float32).astype(
        jnp.bfloat16
    )
    grad_blocks = d_attended.reshape(block_count, block_rows, head_count, HEAD_DIM)

    def back_block(carry_sums, pieces):
        return attend_backward(carry_sums, pieces, key_rows, values, segment, position, score_scale)

    empty_sum = jnp.zeros((seq_length, head_count, HEAD_DIM), jnp.float32)
    block_sums, query_grad = lax.scan(
        back_block,
        (empty_sum, empty_sum),
        (query_blocks, grad_blocks, log_totals, seg_blocks, pos_blocks),
    )
    key_grad, value_grad = block_sums
    query_raw = (
        rotate_back(query_grad.reshape(seq_length, head_count, HEAD_DIM), cos_table, sine_table)
        .reshape(seq_length, head_width)
        .astype(jnp.bfloat16)
    )
    key_raw = (
        rotate_back(key_grad, cos_table, sine_table)
        .reshape(seq_length, head_width)
        .astype(jnp.bfloat16)
    )
    value_raw = value_grad.reshape(seq_length, head_width).astype(jnp.bfloat16)
    attn_stack = jnp.stack(
        [
            dot_over_rows(first_in, query_raw),
            dot_over_rows(first_in, key_raw),
            dot_over_rows(first_in, value_raw),
            out_proj_grad,
        ]
    )
    attn_grad = lax.psum_scatter(attn_stack, "dp", scatter_dimension=1, tiled=True)
    d_first = lax.psum_scatter(
        dot_transposed(query_raw, attn_back[0])
        + dot_transposed(key_raw, attn_back[1])
        + dot_transposed(value_raw, attn_back[2]),
        "tensor",
        scatter_dimension=0,
        tiled=True,
    )
    d_input, gain_one = norm_backward(d_first, normed_one, inv_one, norm_gains[0])
    grad_in = d_input + d_middle
    gain_grad = lax.psum(jnp.stack([gain_one, gain_two]), ("dp", "tensor"))
    gain_first_new, gain_second_new, gain_new = adam_update(
        norm_gains, gain_grad, gain_first, gain_second, GAIN_RATE
    )
    attn_first_new, attn_second_new, attn_new = adam_update(
        attn_weight, attn_grad, attn_first, attn_second, attn_rates()
    )
    mlp_first_new, mlp_second_new, mlp_new = adam_update(
        mlp_weight, mlp_grad, mlp_first, mlp_second, 0.5 * D ** (-0.5)
    )
    return (
        layer_out.astype(jnp.bfloat16),
        grad_in,
        gain_grad,
        attn_grad,
        mlp_grad,
        gain_first_new,
        attn_first_new,
        mlp_first_new,
        gain_second_new,
        attn_second_new,
        mlp_second_new,
        gain_new,
        attn_new,
        mlp_new,
    )


def solution(mesh):
    placed = (
        P(("dp", "tensor"), None),
        P(("dp", "tensor"), None),
        P("dp", None),
        P(),
        P(None, "dp", "tensor"),
        P(None, "dp", "tensor"),
        P(),
        P(None, "dp", "tensor"),
        P(None, "dp", "tensor"),
        P(),
        P(None, "dp", "tensor"),
        P(None, "dp", "tensor"),
    )
    return jax.shard_map(
        local,
        mesh=mesh,
        in_specs=placed,
        out_specs=(
            P(("dp", "tensor"), None),
            P(("dp", "tensor"), None),
            P(),
            P(None, "dp", "tensor"),
            P(None, "dp", "tensor"),
            P(),
            P(None, "dp", "tensor"),
            P(None, "dp", "tensor"),
            P(),
            P(None, "dp", "tensor"),
            P(None, "dp", "tensor"),
            P(),
            P(None, "dp", "tensor"),
            P(None, "dp", "tensor"),
        ),
        check_vma=False,
    )
```

profile of v0, /device:TPU:0, one launch (start us, length us, event | category | flops | bytes accessed | tf_op | source)
XLA Modules:
  0.0 1799.2 jit_solution(9624020400183222324)
XLA Ops:
  14.0 53.7 %all-gather.9.cloned.1.call-done = bf16[4,2048,512]{2,1,0:T(8,128)(2,1)} async-done(((bf16[4,256,512]{2,1,0:T(8,128)(2,1)}), bf16[4,2048,512]{2,1,0:T(8,128)(2,1)}) %all-gather.9.cloned.1.call-update) | async-done | bytes 8388624 | tf_op jit(solution)/shard_map/all_gather | solution.py:185
  83.2 67.4 %all-gather.7.cloned.1.call-done = bf16[1024,2048]{1,0:T(8,128)(2,1)} async-done(((bf16[256,2048]{1,0:T(8,128)(2,1)}), bf16[1024,2048]{1,0:T(8,128)(2,1)}) %all-gather.7.cloned.1.call-update) | async-done | bytes 4194320 | tf_op jit(solution)/shard_map/all_gather | solution.py:182
  162.4 28.5 %while.27 = (s32[]{:T(128)}, bf16[2,512,8,64]{1,3,2,0:T(8,128)(2,1)}, f32[2,8,512]{2,1,0:T(8,128)S(1)}, s32[2,512]{1,0:T(2,128)S(1)}, s32[1024]{0:T(1024)S(1)}, ...) while((s32[]{:T(128)}, ...), condition=%wide.region_7.8_spmd, body=%wide.region_4.7_spmd.sunk | while | flops 1125904384 | bytes 64114876 | solution.py:202
  202.6 143.1 %reduce-scatter.7.cloned.1.call-done = f32[256,2048]{1,0:T(8,128)} async-done(((f32[1024,2048]{1,0:T(8,128)}), f32[256,2048]{1,0:T(8,128)}) %reduce-scatter.7.cloned.1.call-update) | async-done | bytes 2097168 | tf_op jit(solution)/shard_map/reduce_scatter | solution.py:204
  355.1 76.0 %all-gather.11.cloned.1.call-done = bf16[1024,2048]{1,0:T(8,128)(2,1)} async-done(((bf16[256,2048]{1,0:T(8,128)(2,1)}), bf16[1024,2048]{1,0:T(8,128)(2,1)}) %all-gather.11.cloned.1.call-update) | async-done | bytes 4194320 | tf_op jit(solution)/shard_map/all_gather | solution.py:208
  431.1 126.2 %all-gather.13.cloned.1.call-done = bf16[3,2048,2048]{2,1,0:T(8,128)(2,1)} async-done(((bf16[3,256,2048]{2,1,0:T(8,128)(2,1)}), bf16[3,2048,2048]{2,1,0:T(8,128)(2,1)}) %all-gather.13.cloned.1.call-update) | async-done | bytes 25165840 | tf_op jit(solution)/shard_map/all_gather | solution.py:211
  557.3 15.9 fusion.34
  586.4 53.1 %all-gather.15.cloned.1.call-done = bf16[1024,2048]{1,0:T(8,128)(2,1)} async-done(((bf16[256,2048]{1,0:T(8,128)(2,1)}), bf16[1024,2048]{1,0:T(8,128)(2,1)}) %all-gather.15.cloned.1.call-update) | async-done | bytes 4194320 | tf_op jit(solution)/shard_map/all_gather | solution.py:223
  639.5 21.5 %multiply_convert_fusion.1 = (bf16[1024,2048]{1,0:T(8,128)(2,1)}, bf16[1024,2048]{1,0:T(8,128)(2,1)}, bf16[1024,2048]{1,0:T(8,128)(2,1)}) fusion(f32[1024,2048]{1,0:T(8,128)} %fusion.32, f32[1024,2048]{1,0:T(8,128)} %fusion.34, bf16[1024,2048]{1,0:T(8,128)(2,1)} %all-gather.15.cloned.1.call-done, bf16[3,2048,2048]{2,1,0:T(8,128)(2,1)} %all-gather.13.cloned.1.call-done), kind=kOutput, calls=%fused_computation.55 | convolution fusion | flops 8621391872 | bytes 41943040 | tf_op jit(solution)/shard_map/dot_general | solution.py:224
  673.9 13.5 fusion.38
  687.5 143.1 %reduce-scatter.11.cloned.1.call-done = f32[256,2048]{1,0:T(8,128)} async-done(((f32[1024,2048]{1,0:T(8,128)}), f32[256,2048]{1,0:T(8,128)}) %reduce-scatter.11.cloned.1.call-update) | async-done | bytes 2097168 | tf_op jit(solution)/shard_map/reduce_scatter | solution.py:234
  835.3 81.6 %all-gather.17.cloned.1.call-done = bf16[1024,2048]{1,0:T(8,128)(2,1)} async-done(((bf16[256,2048]{1,0:T(8,128)(2,1)}), bf16[1024,2048]{1,0:T(8,128)(2,1)}) %all-gather.17.cloned.1.call-update) | async-done | bytes 4194320 | tf_op jit(solution)/shard_map/all_gather | solution.py:242
  928.0 123.3 %while.28 = (s32[]{:T(128)}, f32[1024,8,64]{0,2,1:T(8,128)}, f32[1024,8,64]{0,2,1:T(8,128)}, f32[2,512,8,64]{1,0,3,2:T(2,128)}, bf16[2,512,8,64]{1,3,2,0:T(8,128...) while((s32[]{:T(128)}, f32[1024,8,64]{0,2,1:T(8,128)}, ...), condition=%wide.region_15.16_spmd.clone, body=%wide.region_13.15_spmd.clone.sunk | while | flops 2726555648 | bytes 200675760 | solution.py:253
  969.3 19.6 %dynamic_update_slice.20 = f32[2,512,8,64]{1,0,3,2:T(2,128)} dynamic-update-slice(f32[2,512,8,64]{1,0,3,2:T(2,128)} %get-tuple-element.526, f32[1,512,8,64]{1,0,3,2:T(1,128)} %copy.72, s32[]{:T(128)S(6)} %copy.90, s32[]{:T(128)} %constant.43.clone.1..sunk, s32[]{:T(128)} %constant.43.clone.1..sunk, s32[]{:T(128)} %constant.43.clone.1..sunk) | dynamic-update-slice | bytes 2097156 | tf_op jit(solution)/shard_map/while/body/jit(dynamic_update_index_in_dim)/dynamic_update_slice | solution.py:253
  1031.7 19.6 %dynamic_update_slice.20 = f32[2,512,8,64]{1,0,3,2:T(2,128)} dynamic-update-slice(f32[2,512,8,64]{1,0,3,2:T(2,128)} %get-tuple-element.526, f32[1,512,8,64]{1,0,3,2:T(1,128)} %copy.72, s32[]{:T(128)S(6)} %copy.90, s32[]{:T(128)} %constant.43.clone.1..sunk, s32[]{:T(128)} %constant.43.clone.1..sunk, s32[]{:T(128)} %constant.43.clone.1..sunk) | dynamic-update-slice | bytes 2097156 | tf_op jit(solution)/shard_map/while/body/jit(dynamic_update_index_in_dim)/dynamic_update_slice | solution.py:253
  1075.0 14.5 fusion.36
  1109.3 15.5 convolution_bitcast_fusion
  1148.1 35.8 %pad_maximum_fusion = f32[3,2048,2048]{2,1,0:T(8,128)} fusion(f32[1,2048,2048]{2,1,0:T(8,128)} %convolution_bitcast_fusion, f32[1,2048,2048]{2,1,0:T(8,128)} %convolution_bitcast_fusion.1, f32[1,2048,2048]{2,1,0:T(8,128)} %convolution_bitcast_fusion.2), kind=kLoop, calls=%fused_computation.45 | loop fusion | flops 25165824 | bytes 100663296 | tf_op jit(solution)/shard_map/stack | solution.py:230
  1184.0 34.0 %reduce-scatter.13.cloned.1.call-done = f32[256,2048]{1,0:T(8,128)} async-done(((f32[1024,2048]{1,0:T(8,128)}), f32[256,2048]{1,0:T(8,128)}) %reduce-scatter.13.cloned.1.call-update) | async-done | bytes 2097168 | tf_op jit(solution)/shard_map/reduce_scatter | solution.py:279
  1220.4 46.3 %psum.7 = f32[2,2048]{1,0:T(2,128)S(1)} all-reduce(f32[2,2048]{1,0:T(2,128)S(1)} %pad_maximum_fusion.3), channel_id=1, replica_groups=mesh['dp'=8,'tensor'=4] {'dp','tensor'}, use_global_device_ids=true, to_apply=%region_20.21 | all-reduce | flops 4096 | bytes 32768 | tf_op jit(solution)/shard_map/psum | solution.py:289
  1267.4 99.0 %reduce-scatter.9.cloned.1.call-done = f32[256,2048]{1,0:T(8,128)} async-done(((f32[1024,2048]{1,0:T(8,128)}), f32[256,2048]{1,0:T(8,128)}) %reduce-scatter.9.cloned.1.call-update) | async-done | bytes 2097168 | tf_op jit(solution)/shard_map/reduce_scatter | solution.py:216
  1372.4 115.0 %reduce-scatter.15.cloned.1.call-done = f32[4,256,512]{2,1,0:T(8,128)} async-done(((f32[4,2048,512]{2,1,0:T(8,128)}), f32[4,256,512]{2,1,0:T(8,128)}) %reduce-scatter.15.cloned.1.call-update) | async-done | bytes 2097168 | tf_op jit(solution)/shard_map/reduce_scatter | solution.py:278
  1494.8 282.6 %reduce-scatter.17.cloned.1.call-done = f32[3,256,2048]{2,1,0:T(8,128)} async-done(((f32[3,2048,2048]{2,1,0:T(8,128)}), f32[3,256,2048]{2,1,0:T(8,128)}) %reduce-scatter.17.cloned.1.call-update) | async-done | bytes 6291472 | tf_op jit(solution)/shard_map/reduce_scatter | solution.py:233
  1777.4 14.5 multiply_subtract_fusion
  (252 shorter events, 291.5 us)
Async XLA Ops:
  7.2 60.4 %all-gather.9.cloned.1.call-start = ((), (), s32[]{:S(2)}) async-start(), calls=%async_computation.7 | async-start | bytes 9437184 | tf_op jit(solution)/shard_map/all_gather | solution.py:185
  10.1 140.5 %all-gather.7.cloned.1.call-start = ((), (), s32[]{:S(2)}) async-start(), calls=%async_computation.6 | async-start | bytes 5242880 | tf_op jit(solution)/shard_map/all_gather | solution.py:182
  12.9 332.8 %reduce-scatter.7.cloned.1.call-start = ((), (), s32[]{:S(2)}) async-start(), calls=%async_computation.8 | async-start | bytes 10485760 | tf_op jit(solution)/shard_map/reduce_scatter | solution.py:204
  14.0 144.4 %copy-start.16 = (f32[1024,32]{0,1:T(8,128)}, f32[1024,32]{0,1:T(8,128)S(1)}, u32[]{:S(2)}) copy-start(f32[1024,32]{0,1:T(8,128)S(1)} %get-tuple-element.313) | copy-start | bytes 393220
  14.0 144.4 %copy-start.18 = (f32[1024,32]{0,1:T(8,128)}, f32[1024,32]{0,1:T(8,128)S(1)}, u32[]{:S(2)}) copy-start(f32[1024,32]{0,1:T(8,128)S(1)} %get-tuple-element.314) | copy-start | bytes 393220
  202.6 145.4 %copy-start.26 = (f32[1,2048]{1,0:T(1,128)S(1)}, f32[1,2048]{1,0:T(1,128)}, u32[]{:S(2)}) copy-start(f32[1,2048]{1,0:T(1,128)} %get-tuple-element.311) | copy-start | bytes 24580
  202.6 228.5 %all-gather.11.cloned.1.call-start = ((), (), s32[]{:S(2)}) async-start(), calls=%async_computation.9 | async-start | bytes 5242880 | tf_op jit(solution)/shard_map/all_gather | solution.py:208
  348.0 485.6 %copy-start.4 = (f32[256,2048]{1,0:T(8,128)}, f32[256,2048]{1,0:T(8,128)S(1)}, u32[]{:S(2)}) copy-start(f32[256,2048]{1,0:T(8,128)S(1)} %get-tuple-element.282) | copy-start | bytes 6291460
  348.0 485.5 %copy-start.38 = (f32[256]{0:T(256)}, f32[256]{0:T(256)S(1)}, u32[]{:S(2)}) copy-start(f32[256]{0:T(256)S(1)} %add_rsqrt_fusion) | copy-start | bytes 3076
  349.4 207.8 %all-gather.13.cloned.1.call-start = ((), (), s32[]{:S(2)}) async-start(), calls=%async_computation.10 | async-start | bytes 28311552 | tf_op jit(solution)/shard_map/all_gather | solution.py:211
  354.4 285.1 %all-gather.15.cloned.1.call-start = ((), (), s32[]{:S(2)}) async-start(), calls=%async_computation.12 | async-start | bytes 5242880 | tf_op jit(solution)/shard_map/all_gather | solution.py:223
  355.0 475.6 %reduce-scatter.11.cloned.1.call-start = ((), (), s32[]{:S(2)}) async-start(), calls=%async_computation.13 | async-start | bytes 10485760 | tf_op jit(solution)/shard_map/reduce_scatter | solution.py:234
  687.4 229.4 %all-gather.17.cloned.1.call-start = ((), (), s32[]{:S(2)}) async-start(), calls=%async_computation.14 | async-start | bytes 5242880 | tf_op jit(solution)/shard_map/all_gather | solution.py:242
  833.5 89.5 %copy-start.44 = (f32[256]{0:T(256)}, f32[256]{0:T(256)S(1)}, u32[]{:S(2)}) copy-start(f32[256]{0:T(256)S(1)} %broadcast_multiply_fusion.1) | copy-start | bytes 3076
  835.2 382.8 %reduce-scatter.13.cloned.1.call-start = ((), (), s32[]{:S(2)}) async-start(), calls=%async_computation.15 | async-start | bytes 10485760 | tf_op jit(solution)/shard_map/reduce_scatter | solution.py:279
  1074.9 291.5 %reduce-scatter.9.cloned.1.call-start = ((), (), s32[]{:S(2)}) async-start(), calls=%async_computation.11 | async-start | bytes 10485760 | tf_op jit(solution)/shard_map/reduce_scatter | solution.py:216
  1089.5 397.9 %reduce-scatter.15.cloned.1.call-start = ((), (), s32[]{:S(2)}) async-start(), calls=%async_computation.16 | async-start | bytes 18874368 | tf_op jit(solution)/shard_map/reduce_scatter | solution.py:278
  1109.0 668.3 %reduce-scatter.17.cloned.1.call-start = ((), (), s32[]{:S(2)}) async-start(), calls=%async_computation.17 | async-start | bytes 56623104 | tf_op jit(solution)/shard_map/reduce_scatter | solution.py:233
  1184.0 182.5 %copy-start.27 = (f32[1,2048]{1,0:T(1,128)S(1)}, f32[1,2048]{1,0:T(1,128)}, u32[]{:S(2)}) copy-start(f32[1,2048]{1,0:T(1,128)} %get-tuple-element.311) | copy-start | bytes 24580
  1184.0 182.5 %copy-start.39 = (f32[256]{0:T(256)S(1)}, f32[256]{0:T(256)}, u32[]{:S(2)}) copy-start(f32[256]{0:T(256)} %copy-done.38) | copy-start | bytes 3076
  1184.0 182.4 %copy-start.45 = (f32[256]{0:T(256)S(1)}, f32[256]{0:T(256)}, u32[]{:S(2)}) copy-start(f32[256]{0:T(256)} %copy-done.44) | copy-start | bytes 3076
  1184.0 182.4 %copy-start.5 = (f32[256,2048]{1,0:T(8,128)S(1)}, f32[256,2048]{1,0:T(8,128)}, u32[]{:S(2)}) copy-start(f32[256,2048]{1,0:T(8,128)} %copy-done.4) | copy-start | bytes 6291460
  1266.7 105.7 %copy-start.36 = (f32[2,2048]{1,0:T(2,128)}, f32[2,2048]{1,0:T(2,128)S(1)}, u32[]{:S(2)}) copy-start(f32[2,2048]{1,0:T(2,128)S(1)} %psum.7) | copy-start | bytes 49156
  1267.4 220.0 %copy-start.46 = (f32[4]{0:T(128)S(1)}, f32[4]{0:T(128)}, u32[]{:S(2)}) copy-start(f32[4]{0:T(128)} %constant.115) | copy-start | bytes 52
  (53 other events, 729.0 us)
Sparse Core Ops, SparseCore 0:
  10.5 57.0 all-gather.8
  69.8 80.7 all-gather.6
  202.7 143.0 reduce-scatter.6
  349.6 81.4 all-gather.10
  433.4 123.8 all-gather.12
  558.7 80.7 all-gather.14
  687.6 143.0 reduce-scatter.10
  835.3 81.4 all-gather.16
  1075.0 142.9 reduce-scatter.12
  1220.3 146.1 reduce-scatter.8
  1370.6 116.8 reduce-scatter.14
  1491.5 285.8 reduce-scatter.16
where the time goes:
time: 1810 us; the launch traced here: 1800 us
  waiting for transfers between devices  1280 us (71%)
  matrix products  257 us (14%)
  other arithmetic  124 us (7%)
  local copies, waits for them, and re-layouts  79.8 us (4%)
  blocking collectives  46.3 us (3%)
    reduce_scatter x1, waiting for transfers between devices, local(): lax.psum_scatter(mlp_stack, 'dp', scatter_dimension=1, tiled=True)  283 us
    reduce_scatter x1, waiting for transfers between devices, local(): lax.psum_scatter(dot_transposed(d_gate, mlp_back[0]) + dot_transposed(d_u...  143 us
    reduce_scatter x1, waiting for transfers between devices, local(): lax.psum_scatter(dot_transposed(attended, attn_low[3]), 'tensor', scatter...  143 us
    all_gather x1, waiting for transfers between devices, local(): lax.all_gather(mlp_weight.astype(jnp.bfloat16), 'dp', axis=1, tiled=True)  126 us
    reduce_scatter x1, waiting for transfers between devices, local(): lax.psum_scatter(attn_stack, 'dp', scatter_dimension=1, tiled=True)  115 us
    reduce_scatter x1, waiting for transfers between devices, local(): lax.psum_scatter(dot_transposed(hidden, mlp_low[2]), 'tensor', scatter_di...  99 us
    all_gather x1, waiting for transfers between devices, local(): lax.all_gather(d_middle.astype(jnp.bfloat16), 'tensor', axis=0, tiled=True)  81.6 us
    all_gather x1, waiting for transfers between devices, local(): lax.all_gather((normed_two * norm_gains[1]).astype(jnp.bfloat16), 'tensor...  76 us
  transfers between devices with their start and end apart: 12, of which 12 were waited for; matrix products, arithmetic and copies ran while one was open for 10% of the time, Pallas kernels for 0%

commit v1 on v0

--- a/solution.py
+++ b/solution.py
@@ -202,8 +202,11 @@
     attended, log_totals = lax.map(forward_block, (query_blocks, seg_blocks, pos_blocks))
     attended = attended.reshape(seq_length, head_width)
     middle = layer_in + lax.psum_scatter(
-        dot_transposed(attended, attn_low[3]), "tensor", scatter_dimension=0, tiled=True
-    )
+        dot_transposed(attended, attn_low[3]).astype(jnp.bfloat16),
+        "tensor",
+        scatter_dimension=0,
+        tiled=True,
+    ).astype(jnp.float32)
     normed_two, inv_two = norm_forward(middle)
     second_in = lax.all_gather(
         (normed_two * norm_gains[1]).astype(jnp.bfloat16), "tensor", axis=0, tiled=True
@@ -214,8 +217,11 @@
     sigmoid_gate = jax.nn.sigmoid(gate_proj)
     hidden = (gate_proj * sigmoid_gate * up_proj).astype(jnp.bfloat16)
     layer_out = middle + lax.psum_scatter(
-        dot_transposed(hidden, mlp_low[2]), "tensor", scatter_dimension=0, tiled=True
-    )
+        dot_transposed(hidden, mlp_low[2]).astype(jnp.bfloat16),
+        "tensor",
+        scatter_dimension=0,
+        tiled=True,
+    ).astype(jnp.float32)
     attn_back, mlp_back = (
         lax.all_gather(attn_weight.astype(jnp.bfloat16), "dp", axis=1, tiled=True),
         lax.all_gather(mlp_weight.astype(jnp.bfloat16), "dp", axis=1, tiled=True),
@@ -227,16 +233,27 @@
         d_hidden * up_proj * (sigmoid_gate * (1.0 + gate_proj * (1.0 - sigmoid_gate)))
     ).astype(jnp.bfloat16)
     d_up = (d_hidden * (gate_proj * sigmoid_gate)).astype(jnp.bfloat16)
-    mlp_stack = jnp.stack(
-        [dot_over_rows(second_in, d_gate), dot_over_rows(second_in, d_up), down_grad]
-    )
-    mlp_grad = lax.psum_scatter(mlp_stack, "dp", scatter_dimension=1, tiled=True)
+
+    def to_owner(partial):
+        return lax.psum_scatter(
+            partial.astype(jnp.bfloat16), "dp", scatter_dimension=0, tiled=True
+        ).astype(jnp.float32)
+
+    mlp_grad = jnp.stack(
+        [
+            to_owner(dot_over_rows(second_in, d_gate)),
+            to_owner(dot_over_rows(second_in, d_up)),
+            to_owner(down_grad),
+        ]
+    )
     d_second = lax.psum_scatter(
-        dot_transposed(d_gate, mlp_back[0]) + dot_transposed(d_up, mlp_back[1]),
+        (dot_transposed(d_gate, mlp_back[0]) + dot_transposed(d_up, mlp_back[1])).astype(
+            jnp.bfloat16
+        ),
         "tensor",
         scatter_dimension=0,
         tiled=True,
-    )
+    ).astype(jnp.float32)
     d_middle, gain_two = norm_backward(d_second, normed_two, inv_two, norm_gains[1])
     d_middle = d_middle + cotangent.astype(jnp.float32)
     d_attn = lax.all_gather(d_middle.astype(jnp.bfloat16), "tensor", axis=0, tiled=True)
@@ -267,23 +284,24 @@
         .astype(jnp.bfloat16)
     )
     value_raw = value_grad.reshape(seq_length, head_width).astype(jnp.bfloat16)
-    attn_stack = jnp.stack(
+    attn_grad = jnp.stack(
         [
-            dot_over_rows(first_in, query_raw),
-            dot_over_rows(first_in, key_raw),
-            dot_over_rows(first_in, value_raw),
-            out_proj_grad,
+            to_owner(dot_over_rows(first_in, query_raw)),
+            to_owner(dot_over_rows(first_in, key_raw)),
+            to_owner(dot_over_rows(first_in, value_raw)),
+            to_owner(out_proj_grad),
         ]
     )
-    attn_grad = lax.psum_scatter(attn_stack, "dp", scatter_dimension=1, tiled=True)
     d_first = lax.psum_scatter(
-        dot_transposed(query_raw, attn_back[0])
-        + dot_transposed(key_raw, attn_back[1])
-        + dot_transposed(value_raw, attn_back[2]),
+        (
+            dot_transposed(query_raw, attn_back[0])
+            + dot_transposed(key_raw, attn_back[1])
+            + dot_transposed(value_raw, attn_back[2])
+        ).astype(jnp.bfloat16),
         "tensor",
         scatter_dimension=0,
         tiled=True,
-    )
+    ).astype(jnp.float32)
     d_input, gain_one = norm_backward(d_first, normed_one, inv_one, norm_gains[0])
     grad_in = d_input + d_middle
     gain_grad = lax.psum(jnp.stack([gain_one, gain_two]), ("dp", "tensor"))

time: 1810 us -> 1370 us (0.76)
  waiting for transfers between devices: 1280 us -> 862 us
  other arithmetic: 124 us -> 88 us
    reduce_scatter x6 -> x11, waiting for transfers between devices: 817 us -> 446 us  [the longest x7 188 us: to_owner(): lax.psum_scatter(partial.astype(jnp.bfloat16), 'dp', scatter_dimension=0,...]
    all_gather x1, waiting for transfers between devices: 81.6 us -> 38.6 us  [local(): lax.all_gather(d_middle.astype(jnp.bfloat16), 'tensor', axis=0, tiled=True)]
    another operation x4 -> x2, other arithmetic: 42.9 us -> 0.9 us  [the longest x1 35.8 us: local(): jnp.stack([dot_over_rows(second_in, d_gate), dot_over_rows(second_in, d_u...]
  transfers between devices with their start and end apart: 12 -> 17, of which waited for: 12 -> 15; matrix products, arithmetic and copies ran while one was open for 10% -> 23% of each run, Pallas kernels for 0% -> 0%
where the time goes in v1:
time: 1370 us; the launch traced here: 1360 us
  waiting for transfers between devices  862 us (63%)
  matrix products  269 us (20%)
  other arithmetic  88 us (6%)
  local copies, waits for them, and re-layouts  79.4 us (6%)
  blocking collectives  42.9 us (3%)
  between operations  15.1 us (1%)
    reduce_scatter x7, waiting for transfers between devices, to_owner(): lax.psum_scatter(partial.astype(jnp.bfloat16), 'dp', scatter_dimension=0,...  188 us
    all_gather x1, waiting for transfers between devices, local(): lax.all_gather(mlp_weight.astype(jnp.bfloat16), 'dp', axis=1, tiled=True)  126 us
    all_gather x1, waiting for transfers between devices, local(): lax.all_gather((normed_two * norm_gains[1]).astype(jnp.bfloat16), 'tensor...  75.8 us
    reduce_scatter x1, waiting for transfers between devices, local(): lax.psum_scatter(dot_transposed(attended, attn_low[3]).astype(jnp.bfloat1...  75.4 us
    reduce_scatter x1, waiting for transfers between devices, local(): lax.psum_scatter((dot_transposed(d_gate, mlp_back[0]) + dot_transposed(d_...  75.4 us
    reduce_scatter x1, waiting for transfers between devices, local(): lax.psum_scatter((dot_transposed(query_raw, attn_back[0]) + dot_transpose...  72.6 us
    all_gather x1, waiting for transfers between devices, local(): lax.all_gather((normed_one * norm_gains[0]).astype(jnp.bfloat16), 'tensor...  67.4 us
    dot_general x7, matrix products, dot_over_rows(): lax.dot_general(left, right, (((0,), (0,)), ((), ())), preferred_element_...  66.3 us
  transfers between devices with their start and end apart: 17, of which 15 were waited for; matrix products, arithmetic and copies ran while one was open for 23% of the time, Pallas kernels for 0%

profile of v1, /device:TPU:0, one launch (start us, length us, event | category | flops | bytes accessed | tf_op | source)
XLA Modules:
  0.0 1358.4 jit_solution(17429672665173322831)
XLA Ops:
  14.6 53.1 %all-gather.9.cloned.1.call-done = bf16[4,2048,512]{2,1,0:T(8,128)(2,1)} async-done(((bf16[4,256,512]{2,1,0:T(8,128)(2,1)}), bf16[4,2048,512]{2,1,0:T(8,128)(2,1)}) %all-gather.9.cloned.1.call-update) | async-done | bytes 8388624 | tf_op jit(solution)/shard_map/all_gather | solution.py:185
  83.2 67.4 %all-gather.7.cloned.1.call-done = bf16[1024,2048]{1,0:T(8,128)(2,1)} async-done(((bf16[256,2048]{1,0:T(8,128)(2,1)}), bf16[1024,2048]{1,0:T(8,128)(2,1)}) %all-gather.7.cloned.1.call-update) | async-done | bytes 4194320 | tf_op jit(solution)/shard_map/all_gather | solution.py:182
  162.4 29.9 %while.27 = (s32[]{:T(128)}, bf16[2,512,8,64]{1,3,2,0:T(8,128)(2,1)}, f32[2,8,512]{2,1,0:T(8,128)}, s32[2,512]{1,0:T(2,128)S(1)}, s32[1024]{0:T(1024)S(1)}, /*in...) while((s32[]{:T(128)}, ...), condition=%wide.region_7.8_spmd, body=%wide.region_4.7_spmd.sunk | while | flops 1125904384 | bytes 64114876 | solution.py:202
  202.8 75.4 %reduce-scatter.12.cloned.1.call-done = bf16[256,2048]{1,0:T(8,128)(2,1)} async-done(((bf16[1024,2048]{1,0:T(8,128)(2,1)}), bf16[256,2048]{1,0:T(8,128)(2,1)}) %reduce-scatter.12.cloned.1.call-update) | async-done | bytes 1048592 | tf_op jit(solution)/shard_map/reduce_scatter | solution.py:204
  288.1 75.8 %all-gather.11.cloned.1.call-done = bf16[1024,2048]{1,0:T(8,128)(2,1)} async-done(((bf16[256,2048]{1,0:T(8,128)(2,1)}), bf16[1024,2048]{1,0:T(8,128)(2,1)}) %all-gather.11.cloned.1.call-update) | async-done | bytes 4194320 | tf_op jit(solution)/shard_map/all_gather | solution.py:211
  363.9 126.4 %all-gather.13.cloned.1.call-done = bf16[3,2048,2048]{2,1,0:T(8,128)(2,1)} async-done(((bf16[3,256,2048]{2,1,0:T(8,128)(2,1)}), bf16[3,2048,2048]{2,1,0:T(8,128)(2,1)}) %all-gather.13.cloned.1.call-update) | async-done | bytes 25165840 | tf_op jit(solution)/shard_map/all_gather | solution.py:214
  490.3 15.7 %fusion.34 = f32[1024,2048]{1,0:T(8,128)} fusion(bf16[1024,2048]{1,0:T(8,128)(2,1)} %all-gather.11.cloned.1.call-done, bf16[3,2048,2048]{2,1,0:T(8,128)(2,1)} %all-gather.13.cloned.1.call-done), kind=kOutput, calls=%fused_computation.62 | convolution fusion | flops 8589934592 | bytes 20971520 | tf_op jit(solution)/shard_map/dot_general | solution.py:216
  519.2 53.4 %all-gather.15.cloned.1.call-done = bf16[1024,2048]{1,0:T(8,128)(2,1)} async-done(((bf16[256,2048]{1,0:T(8,128)(2,1)}), bf16[1024,2048]{1,0:T(8,128)(2,1)}) %all-gather.15.cloned.1.call-update) | async-done | bytes 4194320 | tf_op jit(solution)/shard_map/all_gather | solution.py:229
  572.6 21.5 %multiply_convert_fusion.1 = (bf16[1024,2048]{1,0:T(8,128)(2,1)}, bf16[1024,2048]{1,0:T(8,128)(2,1)}, bf16[1024,2048]{1,0:T(8,128)(2,1)}) fusion(f32[1024,2048]{1,0:T(8,128)} %fusion.32, f32[1024,2048]{1,0:T(8,128)} %fusion.34, bf16[1024,2048]{1,0:T(8,128)(2,1)} %all-gather.15.cloned.1.call-done, bf16[3,2048,2048]{2,1,0:T(8,128)(2,1)} %all-gather.13.cloned.1.call-done), kind=kOutput, calls=%fused_computation.52 | convolution fusion | flops 8621391872 | bytes 41943040 | tf_op jit(solution)/shard_map/dot_general | solution.py:230
  620.2 75.4 %reduce-scatter.16.cloned.1.call-done = bf16[256,2048]{1,0:T(8,128)(2,1)} async-done(((bf16[1024,2048]{1,0:T(8,128)(2,1)}), bf16[256,2048]{1,0:T(8,128)(2,1)}) %reduce-scatter.16.cloned.1.call-update) | async-done | bytes 1048592 | tf_op jit(solution)/shard_map/reduce_scatter | solution.py:249
  730.0 14.3 %convolution_convert_fusion.1 = bf16[2048,2048]{1,0:T(8,128)(2,1)} fusion(bf16[1024,2048]{1,0:T(8,128)(2,1)} %all-gather.11.cloned.1.call-done, bf16[1024,2048]{1,0:T(8,128)(2,1)} %get-tuple-element.292), kind=kOutput, calls=%fused_computation.58 | convolution fusion | flops 8594128896 | bytes 16777216 | tf_op jit(solution)/shard_map/dot_general | solution.py:84
  744.4 38.6 %all-gather.17.cloned.1.call-done = bf16[1024,2048]{1,0:T(8,128)(2,1)} async-done(((bf16[256,2048]{1,0:T(8,128)(2,1)}), bf16[1024,2048]{1,0:T(8,128)(2,1)}) %all-gather.17.cloned.1.call-update) | async-done | bytes 4194320 | tf_op jit(solution)/shard_map/all_gather | solution.py:259
  799.0 128.0 %while.28 = (s32[]{:T(128)}, f32[1024,8,64]{0,2,1:T(8,128)}, f32[1024,8,64]{0,2,1:T(8,128)}, f32[2,512,8,64]{1,0,3,2:T(2,128)}, bf16[2,512,8,64]{1,3,2,0:T(8,128...) while((s32[]{:T(128)}, f32[1024,8,64]{0,2,1:T(8,128)}, ...), condition=%wide.region_15.16_spmd.clone, body=%wide.region_13.15_spmd.clone.sunk | while | flops 2726555648 | bytes 200380720 | solution.py:270
  842.5 19.7 %dynamic_update_slice.20 = f32[2,512,8,64]{1,0,3,2:T(2,128)} dynamic-update-slice(f32[2,512,8,64]{1,0,3,2:T(2,128)} %get-tuple-element.526, f32[1,512,8,64]{1,0,3,2:T(1,128)} %copy.72, s32[]{:T(128)S(6)} %copy.90, s32[]{:T(128)} %constant.43.clone.1..sunk, s32[]{:T(128)} %constant.43.clone.1..sunk, s32[]{:T(128)} %constant.43.clone.1..sunk) | dynamic-update-slice | bytes 2097156 | tf_op jit(solution)/shard_map/while/body/jit(dynamic_update_index_in_dim)/dynamic_update_slice | solution.py:270
  907.1 19.7 %dynamic_update_slice.20 = f32[2,512,8,64]{1,0,3,2:T(2,128)} dynamic-update-slice(f32[2,512,8,64]{1,0,3,2:T(2,128)} %get-tuple-element.526, f32[1,512,8,64]{1,0,3,2:T(1,128)} %copy.72, s32[]{:T(128)S(6)} %copy.90, s32[]{:T(128)} %constant.43.clone.1..sunk, s32[]{:T(128)} %constant.43.clone.1..sunk, s32[]{:T(128)} %constant.43.clone.1..sunk) | dynamic-update-slice | bytes 2097156 | tf_op jit(solution)/shard_map/while/body/jit(dynamic_update_index_in_dim)/dynamic_update_slice | solution.py:270
  982.9 23.2 %reduce-scatter.28.cloned.1.call-done = bf16[256,2048]{1,0:T(8,128)(2,1)} async-done(((bf16[2048,2048]{1,0:T(8,128)(2,1)}), bf16[256,2048]{1,0:T(8,128)(2,1)}) %reduce-scatter.28.cloned.1.call-update) | async-done | bytes 1048592 | tf_op jit(solution)/shard_map/reduce_scatter | solution.py:238
  1006.1 15.7 %multiply_subtract_fusion = (f32[3,256,2048]{2,1,0:T(8,128)}, f32[3,256,2048]{2,1,0:T(8,128)}, f32[3,256,2048]{2,1,0:T(8,128)}, f32[3,256,2048]{2,1,0:T(8,128)}) fusion(f32[3,256,2048]{2,1,0:T(8,128)} %param.22, f32[3,256,2048]{2,1,0:T(8,128)} %param.28, f32[3,256,2048]{2,1,0:T(8,128)} %param.25, bf16[1,256,2048]{2,1,0:T(8,128)(2,1)} %bitcast.217, ...), kind=kLoop, calls=%fused_computation.66 | loop fusion | flops 28311552 | bytes 47185920 | tf_op jit(solution)/shard_map/sub | solution.py:149
  1021.8 29.6 %reduce-scatter.26.cloned.1.call-done = bf16[256,512]{1,0:T(8,128)(2,1)} async-done(((bf16[2048,512]{1,0:T(8,128)(2,1)}), bf16[256,512]{1,0:T(8,128)(2,1)}) %reduce-scatter.26.cloned.1.call-update) | async-done | bytes 262160 | tf_op jit(solution)/shard_map/reduce_scatter | solution.py:238
  1051.4 45.1 %reduce-scatter.24.cloned.1.call-done = bf16[256,512]{1,0:T(8,128)(2,1)} async-done(((bf16[2048,512]{1,0:T(8,128)(2,1)}), bf16[256,512]{1,0:T(8,128)(2,1)}) %reduce-scatter.24.cloned.1.call-update) | async-done | bytes 262160 | tf_op jit(solution)/shard_map/reduce_scatter | solution.py:238
  1096.5 45.3 %reduce-scatter.20.cloned.1.call-done = bf16[256,512]{1,0:T(8,128)(2,1)} async-done(((bf16[2048,512]{1,0:T(8,128)(2,1)}), bf16[256,512]{1,0:T(8,128)(2,1)}) %reduce-scatter.20.cloned.1.call-update) | async-done | bytes 262160 | tf_op jit(solution)/shard_map/reduce_scatter | solution.py:238
  1141.8 44.9 %reduce-scatter.22.cloned.1.call-done = bf16[256,512]{1,0:T(8,128)(2,1)} async-done(((bf16[2048,512]{1,0:T(8,128)(2,1)}), bf16[256,512]{1,0:T(8,128)(2,1)}) %reduce-scatter.22.cloned.1.call-update) | async-done | bytes 262160 | tf_op jit(solution)/shard_map/reduce_scatter | solution.py:238
  1193.1 72.6 %reduce-scatter.18.cloned.1.call-done = bf16[256,2048]{1,0:T(8,128)(2,1)} async-done(((bf16[1024,2048]{1,0:T(8,128)(2,1)}), bf16[256,2048]{1,0:T(8,128)(2,1)}) %reduce-scatter.18.cloned.1.call-update) | async-done | bytes 1048592 | tf_op jit(solution)/shard_map/reduce_scatter | solution.py:295
  1267.9 42.9 %psum.7 = f32[2,2048]{1,0:T(2,128)S(1)} all-reduce(f32[2,2048]{1,0:T(2,128)S(1)} %pad_maximum_fusion.1), channel_id=1, replica_groups=mesh['dp'=8,'tensor'=4] {'dp','tensor'}, use_global_device_ids=true, to_apply=%region_20.21 | all-reduce | flops 4096 | bytes 32768 | tf_op jit(solution)/shard_map/psum | solution.py:307
  1311.5 34.8 %reduce-scatter.14.cloned.1.call-done = bf16[256,2048]{1,0:T(8,128)(2,1)} async-done(((bf16[1024,2048]{1,0:T(8,128)(2,1)}), bf16[256,2048]{1,0:T(8,128)(2,1)}) %reduce-scatter.14.cloned.1.call-update) | async-done | bytes 1048592 | tf_op jit(solution)/shard_map/reduce_scatter | solution.py:219
  (255 shorter events, 331.9 us)
Async XLA Ops:
  7.2 60.4 %all-gather.9.cloned.1.call-start = ((), (), s32[]{:S(2)}) async-start(), calls=%async_computation.12 | async-start | bytes 9437184 | tf_op jit(solution)/shard_map/all_gather | solution.py:185
  10.1 140.5 %all-gather.7.cloned.1.call-start = ((), (), s32[]{:S(2)}) async-start(), calls=%async_computation.11 | async-start | bytes 5242880 | tf_op jit(solution)/shard_map/all_gather | solution.py:182
  12.9 265.2 %reduce-scatter.12.cloned.1.call-start = ((), (), s32[]{:S(2)}) async-start(), calls=%async_computation.13 | async-start | bytes 5242880 | tf_op jit(solution)/shard_map/reduce_scatter | solution.py:204
  202.7 161.2 %all-gather.11.cloned.1.call-start = ((), (), s32[]{:S(2)}) async-start(), calls=%async_computation.14 | async-start | bytes 5242880 | tf_op jit(solution)/shard_map/all_gather | solution.py:211
  279.8 418.5 %copy-start.40 = (f32[256]{0:T(256)}, f32[256]{0:T(256)S(1)}, u32[]{:S(2)}) copy-start(f32[256]{0:T(256)S(1)} %add_rsqrt_fusion) | copy-start | bytes 3076
  282.4 207.8 %all-gather.13.cloned.1.call-start = ((), (), s32[]{:S(2)}) async-start(), calls=%async_computation.15 | async-start | bytes 28311552 | tf_op jit(solution)/shard_map/all_gather | solution.py:214
  287.5 285.1 %all-gather.15.cloned.1.call-start = ((), (), s32[]{:S(2)}) async-start(), calls=%async_computation.17 | async-start | bytes 5242880 | tf_op jit(solution)/shard_map/all_gather | solution.py:229
  288.0 407.5 %reduce-scatter.16.cloned.1.call-start = ((), (), s32[]{:S(2)}) async-start(), calls=%async_computation.18 | async-start | bytes 5242880 | tf_op jit(solution)/shard_map/reduce_scatter | solution.py:249
  620.1 162.9 %all-gather.17.cloned.1.call-start = ((), (), s32[]{:S(2)}) async-start(), calls=%async_computation.19 | async-start | bytes 5242880 | tf_op jit(solution)/shard_map/all_gather | solution.py:259
  701.6 281.3 %reduce-scatter.32.cloned.1.call-start = ((), (), s32[]{:S(2)}) async-start(), calls=%async_computation.27 | async-start | bytes 9437184 | tf_op jit(solution)/shard_map/reduce_scatter | solution.py:238
  715.7 267.1 %reduce-scatter.30.cloned.1.call-start = ((), (), s32[]{:S(2)}) async-start(), calls=%async_computation.26 | async-start | bytes 9437184 | tf_op jit(solution)/shard_map/reduce_scatter | solution.py:238
  729.9 276.2 %reduce-scatter.28.cloned.1.call-start = ((), (), s32[]{:S(2)}) async-start(), calls=%async_computation.25 | async-start | bytes 9437184 | tf_op jit(solution)/shard_map/reduce_scatter | solution.py:238
  744.3 307.1 %reduce-scatter.26.cloned.1.call-start = ((), (), s32[]{:S(2)}) async-start(), calls=%async_computation.24 | async-start | bytes 2359296 | tf_op jit(solution)/shard_map/reduce_scatter | solution.py:238
  798.9 297.5 %reduce-scatter.24.cloned.1.call-start = ((), (), s32[]{:S(2)}) async-start(), calls=%async_computation.23 | async-start | bytes 2359296 | tf_op jit(solution)/shard_map/reduce_scatter | solution.py:238
  934.7 207.1 %reduce-scatter.20.cloned.1.call-start = ((), (), s32[]{:S(2)}) async-start(), calls=%async_computation.21 | async-start | bytes 2359296 | tf_op jit(solution)/shard_map/reduce_scatter | solution.py:238
  946.8 239.9 %reduce-scatter.22.cloned.1.call-start = ((), (), s32[]{:S(2)}) async-start(), calls=%async_computation.22 | async-start | bytes 2359296 | tf_op jit(solution)/shard_map/reduce_scatter | solution.py:238
  953.6 312.2 %reduce-scatter.18.cloned.1.call-start = ((), (), s32[]{:S(2)}) async-start(), calls=%async_computation.20 | async-start | bytes 5242880 | tf_op jit(solution)/shard_map/reduce_scatter | solution.py:295
  968.3 378.0 %reduce-scatter.14.cloned.1.call-start = ((), (), s32[]{:S(2)}) async-start(), calls=%async_computation.16 | async-start | bytes 5242880 | tf_op jit(solution)/shard_map/reduce_scatter | solution.py:219
  1006.1 180.7 %copy-start.48 = (f32[4]{0:T(128)S(1)}, f32[4]{0:T(128)}, u32[]{:S(2)}) copy-start(f32[4]{0:T(128)} %constant.115) | copy-start | bytes 52
  1186.8 159.5 %copy-start.13 = (bf16[256,2048]{1,0:T(8,128)(2,1)S(1)}, bf16[256,2048]{1,0:T(8,128)(2,1)}, u32[]{:S(2)}) copy-start(bf16[256,2048]{1,0:T(8,128)(2,1)} %reduce-scatter.12.cloned.1.call-done) | copy-start | bytes 3145732
  1186.8 159.5 %copy-start.15 = (bf16[256,2048]{1,0:T(8,128)(2,1)S(1)}, bf16[256,2048]{1,0:T(8,128)(2,1)}, u32[]{:S(2)}) copy-start(bf16[256,2048]{1,0:T(8,128)(2,1)} %param.18) | copy-start | bytes 3145732
  1186.8 159.5 %copy-start.31 = (f32[1,2048]{1,0:T(1,128)S(1)}, f32[1,2048]{1,0:T(1,128)}, u32[]{:S(2)}) copy-start(f32[1,2048]{1,0:T(1,128)} %get-tuple-element.311) | copy-start | bytes 24580
  1186.8 159.5 %copy-start.41 = (f32[256]{0:T(256)S(1)}, f32[256]{0:T(256)}, u32[]{:S(2)}) copy-start(f32[256]{0:T(256)} %copy-done.40) | copy-start | bytes 3076
  1186.8 159.5 %copy-start.47 = (f32[256]{0:T(256)S(1)}, f32[256]{0:T(256)}, u32[]{:S(2)}) copy-start(f32[256]{0:T(256)} %copy-done.46) | copy-start | bytes 3076
  (53 other events, 1585.7 us)
Sparse Core Ops, SparseCore 0:
  10.5 57.0 all-gather.8
  69.8 80.7 all-gather.6
  202.8 75.2 reduce-scatter.11
  282.6 81.2 all-gather.10
  366.4 123.8 all-gather.12
  491.8 80.7 all-gather.14
  620.2 75.2 reduce-scatter.15
  701.7 81.2 all-gather.16
  786.5 69.7 reduce-scatter.31
  860.0 71.2 reduce-scatter.29
  934.8 71.2 reduce-scatter.27
  1010.1 41.1 reduce-scatter.25
  1055.2 41.1 reduce-scatter.23
  1100.5 41.2 reduce-scatter.19
  1145.5 41.1 reduce-scatter.21
  1189.0 76.7 reduce-scatter.17
  1267.9 78.3 reduce-scatter.13

commit v2 on v1

--- a/solution.py
+++ b/solution.py
@@ -1,6 +1,10 @@
+import functools
+
 import jax
 import jax.numpy as jnp
 from jax import lax
+from jax.experimental import pallas as pl
+from jax.experimental.pallas import tpu as pltpu
 from jax.sharding import PartitionSpec as P
 
 D = 2048
@@ -63,17 +67,6 @@
     )
 
 
-def norm_forward(field):
-    inv_scale = lax.rsqrt(jnp.mean(field * field, axis=-1, keepdims=True) + EPS_NORM)
-    return (field * inv_scale, inv_scale)
-
-
-def norm_backward(gradient, normed, inv_scale, gain_row):
-    scaled = gradient * gain_row
-    field_grad = inv_scale * (scaled - normed * jnp.mean(scaled * normed, axis=-1, keepdims=True))
-    return (field_grad, jnp.sum(gradient * normed, axis=0))
-
-
 def dot_transposed(left, right):
     return lax.dot_general(
         left, right, (((1,), (1,)), ((), ())), preferred_element_type=jnp.float32
@@ -135,6 +128,272 @@
         * score_scale
     )
     return ((key_sum, value_sum), query_grad)
+
+
+MESH = pl.DeviceIdType.MESH
+BLOCK = 32
+TILE = 256
+
+
+def line_kernel(n, parts, products, extras, outs, gathers, finish, *refs):
+    refs = list(refs)
+    take = lambda count: [refs.pop(0) for _ in range(count)]
+    lefts, rights, more, results = take(products), take(products), take(extras), take(outs)
+    gathered = take(1)[0] if gathers else None
+    if products:
+        totals, run_right, run_left, sums_sent, sums_got = take(5)
+    if gathers:
+        rows_sent, rows_got = take(2)
+    me = lax.axis_index("tensor")
+    has_left, has_right = me > 0, me < n - 1
+    rows = totals.shape[1] if products else gathered.shape[0] // n
+    part_rows = rows // parts
+    hops = n - 1
+
+    def sum_copy(way, part, hop):
+        slot = part * hops + hop
+        run = (run_right, run_left)[way]
+        return pltpu.make_async_remote_copy(
+            src_ref=run.at[slot],
+            dst_ref=run.at[slot],
+            send_sem=sums_sent.at[way, slot],
+            recv_sem=sums_got.at[way, slot],
+            device_id={"tensor": me + 1 - 2 * way},
+            device_id_type=MESH,
+        )
+
+    def product(dest):
+        first = pl.multiple_of(dest * rows, rows)
+
+        @pl.loop(0, totals.shape[2] // TILE)
+        def _(tile):
+            columns = pl.ds(pl.multiple_of(tile * TILE, TILE), TILE)
+            value = None
+            for left, right in zip(lefts, rights):
+                term = lax.dot_general(
+                    left[pl.ds(first, rows), :],
+                    right[columns, :],
+                    (((1,), (1,)), ((), ())),
+                    preferred_element_type=jnp.float32,
+                )
+                value = term if value is None else value + term
+            totals[dest, :, columns] = value
+
+    def pass_on(way, part, hop, dest):
+        run, slot = (run_right, run_left)[way], part * hops + hop
+        fed = (has_left, has_right)[way]
+        copy = sum_copy(way, part, hop)
+
+        @pl.when(fed)
+        def _():
+            copy.wait_recv()
+
+            @pl.loop(0, part_rows // BLOCK)
+            def _(block):
+                at = pl.multiple_of(block * BLOCK, BLOCK)
+                own = totals[dest, pl.ds(part * part_rows + at, BLOCK), :]
+                came = run[slot, pl.ds(at, BLOCK), :].astype(jnp.float32)
+                run[slot, pl.ds(at, BLOCK), :] = (own + came).astype(jnp.bfloat16)
+
+        @pl.when(jnp.logical_not(fed))
+        def _():
+            @pl.loop(0, part_rows // BLOCK)
+            def _(block):
+                at = pl.multiple_of(block * BLOCK, BLOCK)
+                own = totals[dest, pl.ds(part * part_rows + at, BLOCK), :]
+                run[slot, pl.ds(at, BLOCK), :] = own.astype(jnp.bfloat16)
+
+        copy.start()
+
+    def sum_step(part, hop):
+        far, near = n - 1 - hop, hop
+        if part == 0:
+            pl.when(far > me)(lambda: product(far))
+            pl.when(near < me)(lambda: product(near))
+            if hop == 0:
+                product(me)
+        pl.when(far > me)(lambda: pass_on(0, part, hop, far))
+        pl.when(near < me)(lambda: pass_on(1, part, hop, near))
+
+    def last_sum(part):
+        for way, fed, hop in ((0, has_left, n - 1 - me), (1, has_right, me)):
+            run = (run_right, run_left)[way]
+
+            @pl.when(fed)
+            def _():
+                sum_copy(way, part, hop).wait_recv()
+                slot = part * hops + hop
+
+                @pl.loop(0, part_rows // BLOCK)
+                def _(block):
+                    at = pl.multiple_of(block * BLOCK, BLOCK)
+                    own = pl.ds(part * part_rows + at, BLOCK)
+                    came = run[slot, pl.ds(at, BLOCK), :].astype(jnp.float32)
+                    totals[me, own, :] = totals[me, own, :] + came
+
+    def finish_part(part):
+        @pl.loop(0, part_rows // BLOCK)
+        def _(block):
+            at = pl.multiple_of(part * part_rows + block * BLOCK, BLOCK)
+            total = totals[me, pl.ds(at, BLOCK), :] if products else None
+            sent = finish(at, total, more, results)
+            if gathers:
+                gathered[pl.ds(pl.multiple_of(me * rows + at, BLOCK), BLOCK), :] = sent
+
+    def row_copy(way, part, hop, owner):
+        place = gathered.at[pl.ds(pl.multiple_of(owner * rows + part * part_rows, part_rows), part_rows), :]
+        slot = part * hops + hop
+        return pltpu.make_async_remote_copy(
+            src_ref=place,
+            dst_ref=place,
+            send_sem=rows_sent.at[way, slot],
+            recv_sem=rows_got.at[way, slot],
+            device_id={"tensor": me + 1 - 2 * way},
+            device_id_type=MESH,
+        )
+
+    def rows_start(part):
+        pl.when(has_right)(lambda: row_copy(0, part, 0, me).start())
+        pl.when(has_left)(lambda: row_copy(1, part, 0, me).start())
+
+    def rows_step(part, hop):
+        @pl.when(hop < me)
+        def _():
+            owner = me - 1 - hop
+            row_copy(0, part, hop, owner).wait_recv()
+            if hop + 1 < hops:
+                pl.when(has_right)(lambda: row_copy(0, part, hop + 1, owner).start())
+
+        @pl.when(hop < n - 1 - me)
+        def _():
+            owner = me + 1 + hop
+            row_copy(1, part, hop, owner).wait_recv()
+            if hop + 1 < hops:
+                pl.when(has_left)(lambda: row_copy(1, part, hop + 1, owner).start())
+
+    barrier = pltpu.get_barrier_semaphore()
+    for there, step in ((has_left, -1), (has_right, 1)):
+
+        @pl.when(there)
+        def _():
+            pl.semaphore_signal(barrier, inc=1, device_id={"tensor": me + step}, device_id_type=MESH)
+
+    pl.semaphore_wait(barrier, has_left.astype(jnp.int32) + has_right.astype(jnp.int32))
+
+    for result in results:
+        if result.shape[0] == 8:
+            result[...] = jnp.zeros_like(result)
+    for part in range(parts):
+        for hop in range(hops):
+            if products:
+                sum_step(part, hop)
+            if gathers and part > 0:
+                rows_step(part - 1, hop)
+        if products:
+            last_sum(part)
+        finish_part(part)
+        if gathers:
+            rows_start(part)
+    if gathers:
+        for hop in range(hops):
+            rows_step(parts - 1, hop)
+    for part in range(parts):
+        for hop in range(hops):
+            if products:
+                pl.when(n - 1 - hop > me)(lambda: sum_copy(0, part, hop).wait_send())
+                pl.when(hop < me)(lambda: sum_copy(1, part, hop).wait_send())
+            if gathers:
+                pl.when(has_right & (hop <= me))(lambda: row_copy(0, part, hop, me - hop).wait_send())
+                pl.when(has_left & (hop <= n - 1 - me))(
+                    lambda: row_copy(1, part, hop, me + hop).wait_send()
+                )
+
+
+def line_exchange(name, collective_id, pairs, extras, outs, rows, width, finish, gathers, parts):
+    n = lax.axis_size("tensor")
+    hops = n - 1
+    scratch = []
+    if pairs:
+        scratch = scratch + [
+            pltpu.VMEM((n, rows, width), jnp.float32),
+            pltpu.VMEM((parts * hops, rows // parts, width), jnp.bfloat16),
+            pltpu.VMEM((parts * hops, rows // parts, width), jnp.bfloat16),
+            pltpu.SemaphoreType.DMA((2, parts * hops)),
+            pltpu.SemaphoreType.DMA((2, parts * hops)),
+        ]
+    if gathers:
+        scratch = scratch + [
+            pltpu.SemaphoreType.DMA((2, parts * hops)),
+            pltpu.SemaphoreType.DMA((2, parts * hops)),
+        ]
+        outs = outs + [jax.ShapeDtypeStruct((n * rows, width), jnp.bfloat16)]
+    operands = [pair[0] for pair in pairs] + [pair[1] for pair in pairs] + list(extras)
+    depth = sum(pair[0].shape[1] for pair in pairs)
+    whole = pl.BlockSpec(memory_space=pltpu.VMEM)
+    return pl.pallas_call(
+        functools.partial(
+            line_kernel, n, parts, len(pairs), len(extras), len(outs) - gathers, gathers, finish
+        ),
+        out_shape=outs,
+        in_specs=[whole] * len(operands),
+        out_specs=[whole] * len(outs),
+        scratch_shapes=scratch,
+        compiler_params=pltpu.CompilerParams(
+            collective_id=collective_id, has_side_effects=True, vmem_limit_bytes=60 * 2**20
+        ),
+        cost_estimate=pl.CostEstimate(
+            flops=2 * n * rows * width * max(depth, 1),
+            bytes_accessed=200 * 2**20,
+            transcendentals=0,
+        ),
+        name=name,
+    )(*operands)
+
+
+def inverse_scale(field):
+    return lax.rsqrt(jnp.mean(field * field, axis=-1, keepdims=True) + EPS_NORM)
+
+
+def first_norm(at, total, more, results):
+    layer_in, gains = more
+    field = layer_in[pl.ds(at, BLOCK), :].astype(jnp.float32)
+    return (field * inverse_scale(field) * gains[0:1, :]).astype(jnp.bfloat16)
+
+
+def second_norm(at, total, more, results):
+    layer_in, gains = more
+    field = layer_in[pl.ds(at, BLOCK), :].astype(jnp.float32) + total
+    results[0][pl.ds(at, BLOCK), :] = field
+    return (field * inverse_scale(field) * gains[1:2, :]).astype(jnp.bfloat16)
+
+
+def norm_back(field, gradient, gain_row, gain_out):
+    inv_scale = inverse_scale(field)
+    normed = field * inv_scale
+    scaled = gradient * gain_row
+    back = inv_scale * (scaled - normed * jnp.mean(scaled * normed, axis=-1, keepdims=True))
+    product = gradient * normed
+    folded = product[0:8]
+    for k in range(8, BLOCK, 8):
+        folded = folded + product[k : k + 8]
+    gain_out[...] = gain_out[...] + folded
+    return back
+
+
+def second_back(at, total, more, results):
+    middle, cotangent, gains = more
+    rows = pl.ds(at, BLOCK)
+    back = norm_back(middle[rows, :], total, gains[1:2, :], results[1])
+    back = back + cotangent[rows, :].astype(jnp.float32)
+    results[0][rows, :] = back
+    return back.astype(jnp.bfloat16)
+
+
+def first_back(at, total, more, results):
+    layer_in, d_middle, gains = more
+    rows = pl.ds(at, BLOCK)
+    back = norm_back(layer_in[rows, :].astype(jnp.float32), total, gains[0:1, :], results[1])
+    results[0][rows, :] = back + d_middle[rows, :]
 
 
 def attn_rates():
@@ -177,10 +436,12 @@
     seg_blocks = segment.reshape(block_count, block_rows)
     pos_blocks = position.reshape(block_count, block_rows)
     score_scale = HEAD_DIM ** (-0.5)
-    layer_in = inputs.astype(jnp.float32)
-    normed_one, inv_one = norm_forward(layer_in)
-    first_in = lax.all_gather(
-        (normed_one * norm_gains[0]).astype(jnp.bfloat16), "tensor", axis=0, tiled=True
+    width = inputs.shape[1]
+    rows_f32 = jax.ShapeDtypeStruct((row_count, width), jnp.float32)
+    gain_f32 = jax.ShapeDtypeStruct((8, width), jnp.float32)
+    exchange = functools.partial(line_exchange, rows=row_count, width=width)
+    (first_in,) = exchange(
+        "first_norm", 1, [], [inputs, norm_gains], [], finish=first_norm, gathers=True, parts=1
     )
     attn_low = lax.all_gather(attn_weight.astype(jnp.bfloat16), "dp", axis=1, tiled=True)
 
@@ -201,15 +462,15 @@
 
     attended, log_totals = lax.map(forward_block, (query_blocks, seg_blocks, pos_blocks))
     attended = attended.reshape(seq_length, head_width)
-    middle = layer_in + lax.psum_scatter(
-        dot_transposed(attended, attn_low[3]).astype(jnp.bfloat16),
-        "tensor",
-        scatter_dimension=0,
-        tiled=True,
-    ).astype(jnp.float32)
-    normed_two, inv_two = norm_forward(middle)
-    second_in = lax.all_gather(
-        (normed_two * norm_gains[1]).astype(jnp.bfloat16), "tensor", axis=0, tiled=True
+    middle, second_in = exchange(
+        "attention_out",
+        2,
+        [(attended, attn_low[3])],
+        [inputs, norm_gains],
+        [rows_f32],
+        finish=second_norm,
+        gathers=True,
+        parts=2,
     )
     mlp_low = lax.all_gather(mlp_weight.astype(jnp.bfloat16), "dp", axis=1, tiled=True)
     gate_proj = jnp.dot(second_in, mlp_low[0], preferred_element_type=jnp.float32)
@@ -246,17 +507,16 @@
             to_owner(down_grad),
         ]
     )
-    d_second = lax.psum_scatter(
-        (dot_transposed(d_gate, mlp_back[0]) + dot_transposed(d_up, mlp_back[1])).astype(
-            jnp.bfloat16
-        ),
-        "tensor",
-        scatter_dimension=0,
-        tiled=True,
-    ).astype(jnp.float32)
-    d_middle, gain_two = norm_backward(d_second, normed_two, inv_two, norm_gains[1])
-    d_middle = d_middle + cotangent.astype(jnp.float32)
-    d_attn = lax.all_gather(d_middle.astype(jnp.bfloat16), "tensor", axis=0, tiled=True)
+    d_middle, gain_two, d_attn = exchange(
+        "mlp_back",
+        3,
+        [(d_gate, mlp_back[0]), (d_up, mlp_back[1])],
+        [middle, cotangent, norm_gains],
+        [rows_f32, gain_f32],
+        finish=second_back,
+        gathers=True,
+        parts=2,
+    )
     out_proj_grad = dot_over_rows(d_attn, attended)
     d_attended = jnp.dot(d_attn, attn_back[3], preferred_element_type=jnp.float32).astype(
         jnp.bfloat16
@@ -292,19 +552,17 @@
             to_owner(out_proj_grad),
         ]
     )
-    d_first = lax.psum_scatter(
-        (
-            dot_transposed(query_raw, attn_back[0])
-            + dot_transposed(key_raw, attn_back[1])
-            + dot_transposed(value_raw, attn_back[2])
-        ).astype(jnp.bfloat16),
-        "tensor",
-        scatter_dimension=0,
-        tiled=True,
-    ).astype(jnp.float32)
-    d_input, gain_one = norm_backward(d_first, normed_one, inv_one, norm_gains[0])
-    grad_in = d_input + d_middle
-    gain_grad = lax.psum(jnp.stack([gain_one, gain_two]), ("dp", "tensor"))
+    grad_in, gain_one = exchange(
+        "attention_back",
+        4,
+        [(query_raw, attn_back[0]), (key_raw, attn_back[1]), (value_raw, attn_back[2])],
+        [inputs, d_middle, norm_gains],
+        [rows_f32, gain_f32],
+        finish=first_back,
+        gathers=False,
+        parts=1,
+    )
+    gain_grad = lax.psum(jnp.stack([jnp.sum(gain_one, axis=0), jnp.sum(gain_two, axis=0)]), ("dp", "tensor"))
     gain_first_new, gain_second_new, gain_new = adam_update(
         norm_gains, gain_grad, gain_first, gain_second, GAIN_RATE
     )

time: 1370 us -> 1250 us (0.912)
  waiting for transfers between devices: 862 us -> 183 us
  Pallas kernels: 0 us -> 588 us
  matrix products: 269 us -> 233 us
  local copies, waits for them, and re-layouts: 79.4 us -> 105 us
  other arithmetic: 88 us -> 72.2 us
    pallas_call x0 -> x4, Pallas kernels: none -> 588 us  [line_exchange(): pl.pallas_call(functools.partial(line_kernel, n, parts, len(pairs), len(e...]
    reduce_scatter x3 -> x0, waiting for transfers between devices: 223 us -> none  [the longest x1 75.4 us: local(): lax.psum_scatter(dot_transposed(attended, attn_low[3]).astype(jnp.bfloat1...]
    all_gather x3 -> x0, waiting for transfers between devices: 182 us -> none  [the longest x1 75.8 us: local(): lax.all_gather((normed_two * norm_gains[1]).astype(jnp.bfloat16), 'tensor...]
    all_gather x1, waiting for transfers between devices: 126 us -> 0.02 us  [local(): lax.all_gather(mlp_weight.astype(jnp.bfloat16), 'dp', axis=1, tiled=True)]
    all_gather x1, waiting for transfers between devices: 53.4 us -> 0.01 us  [local(): grad_out = lax.all_gather(cotangent, 'tensor', axis=0, tiled=True)]
    all_gather x1, waiting for transfers between devices: 53.1 us -> 0.02 us  [local(): lax.all_gather(attn_weight.astype(jnp.bfloat16), 'dp', axis=1, tiled=True)]
    dot_general x7 -> x1, matrix products: 60.6 us -> 14.3 us  [dot_transposed(): lax.dot_general(left, right, (((1,), (1,)), ((), ())), preferred_element_...]
    reduce_scatter x1, waiting for transfers between devices: 34.8 us -> 0.02 us  [local(): lax.psum_scatter(dot_transposed(hidden, mlp_low[2]).astype(jnp.bfloat16),...]
  transfers between devices with their start and end apart: 17 -> 11, of which waited for: 15 -> 3; matrix products, arithmetic and copies ran while one was open for 23% -> 28% of each run, Pallas kernels for 0% -> 34%
where the time goes in v2:
time: 1250 us; the launch traced here: 1240 us
  Pallas kernels  588 us (47%)
  matrix products  233 us (19%)
  waiting for transfers between devices  183 us (15%)
  local copies, waits for them, and re-layouts  105 us (8%)
  other arithmetic  72.2 us (6%)
  blocking collectives  38.4 us (3%)
  between operations  14.5 us (1%)
    pallas_call x4, Pallas kernels, line_exchange(): pl.pallas_call(functools.partial(line_kernel, n, parts, len(pairs), len(e...  588 us
    reduce_scatter x7, waiting for transfers between devices, to_owner(): lax.psum_scatter(partial.astype(jnp.bfloat16), 'dp', scatter_dimension=0,...  182 us
    dot_general x7, matrix products, dot_over_rows(): lax.dot_general(left, right, (((0,), (0,)), ((), ())), preferred_element_...  64.4 us
    dynamic_update_slice x4, local copies, waits for them, and re-layouts, local(): lax.scan(back_block, (empty_sum, empty_sum), (query_blocks, grad_blocks,...  41.3 us
    psum x1, blocking collectives, local(): lax.psum(jnp.stack([jnp.sum(gain_one, axis=0), jnp.sum(gain_two, axis=0)]...  38.4 us
  transfers between devices with their start and end apart: 11, of which 3 were waited for; matrix products, arithmetic and copies ran while one was open for 28% of the time, Pallas kernels for 34%

profile of v2, /device:TPU:0, one launch (start us, length us, event | category | flops | bytes accessed | tf_op | source)
XLA Modules:
  0.0 1235.5 jit_solution(8034704964647195223)
XLA Ops:
  16.8 78.3 %first_norm.1 = bf16[1024,2048]{1,0:T(8,128)(2,1)} custom-call(bf16[256,2048]{1,0:T(8,128)(2,1)} %refs_6_.3, f32[2,2048]{1,0:T(2,128)} %refs_8_.1), custom_call_target="tpu_custom_call" | custom-call | flops 4194304 | bytes 209715200 | tf_op jit(solution)/shard_map/first_norm/pallas_call | solution.py:333
  132.5 31.0 %while.27 = (s32[]{:T(128)}, bf16[2,512,8,64]{1,3,2,0:T(8,128)(2,1)S(1)}, f32[2,8,512]{2,1,0:T(8,128)}, s32[2,512]{1,0:T(2,128)S(1)}, s32[1024]{0:T(1024)S(1)}, ...) while((s32[]{:T(128)}, ...), condition=%wide.region_6.7_spmd, body=%wide.region_3.6_spmd.sunk | while | flops 1125904384 | bytes 55726212 | solution.py:463
  166.2 209.3 %attention_out.1 = (f32[256,2048]{1,0:T(8,128)}, bf16[1024,2048]{1,0:T(8,128)(2,1)}) custom-call(bf16[1024,512]{1,0:T(8,128)(2,1)} %copy.59.refs_0_, bf16[2048,512]{1,0:T(8,128)(2,1)} %get-tuple-element.310.refs_1_, bf16[256,2048]{1,0:T(8,128)(2,1)} %refs_6_.3, f32[2,2048]{1,0:T(2,128)} %refs_8_.1), custom_call_target="tpu_custom_call" | custom-call | flops 2147483648 | bytes 209715200 | tf_op jit(solution)/shard_map/attention_out/pallas_call | solution.py:333
  375.6 13.7 %slice_bitcast_fusion.1 = (bf16[2048,2048]{1,0:T(8,128)(2,1)}, bf16[2048,2048]{1,0:T(8,128)(2,1)}) fusion(bf16[3,2048,2048]{2,1,0:T(8,128)(2,1)} %all-gather.6.cloned.1.call-done), kind=kLoop, calls=%fused_computation.47 | loop fusion | bytes 33554432 | tf_op jit(solution)/shard_map/squeeze | solution.py:477
  394.4 12.8 %fusion.48 = f32[1024,2048]{1,0:T(8,128)} fusion(bf16[1024,2048]{1,0:T(8,128)(2,1)} %get-tuple-element.145, bf16[3,2048,2048]{2,1,0:T(8,128)(2,1)S(1)} %copy-done.5), kind=kOutput, calls=%fused_computation.119 | convolution fusion | flops 8589934592 | bytes 20971520 | tf_op jit(solution)/shard_map/dot_general | solution.py:476
  407.2 12.8 %fusion.49 = f32[1024,2048]{1,0:T(8,128)} fusion(bf16[1024,2048]{1,0:T(8,128)(2,1)} %get-tuple-element.145, bf16[3,2048,2048]{2,1,0:T(8,128)(2,1)S(1)} %copy-done.5), kind=kOutput, calls=%fused_computation.120 | convolution fusion | flops 8589934592 | bytes 20971520 | tf_op jit(solution)/shard_map/dot_general | solution.py:477
  420.0 21.6 %multiply_convert_fusion.1 = (bf16[1024,2048]{1,0:T(8,128)(2,1)}, bf16[1024,2048]{1,0:T(8,128)(2,1)}, bf16[1024,2048]{1,0:T(8,128)(2,1)}) fusion(f32[1024,2048]{1,0:T(8,128)} %fusion.48, f32[1024,2048]{1,0:T(8,128)} %fusion.49, bf16[1024,2048]{1,0:T(8,128)(2,1)} %all-gather.8.cloned.1.call-done, bf16[3,2048,2048]{2,1,0:T(8,128)(2,1)} %all-gather.6.cloned.1.call-done), kind=kOutput, calls=%fused_computation.50 | convolution fusion | flops 8621391872 | bytes 41943040 | tf_op jit(solution)/shard_map/dot_general | solution.py:491
  441.6 168.3 %mlp_back.1 = (f32[256,2048]{1,0:T(8,128)}, f32[8,2048]{1,0:T(8,128)}, bf16[1024,2048]{1,0:T(8,128)(2,1)}) custom-call(bf16[1024,2048]{1,0:T(8,128)(2,1)} %get-tuple-element.304.refs_0_, bf16[1024,2048]{1,0:T(8,128)(2,1)} %get-tuple-element.303.refs_1_, bf16[2048,2048]{1,0:T(8,128)(2,1)} %get-tuple-element.302.refs_2_, ...), custom_call_target="tpu_custom_call" | custom-call | flops 17179869184 | bytes 209715200 | tf_op jit(solution)/shard_map/mlp_back/pallas_call | solution.py:333
  627.3 134.6 %while.28 = (s32[]{:T(128)}, f32[1024,8,64]{0,2,1:T(8,128)}, f32[1024,8,64]{0,2,1:T(8,128)}, f32[2,512,8,64]{1,0,3,2:T(2,128)}, bf16[2,512,8,64]{1,3,2,0:T(8,128...) while((s32[]{:T(128)}, f32[1024,8,64]{0,2,1:T(8,128)}, ...), condition=%wide.region_10.11_spmd.clone, body=%wide.region_8.10_spmd.clone.sunk | while | flops 2726555648 | bytes 313626976 | solution.py:530
  635.1 11.3 multiply_reduce_fusion.2
  646.7 9.5 multiply_convert_fusion.5
  674.7 19.6 %dynamic_update_slice.20 = f32[2,512,8,64]{1,0,3,2:T(2,128)} dynamic-update-slice(f32[2,512,8,64]{1,0,3,2:T(2,128)} %get-tuple-element.538, f32[1,512,8,64]{1,0,3,2:T(1,128)S(1)} %copy.80, s32[]{:T(128)S(6)} %copy.98, s32[]{:T(128)} %constant.41.clone.1..sunk, s32[]{:T(128)} %constant.41.clone.1..sunk, s32[]{:T(128)} %constant.41.clone.1..sunk) | dynamic-update-slice | bytes 2097156 | tf_op jit(solution)/shard_map/while/body/jit(dynamic_update_index_in_dim)/dynamic_update_slice | solution.py:530
  702.0 10.9 multiply_reduce_fusion.2
  742.1 19.6 %dynamic_update_slice.20 = f32[2,512,8,64]{1,0,3,2:T(2,128)} dynamic-update-slice(f32[2,512,8,64]{1,0,3,2:T(2,128)} %get-tuple-element.538, f32[1,512,8,64]{1,0,3,2:T(1,128)S(1)} %copy.80, s32[]{:T(128)S(6)} %copy.98, s32[]{:T(128)} %constant.41.clone.1..sunk, s32[]{:T(128)} %constant.41.clone.1..sunk, s32[]{:T(128)} %constant.41.clone.1..sunk) | dynamic-update-slice | bytes 2097156 | tf_op jit(solution)/shard_map/while/body/jit(dynamic_update_index_in_dim)/dynamic_update_slice | solution.py:530
  786.9 14.3 %fusion.40 = bf16[1024,2048]{1,0:T(8,128)(2,1)} fusion(bf16[1024,2048]{1,0:T(8,128)(2,1)} %get-tuple-element.305, bf16[3,2048,2048]{2,1,0:T(8,128)(2,1)} %all-gather.6.cloned.1.call-done), kind=kOutput, calls=%fused_computation.68 | convolution fusion | flops 8592031744 | bytes 16777216 | tf_op jit(solution)/shard_map/dot_general | solution.py:71
  801.3 14.0 %convert_bitcast_fusion = bf16[2048,2048]{1,0:T(8,128)(2,1)} fusion(bf16[1024,2048]{1,0:T(8,128)(2,1)} %get-tuple-element.305, bf16[1024,2048]{1,0:T(8,128)(2,1)} %all-gather.8.cloned.1.call-done), kind=kOutput, calls=%fused_computation.49 | convolution fusion | flops 8594128896 | bytes 16777216 | tf_op jit(solution)/shard_map/dot_general | solution.py:77
  815.3 14.4 %convolution_convert_fusion = bf16[2048,2048]{1,0:T(8,128)(2,1)} fusion(bf16[1024,2048]{1,0:T(8,128)(2,1)} %get-tuple-element.145, bf16[1024,2048]{1,0:T(8,128)(2,1)} %get-tuple-element.303.refs_1_), kind=kOutput, calls=%fused_computation.55 | convolution fusion | flops 8594128896 | bytes 16777216 | tf_op jit(solution)/shard_map/dot_general | solution.py:77
  829.8 14.4 %convolution_convert_fusion.1 = bf16[2048,2048]{1,0:T(8,128)(2,1)} fusion(bf16[1024,2048]{1,0:T(8,128)(2,1)} %get-tuple-element.145, bf16[1024,2048]{1,0:T(8,128)(2,1)} %get-tuple-element.304.refs_0_), kind=kOutput, calls=%fused_computation.56 | convolution fusion | flops 8594128896 | bytes 16777216 | tf_op jit(solution)/shard_map/dot_general | solution.py:77
  848.3 132.6 %attention_back.1 = (f32[256,2048]{1,0:T(8,128)}, f32[8,2048]{1,0:T(8,128)}) custom-call(bf16[1024,512]{1,0:T(8,128)(2,1)} %copy.63.refs_0_, bf16[1024,512]{1,0:T(8,128)(2,1)} %copy.64.refs_1_, bf16[1024,512]{1,0:T(8,128)(2,1)} %copy.65.refs_2_, bf16[2048,512]{1,0:T(8,128)(2,1)} %get-tuple-element.312.refs_3_, bf16[2048,512]{1,0:T(8,128)(2,1)} %get-tuple-element.311.refs_4_, ...), custom_call_target="tpu_custom_call" | custom-call | flops 6442450944 | bytes 209715200 | tf_op jit(solution)/shard_map/attention_back/pallas_call | solution.py:333
  981.8 38.4 %psum.7 = f32[2,2048]{1,0:T(2,128)S(1)} all-reduce(f32[2,2048]{1,0:T(2,128)S(1)} %pad_maximum_fusion.3), channel_id=1, replica_groups=mesh['dp'=8,'tensor'=4] {'dp','tensor'}, use_global_device_ids=true, to_apply=%region_13.14 | all-reduce | flops 4096 | bytes 32768 | tf_op jit(solution)/shard_map/psum | solution.py:565
  1030.1 32.0 %reduce-scatter.23.cloned.1.call-done = bf16[256,2048]{1,0:T(8,128)(2,1)} async-done(((bf16[2048,2048]{1,0:T(8,128)(2,1)}), bf16[256,2048]{1,0:T(8,128)(2,1)}) %reduce-scatter.23.cloned.1.call-update) | async-done | bytes 1048592 | tf_op jit(solution)/shard_map/reduce_scatter | solution.py:499
  1062.1 74.6 %reduce-scatter.21.cloned.1.call-done = bf16[256,2048]{1,0:T(8,128)(2,1)} async-done(((bf16[2048,2048]{1,0:T(8,128)(2,1)}), bf16[256,2048]{1,0:T(8,128)(2,1)}) %reduce-scatter.21.cloned.1.call-update) | async-done | bytes 1048592 | tf_op jit(solution)/shard_map/reduce_scatter | solution.py:499
  1136.7 75.2 %reduce-scatter.19.cloned.1.call-done = bf16[256,2048]{1,0:T(8,128)(2,1)} async-done(((bf16[2048,2048]{1,0:T(8,128)(2,1)}), bf16[256,2048]{1,0:T(8,128)(2,1)}) %reduce-scatter.19.cloned.1.call-update) | async-done | bytes 1048592 | tf_op jit(solution)/shard_map/reduce_scatter | solution.py:499
  1211.9 15.5 %multiply_subtract_fusion = (f32[3,256,2048]{2,1,0:T(8,128)}, f32[3,256,2048]{2,1,0:T(8,128)}, f32[3,256,2048]{2,1,0:T(8,128)}, f32[3,256,2048]{2,1,0:T(8,128)}) fusion(f32[3,256,2048]{2,1,0:T(8,128)} %param.22, f32[3,256,2048]{2,1,0:T(8,128)} %param.28, f32[3,256,2048]{2,1,0:T(8,128)} %param.25, bf16[1,256,2048]{2,1,0:T(8,128)(2,1)} %bitcast.207, ...), kind=kLoop, calls=%fused_computation.60 | loop fusion | flops 28311552 | bytes 47185920 | tf_op jit(solution)/shard_map/sub | solution.py:408
  (181 shorter events, 207.4 us)
Async XLA Ops:
  7.2 88.5 %all-gather.4.cloned.1.call-start = ((), (), s32[]{:S(2)}) async-start(), calls=%async_computation.8 | async-start | bytes 9437184 | tf_op jit(solution)/shard_map/all_gather | solution.py:446
  9.9 365.6 %all-gather.6.cloned.1.call-start = ((), (), s32[]{:S(2)}) async-start(), calls=%async_computation.9 | async-start | bytes 28311552 | tf_op jit(solution)/shard_map/all_gather | solution.py:475
  15.0 405.0 %all-gather.8.cloned.1.call-start = ((), (), s32[]{:S(2)}) async-start(), calls=%async_computation.11 | async-start | bytes 5242880 | tf_op jit(solution)/shard_map/all_gather | solution.py:490
  15.7 1005.2 %reduce-scatter.17.cloned.1.call-start = ((), (), s32[]{:S(2)}) async-start(), calls=%async_computation.15 | async-start | bytes 2359296 | tf_op jit(solution)/shard_map/reduce_scatter | solution.py:499
  95.7 22.6 %copy-start.13 = (f32[1024,32]{0,1:T(8,128)}, f32[1024,32]{0,1:T(8,128)S(1)}, u32[]{:S(2)}) copy-start(f32[1024,32]{0,1:T(8,128)S(1)} %get-tuple-element.325) | copy-start | bytes 393220
  95.7 22.6 %copy-start.15 = (f32[1024,32]{0,1:T(8,128)}, f32[1024,32]{0,1:T(8,128)S(1)}, u32[]{:S(2)}) copy-start(f32[1024,32]{0,1:T(8,128)S(1)} %get-tuple-element.326) | copy-start | bytes 393220
  375.6 18.9 %copy-start.5 = (bf16[3,2048,2048]{2,1,0:T(8,128)(2,1)S(1)}, bf16[3,2048,2048]{2,1,0:T(8,128)(2,1)}, u32[]{:S(2)}) copy-start(bf16[3,2048,2048]{2,1,0:T(8,128)(2,1)} %all-gather.6.cloned.1.call-done) | copy-start | bytes 75497472
  627.1 393.8 %reduce-scatter.15.cloned.1.call-start = ((), (), s32[]{:S(2)}) async-start(), calls=%async_computation.14 | async-start | bytes 2359296 | tf_op jit(solution)/shard_map/reduce_scatter | solution.py:499
  673.6 20.7 %copy-start.4 = (bf16[1024,8,64]{0,2,1:T(8,128)(2,1)S(1)}, bf16[1024,8,64]{0,2,1:T(8,128)(2,1)}, u32[]{:S(2)}) copy-start(bf16[1024,8,64]{0,2,1:T(8,128)(2,1)} %copy-done.3) | copy-start | bytes 3145732 | tf_op jit(solution)/shard_map/while
  722.6 14.5 %slice-start = ((s8[8388608]{0:T(1024)(128)(4,1)}), s8[4194304]{0:T(1024)(128)(4,1)S(1)}, s32[]{:S(2)}) async-start(s8[8388608]{0:T(1024)(128)(4,1)} %bitcast.191), calls=%async_computation.19 | async-start | bytes 8388608 | tf_op jit(solution)/shard_map/while
  741.0 20.7 %copy-start.4 = (bf16[1024,8,64]{0,2,1:T(8,128)(2,1)S(1)}, bf16[1024,8,64]{0,2,1:T(8,128)(2,1)}, u32[]{:S(2)}) copy-start(bf16[1024,8,64]{0,2,1:T(8,128)(2,1)} %copy-done.3) | copy-start | bytes 3145732 | tf_op jit(solution)/shard_map/while
  769.6 251.3 %reduce-scatter.13.cloned.1.call-start = ((), (), s32[]{:S(2)}) async-start(), calls=%async_computation.13 | async-start | bytes 2359296 | tf_op jit(solution)/shard_map/reduce_scatter | solution.py:499
  780.8 240.1 %reduce-scatter.11.cloned.1.call-start = ((), (), s32[]{:S(2)}) async-start(), calls=%async_computation.12 | async-start | bytes 2359296 | tf_op jit(solution)/shard_map/reduce_scatter | solution.py:499
  786.9 240.0 %reduce-scatter.9.cloned.1.call-start = ((), (), s32[]{:S(2)}) async-start(), calls=%async_computation.10 | async-start | bytes 5242880 | tf_op jit(solution)/shard_map/reduce_scatter | solution.py:480
  801.2 260.9 %reduce-scatter.23.cloned.1.call-start = ((), (), s32[]{:S(2)}) async-start(), calls=%async_computation.18 | async-start | bytes 9437184 | tf_op jit(solution)/shard_map/reduce_scatter | solution.py:499
  815.3 321.4 %reduce-scatter.21.cloned.1.call-start = ((), (), s32[]{:S(2)}) async-start(), calls=%async_computation.17 | async-start | bytes 9437184 | tf_op jit(solution)/shard_map/reduce_scatter | solution.py:499
  829.8 382.1 %reduce-scatter.19.cloned.1.call-start = ((), (), s32[]{:S(2)}) async-start(), calls=%async_computation.16 | async-start | bytes 9437184 | tf_op jit(solution)/shard_map/reduce_scatter | solution.py:499
  848.2 132.6 %copy-start.21 = (f32[8,2048]{1,0:T(8,128)S(1)}, f32[8,2048]{1,0:T(8,128)}, u32[]{:S(2)}) copy-start(f32[8,2048]{1,0:T(8,128)} %get-tuple-element.154) | copy-start | bytes 196612
  848.2 172.0 %copy-start.19 = (f32[2,2048]{1,0:T(2,128)S(1)}, f32[2,2048]{1,0:T(2,128)}, u32[]{:S(2)}) copy-start(f32[2,2048]{1,0:T(2,128)} %refs_8_.1) | copy-start | bytes 49156
  848.2 172.0 %copy-start.22 = (f32[2,2048]{1,0:T(2,128)S(1)}, f32[2,2048]{1,0:T(2,128)}, u32[]{:S(2)}) copy-start(f32[2,2048]{1,0:T(2,128)} %param.26) | copy-start | bytes 49156
  848.2 172.0 %copy-start.23 = (f32[2,2048]{1,0:T(2,128)S(1)}, f32[2,2048]{1,0:T(2,128)}, u32[]{:S(2)}) copy-start(f32[2,2048]{1,0:T(2,128)} %param.23) | copy-start | bytes 49156
  848.2 172.7 %copy-start.6 = (f32[4,256,512]{2,1,0:T(8,128)S(1)}, f32[4,256,512]{2,1,0:T(8,128)}, u32[]{:S(2)}) copy-start(f32[4,256,512]{2,1,0:T(8,128)} %param.21) | copy-start | bytes 6291460
  848.3 172.7 %copy-start.24 = (f32[4]{0:T(128)S(1)}, f32[4]{0:T(128)}, u32[]{:S(2)}) copy-start(f32[4]{0:T(128)} %constant.71) | copy-start | bytes 52
  1211.9 15.5 %copy-start.9 = (f32[256,2048]{1,0:T(8,128)S(1)}, f32[256,2048]{1,0:T(8,128)}, u32[]{:S(2)}) copy-start(f32[256,2048]{1,0:T(8,128)} %get-tuple-element.580) | copy-start | bytes 6291460
  (21 other events, 150.7 us)
Sparse Core Ops, SparseCore 0:
  10.5 57.0 all-gather.3
  70.1 125.3 all-gather.5
  197.0 108.4 all-gather.7
  627.2 37.0 reduce-scatter.16
  769.7 37.1 reduce-scatter.14
  810.6 41.1 reduce-scatter.12
  855.5 41.2 reduce-scatter.10
  899.7 87.9 reduce-scatter.8
  991.6 70.4 reduce-scatter.22
  1065.4 71.2 reduce-scatter.20
  1140.6 71.2 reduce-scatter.18

commit v3 on v0

v3 whole, which is shorter than its diff:
```python
import functools

import jax
import jax.numpy as jnp
from jax import lax
from jax.experimental import pallas as pl
from jax.experimental.pallas import tpu as pltpu
from jax.sharding import PartitionSpec as P

D = 2048
HEAD_DIM = 64
STEP = 10


EPS_NORM = 1e-05
ROPE_BASE = 130000.0
BETA_ONE = 0.9
BETA_TWO = 0.95
EPS_ADAM = 1e-08
WEIGHT_DECAY = 0.1
GAIN_RATE = 0.3
MASKED = -1e30


def doc_layout(lengths, seq_length):
    doc_ends = jnp.cumsum(lengths)
    starts = doc_ends - lengths
    places = jnp.arange(seq_length, dtype=jnp.int32)
    segment = jnp.sum((places[:, None] >= doc_ends[None, :]).astype(jnp.int32), axis=1)
    owners = segment[:, None] == jnp.arange(lengths.shape[0], dtype=jnp.int32)[None, :]
    position = places - jnp.sum(jnp.where(owners, starts[None, :], 0), axis=1)
    return (segment, position)


def rope_tables(position):
    half_dim = HEAD_DIM // 2
    frequencies = jnp.power(
        jnp.float32(ROPE_BASE), -2.0 * jnp.arange(half_dim, dtype=jnp.float32) / HEAD_DIM
    )
    angles = position.astype(jnp.float32)[:, None] * frequencies[None, :]
    cosine, sine = jnp.cos(angles), jnp.sin(angles)
    return (
        jnp.concatenate([cosine, cosine] * 2, axis=1),
        jnp.concatenate([-sine, sine] * 2, axis=1),
    )


MESH = pl.DeviceIdType.MESH
BLOCK = 32
TILE = 256


def whole_part(count):
    return [pl.BlockSpec(memory_space=pltpu.VMEM)] * count


def greet(n, me):
    barrier = pltpu.get_barrier_semaphore()
    for there, step in ((me > 0, -1), (me < n - 1, 1)):

        @pl.when(there)
        def _():
            pl.semaphore_signal(barrier, inc=1, device_id={"tensor": me + step}, device_id_type=MESH)

    pl.semaphore_wait(barrier, (me > 0).astype(jnp.int32) + (me < n - 1).astype(jnp.int32))


def blocks_of(count, body):
    @pl.loop(0, count // BLOCK)
    def _(block):
        body(pl.multiple_of(block * BLOCK, BLOCK))


class RowGather:
    def __init__(self, n, me, parts, place, sent, got):
        self.n, self.me, self.parts, self.place = n, me, parts, place
        self.sent, self.got = sent, got
        self.rows = place.shape[0] // n
        self.has_left, self.has_right = me > 0, me < n - 1

    def copy(self, way, part, hop, owner):
        count = self.rows // self.parts
        first = pl.multiple_of(owner * self.rows + part * count, count)
        block = self.place.at[pl.ds(first, count), :]
        slot = part * (self.n - 1) + hop
        return pltpu.make_async_remote_copy(
            src_ref=block,
            dst_ref=block,
            send_sem=self.sent.at[way, slot],
            recv_sem=self.got.at[way, slot],
            device_id={"tensor": self.me + 1 - 2 * way},
            device_id_type=MESH,
        )

    def start(self, part):
        pl.when(self.has_right)(lambda: self.copy(0, part, 0, self.me).start())
        pl.when(self.has_left)(lambda: self.copy(1, part, 0, self.me).start())

    def step(self, part, hop):
        last = hop + 1 == self.n - 1

        @pl.when(hop < self.me)
        def _():
            owner = self.me - 1 - hop
            self.copy(0, part, hop, owner).wait_recv()
            if not last:
                pl.when(self.has_right)(lambda: self.copy(0, part, hop + 1, owner).start())

        @pl.when(hop < self.n - 1 - self.me)
        def _():
            owner = self.me + 1 + hop
            self.copy(1, part, hop, owner).wait_recv()
            if not last:
                pl.when(self.has_left)(lambda: self.copy(1, part, hop + 1, owner).start())

    def drain(self):
        for part in range(self.parts):
            for hop in range(self.n - 1):
                pl.when(self.has_right & (hop <= self.me))(
                    lambda: self.copy(0, part, hop, self.me - hop).wait_send()
                )
                pl.when(self.has_left & (hop <= self.n - 1 - self.me))(
                    lambda: self.copy(1, part, hop, self.me + hop).wait_send()
                )


class SumScatter:
    def __init__(self, n, me, parts, lefts, rights, totals, runs, sent, got):
        self.n, self.me, self.parts = n, me, parts
        self.lefts, self.rights, self.totals, self.runs = lefts, rights, totals, runs
        self.sent, self.got = sent, got
        self.rows = totals.shape[1]
        self.fed = (me > 0, me < n - 1)

    def copy(self, way, part, hop):
        slot = part * (self.n - 1) + hop
        run = self.runs[way].at[slot]
        return pltpu.make_async_remote_copy(
            src_ref=run,
            dst_ref=run,
            send_sem=self.sent.at[way, slot],
            recv_sem=self.got.at[way, slot],
            device_id={"tensor": self.me + 1 - 2 * way},
            device_id_type=MESH,
        )

    def product(self, dest):
        first = pl.multiple_of(dest * self.rows, self.rows)

        @pl.loop(0, self.totals.shape[2] // TILE)
        def _(tile):
            columns = pl.ds(pl.multiple_of(tile * TILE, TILE), TILE)
            value = None
            for left, right in zip(self.lefts, self.rights):
                term = lax.dot_general(
                    left[pl.ds(first, self.rows), :],
                    right[columns, :],
                    (((1,), (1,)), ((), ())),
                    preferred_element_type=jnp.float32,
                )
                value = term if value is None else value + term
            self.totals[dest, :, columns] = value.astype(self.totals.dtype)

    def dests(self, hop):
        far, near = self.n - 1 - hop, hop
        return ((0, far, far > self.me), (1, near, near < self.me))

    def products(self, hop):
        for way, dest, needed in self.dests(hop):
            pl.when(needed)(lambda: self.product(dest))

    def open(self, part, hop):
        for way, dest, needed in self.dests(hop):
            run, slot = self.runs[way], part * (self.n - 1) + hop
            first = part * (self.rows // self.parts)

            @pl.when(needed & jnp.logical_not(self.fed[way]))
            def _():
                def body(at):
                    own = self.totals[dest, pl.ds(first + at, BLOCK), :]
                    run[slot, pl.ds(at, BLOCK), :] = own.astype(jnp.bfloat16)

                blocks_of(self.rows // self.parts, body)
                self.copy(way, part, hop).start()

    def pass_on(self, part, hop):
        for way, dest, needed in self.dests(hop):
            run, slot = self.runs[way], part * (self.n - 1) + hop
            first = part * (self.rows // self.parts)

            @pl.when(needed & self.fed[way])
            def _():
                self.copy(way, part, hop).wait_recv()

                def body(at):
                    own = self.totals[dest, pl.ds(first + at, BLOCK), :].astype(jnp.float32)
                    came = run[slot, pl.ds(at, BLOCK), :].astype(jnp.float32)
                    run[slot, pl.ds(at, BLOCK), :] = (own + came).astype(jnp.bfloat16)

                blocks_of(self.rows // self.parts, body)
                self.copy(way, part, hop).start()

    def last(self, part):
        first = part * (self.rows // self.parts)
        for way, hop in ((0, self.n - 1 - self.me), (1, self.me)):
            run = self.runs[way]

            @pl.when(self.fed[way])
            def _():
                self.copy(way, part, hop).wait_recv()
                slot = part * (self.n - 1) + hop

                def body(at):
                    own = pl.ds(first + at, BLOCK)
                    came = run[slot, pl.ds(at, BLOCK), :].astype(jnp.float32)
                    total = self.totals[self.me, own, :].astype(jnp.float32) + came
                    self.totals[self.me, own, :] = total.astype(self.totals.dtype)

                blocks_of(self.rows // self.parts, body)

    def drain(self):
        for part in range(self.parts):
            for hop in range(self.n - 1):
                for way, dest, needed in self.dests(hop):
                    pl.when(needed)(lambda: self.copy(way, part, hop).wait_send())


def scatter_scratch(n, parts, rows, width, kept=jnp.float32):
    slots = parts * (n - 1)
    return [
        pltpu.VMEM((n, rows, width), kept),
        pltpu.VMEM((slots, rows // parts, width), jnp.bfloat16),
        pltpu.VMEM((slots, rows // parts, width), jnp.bfloat16),
        pltpu.SemaphoreType.DMA((2, slots)),
        pltpu.SemaphoreType.DMA((2, slots)),
    ]


def gather_scratch(n, parts):
    return [pltpu.SemaphoreType.DMA((2, parts * (n - 1)))] * 2


def line_kernel(n, parts, products, extras, outs, gathers, finish, *refs):
    refs = list(refs)
    take = lambda count: [refs.pop(0) for _ in range(count)]
    lefts, rights, more, results = take(products), take(products), take(extras), take(outs)
    gathered = take(1)[0] if gathers else None
    me = lax.axis_index("tensor")
    if products:
        totals, run_right, run_left, sent, got = take(5)
        sums = SumScatter(n, me, parts, lefts, rights, totals, (run_right, run_left), sent, got)
    if gathers:
        gather = RowGather(n, me, parts, gathered, *take(2))
    rows = totals.shape[1] if products else gathered.shape[0] // n
    part_rows = rows // parts

    def finish_part(part):
        def body(block):
            at = pl.multiple_of(part * part_rows + block, BLOCK)
            total = totals[me, pl.ds(at, BLOCK), :] if products else None
            sent_rows = finish(at, total, more, results)
            if gathers:
                gathered[pl.ds(pl.multiple_of(me * rows + at, BLOCK), BLOCK), :] = sent_rows

        blocks_of(part_rows, body)

    greet(n, me)
    for result in results:
        if result.shape[0] == 8:
            result[...] = jnp.zeros_like(result)
    if products:
        for hop in range(n - 1):
            sums.products(hop)
            sums.open(0, hop)
        for part in range(1, parts):
            for hop in range(n - 1):
                sums.open(part, hop)
        sums.product(me)
    for part in range(parts):
        for hop in range(n - 1):
            if products:
                sums.pass_on(part, hop)
            if gathers and part > 0:
                gather.step(part - 1, hop)
        if products:
            sums.last(part)
        finish_part(part)
        if gathers:
            gather.start(part)
    if gathers:
        for hop in range(n - 1):
            gather.step(parts - 1, hop)
        gather.drain()
    if products:
        sums.drain()


def line_exchange(name, collective_id, pairs, extras, outs, rows, width, finish, gathers, parts):
    n = lax.axis_size("tensor")
    scratch = scatter_scratch(n, parts, rows, width) if pairs else []
    if gathers:
        scratch = scratch + gather_scratch(n, parts)
        outs = outs + [jax.ShapeDtypeStruct((n * rows, width), jnp.bfloat16)]
    operands = [pair[0] for pair in pairs] + [pair[1] for pair in pairs] + list(extras)
    specs = whole_part(len(operands))
    for k, (left, right, which) in enumerate(pairs):
        specs[len(pairs) + k] = pl.BlockSpec(
            (None, *right.shape[1:]), lambda i, which=which: (which, 0, 0), pipeline_mode=pl.Buffered(1)
        )
    depth = sum(pair[0].shape[1] for pair in pairs)
    return pl.pallas_call(
        functools.partial(
            line_kernel, n, parts, len(pairs), len(extras), len(outs) - gathers, gathers, finish
        ),
        grid=(1,),
        out_shape=outs,
        in_specs=specs,
        out_specs=whole_part(len(outs)),
        scratch_shapes=scratch,
        compiler_params=pltpu.CompilerParams(
            collective_id=collective_id, has_side_effects=True, vmem_limit_bytes=60 * 2**20
        ),
        cost_estimate=pl.CostEstimate(
            flops=2 * n * rows * width * max(depth, 1),
            bytes_accessed=200 * 2**20,
            transcendentals=0,
        ),
        name=name,
    )(*operands)


def everywhere_kernel(sizes, field, result, came, sent, got):
    places = [lax.axis_index(name) for name in sizes]
    partners = []
    for name, place in zip(sizes, places):
        stride = 1
        while stride < sizes[name]:
            other = place + stride - 2 * stride * (place // stride % 2)
            partners.append({name: other})
            stride = 2 * stride
    barrier = pltpu.get_barrier_semaphore()
    for partner in partners:
        pl.semaphore_signal(barrier, inc=1, device_id=partner, device_id_type=MESH)
    pl.semaphore_wait(barrier, len(partners))
    result[...] = field[...]
    for k, partner in enumerate(partners):
        came[2 * k] = result[...]
        copy = pltpu.make_async_remote_copy(
            src_ref=came.at[2 * k],
            dst_ref=came.at[2 * k + 1],
            send_sem=sent.at[k],
            recv_sem=got.at[k],
            device_id=partner,
            device_id_type=MESH,
        )
        copy.start()
        copy.wait()
        result[...] = result[...] + came[2 * k + 1]


def sum_everywhere(field):
    sizes = {name: lax.axis_size(name) for name in ("dp", "tensor")}
    steps = sum(size.bit_length() - 1 for size in sizes.values())
    return pl.pallas_call(
        functools.partial(everywhere_kernel, sizes),
        out_shape=jax.ShapeDtypeStruct(field.shape, jnp.float32),
        in_specs=whole_part(1),
        out_specs=pl.BlockSpec(memory_space=pltpu.VMEM),
        scratch_shapes=[
            pltpu.VMEM((2 * steps, *field.shape), jnp.float32),
            pltpu.SemaphoreType.DMA((steps,)),
            pltpu.SemaphoreType.DMA((steps,)),
        ],
        compiler_params=pltpu.CompilerParams(collective_id=7, has_side_effects=True),
        name="gain_sum",
    )(field)


def inverse_scale(field):
    return lax.rsqrt(jnp.mean(field * field, axis=-1, keepdims=True) + EPS_NORM)


def first_norm(at, total, more, results):
    layer_in, gains = more
    field = layer_in[pl.ds(at, BLOCK), :].astype(jnp.float32)
    return (field * inverse_scale(field) * gains[0:1, :]).astype(jnp.bfloat16)


def second_norm(at, total, more, results):
    layer_in, gains = more
    field = layer_in[pl.ds(at, BLOCK), :].astype(jnp.float32) + total
    results[0][pl.ds(at, BLOCK), :] = field
    return (field * inverse_scale(field) * gains[1:2, :]).astype(jnp.bfloat16)


def norm_back(field, gradient, gain_row, gain_out):
    inv_scale = inverse_scale(field)
    normed = field * inv_scale
    scaled = gradient * gain_row
    back = inv_scale * (scaled - normed * jnp.mean(scaled * normed, axis=-1, keepdims=True))
    product = gradient * normed
    folded = product[0:8]
    for k in range(8, BLOCK, 8):
        folded = folded + product[k : k + 8]
    gain_out[...] = gain_out[...] + folded
    return back


def second_back(at, total, more, results):
    middle, cotangent, gains = more
    rows = pl.ds(at, BLOCK)
    back = norm_back(middle[rows, :], total, gains[1:2, :], results[1])
    back = back + cotangent[rows, :].astype(jnp.float32)
    results[0][rows, :] = back
    return back.astype(jnp.bfloat16)


def first_back(at, total, more, results):
    layer_in, d_middle, gains = more
    rows = pl.ds(at, BLOCK)
    back = norm_back(layer_in[rows, :].astype(jnp.float32), total, gains[0:1, :], results[1])
    results[0][rows, :] = back + d_middle[rows, :]


PAIR = 2 * HEAD_DIM
QUERIES = 256


def turned(field, cos_tile, sine_tile):
    lanes = lax.broadcasted_iota(jnp.int32, field.shape, 1)
    ahead = pltpu.roll(field, PAIR - HEAD_DIM // 2, 1)
    behind = pltpu.roll(field, HEAD_DIM // 2, 1)
    partner = jnp.where(lanes % HEAD_DIM < HEAD_DIM // 2, ahead, behind)
    return field * cos_tile + partner * sine_tile


def one_head(tile, head):
    lanes = lax.broadcasted_iota(jnp.int32, tile.shape, 1)
    return jnp.where(lanes // HEAD_DIM == head, tile, jnp.zeros_like(tile))


def over_lanes(left, right):
    return lax.dot_general(
        left, right, (((1,), (1,)), ((), ())), preferred_element_type=jnp.float32
    )


def masked(scores, starts, first_query):
    keys = lax.broadcasted_iota(jnp.int32, scores.shape, 0)
    queries = first_query + lax.broadcasted_iota(jnp.int32, scores.shape, 1)
    return jnp.where((keys >= starts) & (keys <= queries), scores, MASKED)


def attention_forward_kernel(
    n, first_in, weights, cos_ref, sine_ref, starts_ref, own_rows,
    queries, key_rows, values, attended, log_totals, gathered, turned_values, sent, got
):
    me = lax.axis_index("tensor")
    rows = own_rows.shape[0]
    length, width = queries.shape
    greet(n, me)
    gather = RowGather(n, me, 1, gathered, sent, got)
    blocks_of(
        rows,
        lambda at: gathered.__setitem__(
            (pl.ds(pl.multiple_of(me * rows + at, BLOCK), BLOCK), slice(None)),
            own_rows[pl.ds(at, BLOCK), :],
        ),
    )
    gather.start(0)

    @pl.loop(0, length // QUERIES)
    def _(block):
        at = pl.ds(pl.multiple_of(block * QUERIES, QUERIES), QUERIES)
        source = first_in[at, :]
        cos_tile, sine_tile = cos_ref[at, :], sine_ref[at, :]
        for which, target in enumerate((queries, key_rows, values)):
            field = jnp.dot(source, weights[which], preferred_element_type=jnp.float32)
            for pair in range(width // PAIR):
                tile = field[:, pair * PAIR : (pair + 1) * PAIR]
                if which < 2:
                    tile = turned(tile, cos_tile, sine_tile)
                if which == 0:
                    tile = tile.astype(jnp.bfloat16) * HEAD_DIM ** (-0.5)
                target[at, pair * PAIR : (pair + 1) * PAIR] = tile.astype(jnp.bfloat16)

    @pl.loop(0, width // PAIR)
    def _(pair):
        lanes = pl.ds(pl.multiple_of(pair * PAIR, PAIR), PAIR)
        turned_values[...] = values[:, lanes].astype(jnp.float32).T.astype(jnp.bfloat16)
        for block in range(length // QUERIES):
            at = pl.ds(block * QUERIES, QUERIES)
            reach = (block + 1) * QUERIES
            starts = starts_ref[:, at]
            both = []
            for head in range(2):
                query = one_head(queries[at, lanes], head)
                scores = masked(
                    over_lanes(key_rows[0:reach, lanes], query), starts, block * QUERIES
                )
                peak = jnp.max(scores, axis=0, keepdims=True)
                raised = jnp.exp(scores - peak)
                total = jnp.sum(raised, axis=0, keepdims=True)
                result = jnp.dot(
                    turned_values[head * HEAD_DIM : (head + 1) * HEAD_DIM, 0:reach],
                    raised.astype(jnp.bfloat16),
                    preferred_element_type=jnp.float32,
                )
                both.append(result / total)
                log_totals[2 * pair + head, :, at] = peak + jnp.log(total)
            attended[at, lanes] = jnp.concatenate(both, axis=0).T.astype(jnp.bfloat16)

    for hop in range(n - 1):
        gather.step(0, hop)
    gather.drain()


def attention_forward(first_in, weights, cos_tile, sine_tile, starts, own_rows):
    n = lax.axis_size("tensor")
    length, depth = first_in.shape
    width = weights.shape[2]
    narrow = jax.ShapeDtypeStruct((length, width), jnp.bfloat16)
    outs = [
        narrow,
        narrow,
        narrow,
        narrow,
        jax.ShapeDtypeStruct((width // HEAD_DIM, 1, length), jnp.float32),
        jax.ShapeDtypeStruct((length, depth), jnp.bfloat16),
    ]
    specs = whole_part(6)
    specs[1] = pl.BlockSpec((3, depth, width), lambda i: (0, 0, 0), pipeline_mode=pl.Buffered(1))
    return pl.pallas_call(
        functools.partial(attention_forward_kernel, n),
        grid=(1,),
        out_shape=outs,
        in_specs=specs,
        out_specs=whole_part(len(outs)),
        scratch_shapes=[pltpu.VMEM((PAIR, length), jnp.bfloat16)] + gather_scratch(n, 1),
        compiler_params=pltpu.CompilerParams(
            collective_id=5, has_side_effects=True, vmem_limit_bytes=60 * 2**20
        ),
        cost_estimate=pl.CostEstimate(
            flops=6 * length * depth * width, bytes_accessed=200 * 2**20, transcendentals=0
        ),
        name="attention_forward",
    )(first_in, weights, cos_tile, sine_tile, starts, own_rows)


def attention_back_kernel(
    n, d_attn, out_weight, queries, key_rows, values, attended, log_totals, cos_ref, sine_ref,
    starts_ref, middle, hidden, down_weight, query_raw, key_raw, value_raw, layer_out,
    d_attended, turned_keys, key_sum, value_sum, held, held_sems,
    totals, run_right, run_left, sent, got
):
    me = lax.axis_index("tensor")
    length, width = queries.shape

    def fetch(block):
        return pltpu.make_async_copy(
            d_attn.at[pl.ds(block * QUERIES, QUERIES), :], held.at[block % 2], held_sems.at[block % 2]
        )

    fetch(0).start()
    greet(n, me)
    sums = SumScatter(n, me, 1, [hidden], [down_weight], totals, (run_right, run_left), sent, got)
    for hop in range(n - 1):
        sums.products(hop)
        sums.open(0, hop)
    sums.product(me)

    for block in range(length // QUERIES):
        fetch(block).wait()
        if (block + 1) * QUERIES < length:
            fetch(block + 1).start()
        d_attended[block * QUERIES : (block + 1) * QUERIES, :] = jnp.dot(
            held[block % 2], out_weight[0], preferred_element_type=jnp.float32
        ).astype(jnp.bfloat16)

    def back_pair(pair):
        lanes = pl.ds(pl.multiple_of(pair * PAIR, PAIR), PAIR)
        turned_keys[...] = key_rows[:, lanes].astype(jnp.float32).T.astype(jnp.bfloat16)
        key_sum[...] = jnp.zeros_like(key_sum)
        value_sum[...] = jnp.zeros_like(value_sum)
        for block in range(length // QUERIES):
            at = pl.ds(block * QUERIES, QUERIES)
            reach = (block + 1) * QUERIES
            starts = starts_ref[:, at]
            grads = d_attended[at, lanes]
            shares = (grads.astype(jnp.float32) * attended[at, lanes].astype(jnp.float32)).T
            both = []
            for head in range(2):
                heads = slice(head * HEAD_DIM, (head + 1) * HEAD_DIM)
                query = one_head(queries[at, lanes], head)
                grad = one_head(grads, head)
                share = jnp.sum(shares[heads], axis=0, keepdims=True)
                scores = masked(
                    over_lanes(key_rows[0:reach, lanes], query), starts, block * QUERIES
                )
                probs = jnp.exp(scores - log_totals[2 * pair + head, :, at])
                prob_grad = over_lanes(values[0:reach, lanes], grad)
                score_grad = (probs * (prob_grad - share)).astype(jnp.bfloat16)
                value_sum[0:reach, :] = value_sum[0:reach, :] + jnp.dot(
                    probs.astype(jnp.bfloat16), grad, preferred_element_type=jnp.float32
                )
                key_sum[0:reach, :] = key_sum[0:reach, :] + jnp.dot(
                    score_grad, query, preferred_element_type=jnp.float32
                )
                both.append(
                    jnp.dot(
                        turned_keys[heads, 0:reach], score_grad, preferred_element_type=jnp.float32
                    )
                )
            query_grad = jnp.concatenate(both, axis=0).T * HEAD_DIM ** (-0.5)
            query_raw[at, lanes] = turned(query_grad, cos_ref[at, :], -sine_ref[at, :]).astype(
                jnp.bfloat16
            )
        key_raw[:, lanes] = turned(key_sum[...], cos_ref[...], -sine_ref[...]).astype(jnp.bfloat16)
        value_raw[:, lanes] = value_sum[...].astype(jnp.bfloat16)

    pairs = width // PAIR
    pl.loop(0, pairs // 2)(back_pair)
    sums.pass_on(0, 0)
    pl.loop(pairs // 2, pairs)(back_pair)
    for hop in range(1, n - 1):
        sums.pass_on(0, hop)
    sums.last(0)

    def body(at):
        rows = pl.ds(at, BLOCK)
        layer_out[rows, :] = (middle[rows, :] + totals[me, rows, :]).astype(jnp.bfloat16)

    blocks_of(middle.shape[0], body)
    sums.drain()


def attention_back(
    d_attn, attn_low, queries, key_rows, values, attended, log_totals, cos_tile, sine_tile, starts,
    middle, hidden, mlp_low
):
    n = lax.axis_size("tensor")
    length, depth = d_attn.shape
    width, units = queries.shape[1], hidden.shape[1]
    rows = middle.shape[0]
    narrow = jax.ShapeDtypeStruct((length, width), jnp.bfloat16)
    specs = whole_part(13)
    once = pl.Buffered(1)
    specs[0] = pl.BlockSpec(memory_space=pl.ANY)
    specs[1] = pl.BlockSpec((1, depth, width), lambda i: (3, 0, 0), pipeline_mode=once)
    specs[12] = pl.BlockSpec((None, depth, units), lambda i: (2, 0, 0), pipeline_mode=once)
    return pl.pallas_call(
        functools.partial(attention_back_kernel, n),
        grid=(1,),
        out_shape=[narrow, narrow, narrow, jax.ShapeDtypeStruct((rows, depth), jnp.bfloat16)],
        in_specs=specs,
        out_specs=whole_part(4),
        scratch_shapes=[
            pltpu.VMEM((length, width), jnp.bfloat16),
            pltpu.VMEM((PAIR, length), jnp.bfloat16),
            pltpu.VMEM((length, PAIR), jnp.float32),
            pltpu.VMEM((length, PAIR), jnp.float32),
            pltpu.VMEM((2, QUERIES, depth), jnp.bfloat16),
            pltpu.SemaphoreType.DMA((2,)),
        ]
        + scatter_scratch(n, 1, rows, depth, jnp.bfloat16),
        compiler_params=pltpu.CompilerParams(
            collective_id=6, has_side_effects=True, vmem_limit_bytes=60 * 2**20
        ),
        cost_estimate=pl.CostEstimate(
            flops=2 * length * depth * (width + units),
            bytes_accessed=200 * 2**20,
            transcendentals=0,
        ),
        name="attention_back",
    )(
        d_attn, attn_low, queries, key_rows, values, attended, log_totals, cos_tile, sine_tile,
        starts, middle, hidden, mlp_low
    )


def turn_into(target, source):
    @pl.loop(0, source.shape[0] // TILE)
    def _(block):
        at = pl.ds(pl.multiple_of(block * TILE, TILE), TILE)
        for k in range(source.shape[1] // TILE):
            columns = slice(k * TILE, (k + 1) * TILE)
            target[columns, at] = source[at, columns].astype(jnp.float32).T.astype(jnp.bfloat16)


def mlp_kernel(second_in, cotangent, weights, hidden, d_gate, d_up, grads, second_turned, cot_turned):
    @pl.when(pl.program_id(0) == 0)
    def _():
        turn_into(second_turned, second_in)
        turn_into(cot_turned, cotangent)

    for block in range(second_in.shape[0] // QUERIES):
        at = slice(block * QUERIES, (block + 1) * QUERIES)
        source = second_in[at, :]
        gate_proj = jnp.dot(source, weights[0], preferred_element_type=jnp.float32)
        up_proj = jnp.dot(source, weights[1], preferred_element_type=jnp.float32)
        d_hidden = jnp.dot(cotangent[at, :], weights[2], preferred_element_type=jnp.float32)
        sigmoid_gate = jax.nn.sigmoid(gate_proj)
        silu = gate_proj * sigmoid_gate
        hidden[at, :] = (silu * up_proj).astype(jnp.bfloat16)
        slope = sigmoid_gate * (1.0 + gate_proj * (1.0 - sigmoid_gate))
        d_gate[at, :] = (d_hidden * up_proj * slope).astype(jnp.bfloat16)
        d_up[at, :] = (d_hidden * silu).astype(jnp.bfloat16)
    for which, (left, right) in enumerate(
        ((second_turned, d_gate), (second_turned, d_up), (cot_turned, hidden))
    ):

        @pl.loop(0, left.shape[0] // 512)
        def _(block):
            at = pl.ds(pl.multiple_of(block * 512, 512), 512)
            grads[which, at, :] = jnp.dot(
                left[at, :], right[...], preferred_element_type=jnp.float32
            ).astype(jnp.bfloat16)


def mlp_middle(second_in, cotangent, weights):
    length, depth = second_in.shape
    units = weights.shape[2]
    tile = 256
    wide = jax.ShapeDtypeStruct((length, units), jnp.bfloat16)
    column = pl.BlockSpec((length, tile), lambda j: (0, j))
    stacked = pl.BlockSpec((3, depth, tile), lambda j: (0, 0, j))
    return pl.pallas_call(
        mlp_kernel,
        grid=(units // tile,),
        out_shape=[wide, wide, wide, jax.ShapeDtypeStruct((3, depth, units), jnp.bfloat16)],
        in_specs=whole_part(2) + [stacked],
        out_specs=[column, column, column, stacked],
        scratch_shapes=[pltpu.VMEM((depth, length), jnp.bfloat16)] * 2,
        compiler_params=pltpu.CompilerParams(vmem_limit_bytes=60 * 2**20),
        cost_estimate=pl.CostEstimate(
            flops=12 * length * depth * units, bytes_accessed=60 * 2**20, transcendentals=0
        ),
        name="mlp_middle",
    )(second_in, cotangent, weights)


def grads_kernel(first_in, query_raw, key_raw, value_raw, d_attn, attended, grads, turned_rows):
    which = pl.program_id(0)
    pl.when(which == 0)(lambda: turn_into(turned_rows, first_in))
    pl.when(which == 3)(lambda: turn_into(turned_rows, d_attn))
    for k, right in enumerate((query_raw, key_raw, value_raw, attended)):

        @pl.when(which == k)
        def _():
            @pl.loop(0, turned_rows.shape[0] // 512)
            def _(block):
                at = pl.ds(pl.multiple_of(block * 512, 512), 512)
                grads[at, :] = jnp.dot(
                    turned_rows[at, :], right[...], preferred_element_type=jnp.float32
                ).astype(jnp.bfloat16)


def attention_grads(first_in, query_raw, key_raw, value_raw, d_attn, attended):
    length, depth = first_in.shape
    width = attended.shape[1]
    return pl.pallas_call(
        grads_kernel,
        grid=(4,),
        out_shape=jax.ShapeDtypeStruct((4, depth, width), jnp.bfloat16),
        in_specs=whole_part(6),
        out_specs=pl.BlockSpec((None, depth, width), lambda j: (j, 0, 0)),
        scratch_shapes=[pltpu.VMEM((depth, length), jnp.bfloat16)],
        compiler_params=pltpu.CompilerParams(vmem_limit_bytes=60 * 2**20),
        cost_estimate=pl.CostEstimate(
            flops=8 * length * depth * width, bytes_accessed=20 * 2**20, transcendentals=0
        ),
        name="attention_grads",
    )(first_in, query_raw, key_raw, value_raw, d_attn, attended)


def attn_rates():
    return jnp.array([1.0, 1.0, 1.0, 8.0**0.5], jnp.float32).reshape(4, 1, 1) * (0.5 * D ** (-0.5))


def adam_update(weight, gradient, moment_one, moment_two, step_rate):
    first_new = BETA_ONE * moment_one + (1.0 - BETA_ONE) * gradient
    second_new = BETA_TWO * moment_two + (1.0 - BETA_TWO) * gradient * gradient
    fix_one = 1.0 - BETA_ONE**STEP
    fix_two = 1.0 - BETA_TWO**STEP
    weight_new = weight - step_rate * (
        first_new / fix_one / (jnp.sqrt(second_new / fix_two) + EPS_ADAM) + WEIGHT_DECAY * weight
    )
    return (first_new, second_new, weight_new)


def local(
    inputs,
    cotangent,
    doc_lengths,
    norm_gains,
    attn_weight,
    mlp_weight,
    gain_first,
    attn_first,
    mlp_first,
    gain_second,
    attn_second,
    mlp_second,
):
    row_count = inputs.shape[0]
    seq_length = row_count * lax.axis_size("tensor")
    segment, position = doc_layout(doc_lengths[0], seq_length)
    cos_tile, sine_tile = rope_tables(position)
    starts = (jnp.arange(seq_length, dtype=jnp.int32) - position)[None, :]
    width = inputs.shape[1]
    rows_f32 = jax.ShapeDtypeStruct((row_count, width), jnp.float32)
    gain_f32 = jax.ShapeDtypeStruct((8, width), jnp.float32)
    exchange = functools.partial(line_exchange, rows=row_count, width=width)
    (first_in,) = exchange(
        "first_norm", 1, [], [inputs, norm_gains], [], finish=first_norm, gathers=True, parts=1
    )
    attn_low = lax.all_gather(attn_weight.astype(jnp.bfloat16), "dp", axis=1, tiled=True)

    queries, key_rows, values, attended, log_totals, grad_out = attention_forward(
        first_in, attn_low, cos_tile, sine_tile, starts, cotangent
    )
    middle, second_in = exchange(
        "attention_out",
        2,
        [(attended, attn_low, 3)],
        [inputs, norm_gains],
        [rows_f32],
        finish=second_norm,
        gathers=True,
        parts=2,
    )
    mlp_low = lax.all_gather(mlp_weight.astype(jnp.bfloat16), "dp", axis=1, tiled=True)
    hidden, d_gate, d_up, mlp_sums = mlp_middle(second_in, grad_out, mlp_low)

    def to_owner(partial):
        return lax.psum_scatter(partial, "dp", scatter_dimension=1, tiled=True).astype(jnp.float32)

    mlp_grad = to_owner(mlp_sums)
    d_middle, gain_two, d_attn = exchange(
        "mlp_back",
        3,
        [(d_gate, mlp_low, 0), (d_up, mlp_low, 1)],
        [middle, cotangent, norm_gains],
        [rows_f32, gain_f32],
        finish=second_back,
        gathers=True,
        parts=2,
    )
    query_raw, key_raw, value_raw, layer_out = attention_back(
        d_attn,
        attn_low,
        queries,
        key_rows,
        values,
        attended,
        log_totals,
        cos_tile,
        sine_tile,
        starts,
        middle,
        hidden,
        mlp_low,
    )
    attn_sums, mlp_grad = lax.optimization_barrier(
        (attention_grads(first_in, query_raw, key_raw, value_raw, d_attn, attended), mlp_grad)
    )
    attn_grad = to_owner(attn_sums)
    grad_in, gain_one = exchange(
        "input_back",
        4,
        [(query_raw, attn_low, 0), (key_raw, attn_low, 1), (value_raw, attn_low, 2)],
        [inputs, d_middle, norm_gains],
        [rows_f32, gain_f32],
        finish=first_back,
        gathers=False,
        parts=1,
    )
    gain_parts = jnp.stack([jnp.sum(gain_one, axis=0), jnp.sum(gain_two, axis=0)])
    gain_grad = sum_everywhere(gain_parts.reshape(8, -1)).reshape(norm_gains.shape)
    gain_first_new, gain_second_new, gain_new = adam_update(
        norm_gains, gain_grad, gain_first, gain_second, GAIN_RATE
    )
    attn_first_new, attn_second_new, attn_new = adam_update(
        attn_weight, attn_grad, attn_first, attn_second, attn_rates()
    )
    mlp_first_new, mlp_second_new, mlp_new = adam_update(
        mlp_weight, mlp_grad, mlp_first, mlp_second, 0.5 * D ** (-0.5)
    )
    return (
        layer_out,
        grad_in,
        gain_grad,
        attn_grad,
        mlp_grad,
        gain_first_new,
        attn_first_new,
        mlp_first_new,
        gain_second_new,
        attn_second_new,
        mlp_second_new,
        gain_new,
        attn_new,
        mlp_new,
    )


def solution(mesh):
    placed = (
        P(("dp", "tensor"), None),
        P(("dp", "tensor"), None),
        P("dp", None),
        P(),
        P(None, "dp", "tensor"),
        P(None, "dp", "tensor"),
        P(),
        P(None, "dp", "tensor"),
        P(None, "dp", "tensor"),
        P(),
        P(None, "dp", "tensor"),
        P(None, "dp", "tensor"),
    )
    return jax.shard_map(
        local,
        mesh=mesh,
        in_specs=placed,
        out_specs=(
            P(("dp", "tensor"), None),
            P(("dp", "tensor"), None),
            P(),
            P(None, "dp", "tensor"),
            P(None, "dp", "tensor"),
            P(),
            P(None, "dp", "tensor"),
            P(None, "dp", "tensor"),
            P(),
            P(None, "dp", "tensor"),
            P(None, "dp", "tensor"),
            P(),
            P(None, "dp", "tensor"),
            P(None, "dp", "tensor"),
        ),
        check_vma=False,
    )
```

time: 1810 us -> 825 us (0.46)
  waiting for transfers between devices: 1280 us -> 0.11 us
  Pallas kernels: 0 us -> 757 us
  matrix products: 257 us -> 0 us
  other arithmetic: 124 us -> 40.7 us
  local copies, waits for them, and re-layouts: 79.8 us -> 3.7 us
  blocking collectives: 46.3 us -> 0 us
    reduce_scatter x6 -> x2, waiting for transfers between devices: 817 us -> 0.02 us  [to_owner(): lax.psum_scatter(partial, 'dp', scatter_dimension=1, tiled=True)]
    pallas_call x0 -> x9, Pallas kernels: none -> 757 us  [the longest x4 474 us: line_exchange(): pl.pallas_call(functools.partial(line_kernel, n, parts, len(pairs), len(e...]
    all_gather x4 -> x0, waiting for transfers between devices: 278 us -> none  [the longest x1 81.6 us: local(): lax.all_gather(d_middle.astype(jnp.bfloat16), 'tensor', axis=0, tiled=True)]
    dot_general x35 -> x0, matrix products: 257 us -> none  [the longest x7 64 us: dot_transposed(): lax.dot_general(left, right, (((1,), (1,)), ((), ())), preferred_element_...]
    all_gather x1, waiting for transfers between devices: 126 us -> 0.02 us  [local(): lax.all_gather(mlp_weight.astype(jnp.bfloat16), 'dp', axis=1, tiled=True)]
    all_gather x1, waiting for transfers between devices: 53.7 us -> 0.01 us  [local(): lax.all_gather(attn_weight.astype(jnp.bfloat16), 'dp', axis=1, tiled=True)]
    psum x1 -> x0, blocking collectives: 46.3 us -> none  [local(): gain_grad = lax.psum(jnp.stack([gain_one, gain_two]), ('dp', 'tensor'))]
    dynamic_update_slice x4 -> x0, local copies, waits for them, and re-layouts: 43.4 us -> none  [local(): lax.scan(back_block, (empty_sum, empty_sum), (query_blocks, grad_blocks,...]
  transfers between devices with their start and end apart: 12 -> 4, of which waited for: 12 -> 0; matrix products, arithmetic and copies ran while one was open for 10% -> 3% of each run, Pallas kernels for 0% -> 83%
where the time goes in v3:
time: 825 us; the launch traced here: 816 us
  Pallas kernels  757 us (92%)
  other arithmetic  40.7 us (5%)
  between operations  14.5 us (2%)
    pallas_call x4, Pallas kernels, line_exchange(): pl.pallas_call(functools.partial(line_kernel, n, parts, len(pairs), len(e...  474 us
    pallas_call x1, Pallas kernels, attention_back(): pl.pallas_call(functools.partial(attention_back_kernel, n), grid=(1,), ou...  91.4 us
    pallas_call x1, Pallas kernels, mlp_middle(): pl.pallas_call(mlp_kernel, grid=(units // tile,), out_shape=[wide, wide,...  79.7 us
    pallas_call x1, Pallas kernels, attention_forward(): pl.pallas_call(functools.partial(attention_forward_kernel, n), grid=(1,),...  77.6 us
    sub x3, other arithmetic, adam_update(): weight - step_rate * (first_new / fix_one / (jnp.sqrt(second_new / fix_tw...  22.1 us
    pallas_call x1, Pallas kernels, attention_grads(): pl.pallas_call(grads_kernel, grid=(4,), out_shape=jax.ShapeDtypeStruct((4...  20.2 us
  transfers between devices with their start and end apart: 4, of which 0 were waited for; matrix products, arithmetic and copies ran while one was open for 3% of the time, Pallas kernels for 83%

profile of v3, /device:TPU:0, one launch (start us, length us, event | category | flops | bytes accessed | tf_op | source)
XLA Modules:
  0.0 816.4 jit_solution(4060211490602607788)
XLA Ops:
  7.2 2.7 convert_element_type.22
  10.0 4.9 convert_element_type.25
  15.0 0.2 reduce-window.4
  15.2 78.3 %first_norm.1.first_in = bf16[1024,2048]{1,0:T(8,128)(2,1)} custom-call(bf16[256,2048]{1,0:T(8,128)(2,1)} %refs_6_.3, f32[2,2048]{1,0:T(2,128)} %refs_8_.1), custom_call_target="tpu_custom_call" | custom-call | flops 4194304 | bytes 209715200 | tf_op jit(solution)/shard_map/first_norm/pallas_call | solution.py:311
  93.7 1.9 fusion.2
  95.6 1.8 pad_maximum_fusion
  97.4 0.6 subtract_subtract_fusion.starts_ref
  98.0 77.6 %attention_forward.1 = (bf16[1024,512]{1,0:T(8,128)(2,1)}, bf16[1024,512]{1,0:T(8,128)(2,1)}, bf16[1024,512]{1,0:T(8,128)(2,1)}, bf16[1024,512]{1,0:T(8,128)(2,1...) custom-call(bf16[1024,2048]{1,0:T(8,128)(2,1)} %first_norm.1.first_in, ...), custom_call_target="tpu_custom_call" | custom-call | flops 6442450944 | bytes 209715200 | tf_op jit(solution)/shard_map/attention_forward/pallas_call | solution.py:533
  175.7 145.5 %attention_out.1 = (f32[256,2048]{1,0:T(8,128)}, bf16[1024,2048]{1,0:T(8,128)(2,1)}) custom-call(bf16[1024,512]{1,0:T(8,128)(2,1)} %get-tuple-element.37.refs_0_.attended, bf16[4,2048,512]{2,1,0:T(8,128)(2,1)} %all-gather.3.cloned.1.call-done.weights.refs_1_.out_weight.refs_3_.refs_4_.refs_5_, bf16[256,2048]{1,0:T(8,128)(2,1)} %refs_6_.3, f32[2,2048]{1,0:T(2,128)} %refs_8_.1), custom_call_target="tpu_custom_call" | custom-call | flops 2147483648 | bytes 209715200 | tf_op jit(solution)/shard_map/attention_out/pallas_call | solution.py:311
  321.2 79.7 %mlp_middle.1 = (bf16[1024,2048]{1,0:T(8,128)(2,1)}, bf16[1024,2048]{1,0:T(8,128)(2,1)}, bf16[1024,2048]{1,0:T(8,128)(2,1)}, bf16[3,2048,2048]{2,1,0:T(8,128)(2,1)}) custom-call(bf16[1024,2048]{1,0:T(8,128)(2,1)} %get-tuple-element.38.second_in, bf16[1024,2048]{1,0:T(8,128)(2,1)} %get-tuple-element.39.cotangent, ...), custom_call_target="tpu_custom_call" | custom-call | flops 51539607552 | bytes 62914560 | tf_op jit(solution)/shard_map/mlp_middle/pallas_call | solution.py:727
  401.0 162.0 %mlp_back.1 = (f32[256,2048]{1,0:T(8,128)}, f32[8,2048]{1,0:T(8,128)}, bf16[1024,2048]{1,0:T(8,128)(2,1)}) custom-call(bf16[1024,2048]{1,0:T(8,128)(2,1)} %get-tuple-element.40.refs_0_, bf16[1024,2048]{1,0:T(8,128)(2,1)} %get-tuple-element.41.refs_1_, bf16[3,2048,2048]{2,1,0:T(8,128)(2,1)} %all-gather.5.cloned.1.call-done.weights.refs_2_.refs_3_.down_weight, ...), custom_call_target="tpu_custom_call" | custom-call | flops 17179869184 | bytes 209715200 | tf_op jit(solution)/shard_map/mlp_back/pallas_call | solution.py:311
  563.0 91.4 %attention_back.1 = (bf16[1024,512]{1,0:T(8,128)(2,1)}, bf16[1024,512]{1,0:T(8,128)(2,1)}, bf16[1024,512]{1,0:T(8,128)(2,1)}, bf16[256,2048]{1,0:T(8,128)(2,1)}) custom-call(bf16[1024,2048]{1,0:T(8,128)(2,1)} %get-tuple-element.43.d_attn, bf16[4,2048,512]{2,1,0:T(8,128)(2,1)} %all-gather.3.cloned.1.call-done.weights.refs_1_.out_weight.refs_3_.refs_4_.refs_5_, ...), custom_call_target="tpu_custom_call" | custom-call | flops 10737418240 | bytes 209715200 | tf_op jit(solution)/shard_map/attention_back/pallas_call | solution.py:651
  654.4 20.2 %attention_grads.1 = bf16[4,2048,512]{2,1,0:T(8,128)(2,1)} custom-call(bf16[1024,2048]{1,0:T(8,128)(2,1)} %first_norm.1.first_in, bf16[1024,512]{1,0:T(8,128)(2,1)} %get-tuple-element.50.refs_0_.query_raw, bf16[1024,512]{1,0:T(8,128)(2,1)} %get-tuple-element.51.refs_1_.key_raw, bf16[1024,512]{1,0:T(8,128)(2,1)} %get-tuple-element.52.refs_2_.value_raw, ...), custom_call_target="tpu_custom_call" | custom-call | flops 8589934592 | bytes 20971520 | tf_op jit(solution)/shard_map/attention_grads/pallas_call | solution.py:761
  674.6 5.4 convert_element_type.26
  680.1 88.4 %input_back.1 = (f32[256,2048]{1,0:T(8,128)}, f32[8,2048]{1,0:T(8,128)}) custom-call(bf16[1024,512]{1,0:T(8,128)(2,1)} %get-tuple-element.50.refs_0_.query_raw, bf16[1024,512]{1,0:T(8,128)(2,1)} %get-tuple-element.51.refs_1_.key_raw, bf16[1024,512]{1,0:T(8,128)(2,1)} %get-tuple-element.52.refs_2_.value_raw, ...), custom_call_target="tpu_custom_call" | custom-call | flops 6442450944 | bytes 209715200 | tf_op jit(solution)/shard_map/input_back/pallas_call | solution.py:311
  768.5 0.9 reduce_sum.41
  769.4 0.6 reshape.80.field
  770.1 14.2 %gain_sum.1 = f32[8,512]{1,0:T(8,128)} custom-call(f32[8,512]{1,0:T(8,128)} %reshape.80.field), custom_call_target="tpu_custom_call" | custom-call | tf_op jit(solution)/shard_map/gain_sum/pallas_call | solution.py:364
  784.3 0.7 reshape.81
  785.0 0.7 multiply_subtract_fusion.2
  785.7 14.7 %multiply_subtract_fusion = (f32[3,256,2048]{2,1,0:T(8,128)}, f32[3,256,2048]{2,1,0:T(8,128)}, f32[3,256,2048]{2,1,0:T(8,128)}) fusion(f32[3,256,2048]{2,1,0:T(8,128)} %param.18, f32[3,256,2048]{2,1,0:T(8,128)} %convert_element_type.26, f32[3,256,2048]{2,1,0:T(8,128)} %param.24, f32[3,256,2048]{2,1,0:T(8,128)} %param.21), kind=kLoop, calls=%fused_computation.2 | loop fusion | flops 23592960 | bytes 44040192 | tf_op jit(solution)/shard_map/sub | solution.py:785
  800.4 6.7 multiply_subtract_fusion.1
  807.2 1.0 copy.30
  808.1 1.3 copy.31
  (39 shorter events, 0.6 us)
Async XLA Ops:
  7.2 90.9 %all-gather.3.cloned.1.call-start = ((), (), s32[]{:S(2)}) async-start(), calls=%async_computation.2 | async-start | bytes 9437184 | tf_op jit(solution)/shard_map/all_gather | solution.py:817
  9.9 5.1 copy-start.9
  10.0 311.3 %all-gather.5.cloned.1.call-start = ((), (), s32[]{:S(2)}) async-start(), calls=%async_computation.3 | async-start | bytes 28311552 | tf_op jit(solution)/shard_map/all_gather | solution.py:832
  15.0 659.6 %reduce-scatter.3.cloned.1.call-start = ((), (), s32[]{:S(2)}) async-start(), calls=%async_computation.4 | async-start | bytes 28311552 | tf_op jit(solution)/shard_map/reduce_scatter | solution.py:836
  400.9 399.5 %reduce-scatter.5.cloned.1.call-start = ((), (), s32[]{:S(2)}) async-start(), calls=%async_computation.5 | async-start | bytes 9437184 | tf_op jit(solution)/shard_map/reduce_scatter | solution.py:836
  680.1 89.3 %copy-start.5 = (f32[8,2048]{1,0:T(8,128)S(1)}, f32[8,2048]{1,0:T(8,128)}, u32[]{:S(2)}) copy-start(f32[8,2048]{1,0:T(8,128)} %get-tuple-element.56) | copy-start | bytes 196612
  680.1 104.9 %copy-start.3 = (f32[2,2048]{1,0:T(2,128)S(1)}, f32[2,2048]{1,0:T(2,128)}, u32[]{:S(2)}) copy-start(f32[2,2048]{1,0:T(2,128)} %refs_8_.1) | copy-start | bytes 49156
  680.1 104.9 %copy-start.6 = (f32[2,2048]{1,0:T(2,128)S(1)}, f32[2,2048]{1,0:T(2,128)}, u32[]{:S(2)}) copy-start(f32[2,2048]{1,0:T(2,128)} %param.22) | copy-start | bytes 49156
  680.1 104.9 %copy-start.7 = (f32[2,2048]{1,0:T(2,128)S(1)}, f32[2,2048]{1,0:T(2,128)}, u32[]{:S(2)}) copy-start(f32[2,2048]{1,0:T(2,128)} %param.19) | copy-start | bytes 49156
  785.0 15.4 %copy-start.4 = (f32[2,2048]{1,0:T(2,128)}, f32[2,2048]{1,0:T(2,128)S(1)}, u32[]{:S(2)}) copy-start(f32[2,2048]{1,0:T(2,128)S(1)} %reshape.81) | copy-start | bytes 49156
  785.7 14.7 %copy-start = (f32[4,256,512]{2,1,0:T(8,128)S(1)}, f32[4,256,512]{2,1,0:T(8,128)}, u32[]{:S(2)}) copy-start(f32[4,256,512]{2,1,0:T(8,128)} %param.17) | copy-start | bytes 6291460
  785.7 14.7 %copy-start.8 = (f32[4]{0:T(128)S(1)}, f32[4]{0:T(128)}, u32[]{:S(2)}) copy-start(f32[4]{0:T(128)} %constant.12) | copy-start | bytes 52
  800.4 6.8 copy-start.2
  800.4 7.7 copy-start.1
Sparse Core Ops, SparseCore 0:
  10.5 57.0 all-gather.2
  70.1 125.3 all-gather.4
  401.1 156.5 reduce-scatter.2
  680.2 77.5 reduce-scatter.4

commit v4 on v3

--- a/solution.py
+++ b/solution.py
@@ -125,16 +125,16 @@
 
 
 class SumScatter:
-    def __init__(self, n, me, parts, lefts, rights, totals, runs, sent, got):
+    def __init__(self, n, me, parts, lefts, rights, totals, run, sent, got):
         self.n, self.me, self.parts = n, me, parts
-        self.lefts, self.rights, self.totals, self.runs = lefts, rights, totals, runs
+        self.lefts, self.rights, self.totals, self.run = lefts, rights, totals, run
         self.sent, self.got = sent, got
         self.rows = totals.shape[1]
         self.fed = (me > 0, me < n - 1)
 
     def copy(self, way, part, hop):
         slot = part * (self.n - 1) + hop
-        run = self.runs[way].at[slot]
+        run = self.run.at[self.place(way, part, hop)]
         return pltpu.make_async_remote_copy(
             src_ref=run,
             dst_ref=run,
@@ -161,34 +161,42 @@
                 value = term if value is None else value + term
             self.totals[dest, :, columns] = value.astype(self.totals.dtype)
 
-    def dests(self, hop):
-        far, near = self.n - 1 - hop, hop
-        return ((0, far, far > self.me), (1, near, near < self.me))
-
-    def products(self, hop):
-        for way, dest, needed in self.dests(hop):
-            pl.when(needed)(lambda: self.product(dest))
-
-    def open(self, part, hop):
-        for way, dest, needed in self.dests(hop):
-            run, slot = self.runs[way], part * (self.n - 1) + hop
+    def place(self, way, part, hop):
+        return part * (self.n + 1) + (hop, self.n - hop)[way]
+
+    def begin(self):
+        for hop in range(self.n - 1):
+            for way, dest in ((0, self.n - 1 - hop), (1, hop)):
+                needed = (dest > self.me, dest < self.me)[way]
+                run = self.run
+                pl.when(needed)(lambda: self.product(dest))
+
+                @pl.when(needed & jnp.logical_not(self.fed[way]))
+                def _():
+                    for part in range(self.parts):
+                        first = part * (self.rows // self.parts)
+                        slot = self.place(way, part, hop)
+
+                        def body(at):
+                            own = self.totals[dest, pl.ds(first + at, BLOCK), :]
+                            run[slot, pl.ds(at, BLOCK), :] = own.astype(jnp.bfloat16)
+
+                        blocks_of(self.rows // self.parts, body)
+                        self.copy(way, part, hop).start()
+
+        self.product(self.me)
+
+    def arrivals(self, count):
+        for way, behind in ((0, self.me), (1, self.n - 1 - self.me)):
+            hop = count - behind
+            yield way, hop, (self.n - 1 - hop, hop)[way], self.fed[way] & (hop >= 0)
+
+    def pass_on(self, part, count):
+        for way, hop, dest, there in self.arrivals(count):
+            run, slot = self.run, self.place(way, part, hop)
             first = part * (self.rows // self.parts)
 
-            @pl.when(needed & jnp.logical_not(self.fed[way]))
-            def _():
-                def body(at):
-                    own = self.totals[dest, pl.ds(first + at, BLOCK), :]
-                    run[slot, pl.ds(at, BLOCK), :] = own.astype(jnp.bfloat16)
-
-                blocks_of(self.rows // self.parts, body)
-                self.copy(way, part, hop).start()
-
-    def pass_on(self, part, hop):
-        for way, dest, needed in self.dests(hop):
-            run, slot = self.runs[way], part * (self.n - 1) + hop
-            first = part * (self.rows // self.parts)
-
-            @pl.when(needed & self.fed[way])
+            @pl.when(there)
             def _():
                 self.copy(way, part, hop).wait_recv()
 
@@ -202,13 +210,12 @@
 
     def last(self, part):
         first = part * (self.rows // self.parts)
-        for way, hop in ((0, self.n - 1 - self.me), (1, self.me)):
-            run = self.runs[way]
-
-            @pl.when(self.fed[way])
+        for way, hop, dest, there in self.arrivals(self.n - 1):
+            run, slot = self.run, self.place(way, part, hop)
+
+            @pl.when(there)
             def _():
                 self.copy(way, part, hop).wait_recv()
-                slot = part * (self.n - 1) + hop
 
                 def body(at):
                     own = pl.ds(first + at, BLOCK)
@@ -221,16 +228,16 @@
     def drain(self):
         for part in range(self.parts):
             for hop in range(self.n - 1):
-                for way, dest, needed in self.dests(hop):
-                    pl.when(needed)(lambda: self.copy(way, part, hop).wait_send())
-
-
-def scatter_scratch(n, parts, rows, width, kept=jnp.float32):
+                pl.when(self.n - 1 - hop > self.me)(lambda: self.copy(0, part, hop).wait_send())
+                pl.when(hop < self.me)(lambda: self.copy(1, part, hop).wait_send())
+
+
+def scatter_scratch(n, parts, rows, width):
     slots = parts * (n - 1)
+    kept = jnp.float32 if n * rows * width <= 2**21 else jnp.bfloat16
     return [
         pltpu.VMEM((n, rows, width), kept),
-        pltpu.VMEM((slots, rows // parts, width), jnp.bfloat16),
-        pltpu.VMEM((slots, rows // parts, width), jnp.bfloat16),
+        pltpu.VMEM((parts * (n + 1), rows // parts, width), jnp.bfloat16),
         pltpu.SemaphoreType.DMA((2, slots)),
         pltpu.SemaphoreType.DMA((2, slots)),
     ]
@@ -240,15 +247,84 @@
     return [pltpu.SemaphoreType.DMA((2, parts * (n - 1)))] * 2
 
 
-def line_kernel(n, parts, products, extras, outs, gathers, finish, *refs):
+class SideProduct:
+    def __init__(self, source, columns, target, held, weight, staged, sems):
+        self.source, self.columns, self.target = source, columns, target
+        self.held, self.weight, self.staged, self.sems = held, weight, staged, sems
+        self.count = source.shape[0] // QUERIES
+        self.done = 0
+
+    def fetch(self, block):
+        return pltpu.make_async_copy(
+            self.source.at[pl.ds(block * QUERIES, QUERIES), :],
+            self.held.at[block % 2],
+            self.sems.at[block % 2],
+        )
+
+    def store(self, block):
+        return pltpu.make_async_copy(
+            self.staged.at[block % 2],
+            self.target.at[pl.ds(block * QUERIES, QUERIES), :],
+            self.sems.at[2 + block % 2],
+        )
+
+    def fetch_weight(self):
+        return pltpu.make_async_copy(self.columns.at[2], self.weight, self.sems.at[4])
+
+    def open(self, lefts):
+        self.fetch_weight().start()
+        self.fetch(0).start()
+
+    def step(self):
+        block = self.done
+        if block == self.count:
+            return
+        if block == 0:
+            self.fetch_weight().wait()
+        self.fetch(block).wait()
+        if block + 1 < self.count:
+            self.fetch(block + 1).start()
+        if block >= 2:
+            self.store(block - 2).wait()
+
+        @pl.loop(0, self.weight.shape[0] // TILE)
+        def _(tile):
+            columns = pl.ds(pl.multiple_of(tile * TILE, TILE), TILE)
+            self.staged[block % 2, :, columns] = over_lanes(
+                self.held[block % 2], self.weight[columns, :]
+            ).astype(jnp.bfloat16)
+
+        self.store(block).start()
+        self.done = block + 1
+
+    def close(self):
+        while self.done < self.count:
+            self.step()
+        for block in range(max(0, self.count - 2), self.count):
+            self.store(block).wait()
+
+
+def side_scratch(depth, units):
+    return [
+        pltpu.VMEM((2, QUERIES, units), jnp.bfloat16),
+        pltpu.VMEM((depth, units), jnp.bfloat16),
+        pltpu.VMEM((2, QUERIES, depth), jnp.bfloat16),
+        pltpu.SemaphoreType.DMA((5,)),
+    ]
+
+
+def line_kernel(n, parts, products, extras, outs, gathers, side, finish, *refs):
     refs = list(refs)
     take = lambda count: [refs.pop(0) for _ in range(count)]
-    lefts, rights, more, results = take(products), take(products), take(extras), take(outs)
+    lefts, rights, more = take(products), take(products), take(extras)
+    side_in = take(2) if side else None
+    results = take(outs)
     gathered = take(1)[0] if gathers else None
+    filler = SideProduct(*side_in, *take(1), *[refs.pop() for _ in range(4)][::-1]) if side else None
     me = lax.axis_index("tensor")
     if products:
-        totals, run_right, run_left, sent, got = take(5)
-        sums = SumScatter(n, me, parts, lefts, rights, totals, (run_right, run_left), sent, got)
+        totals = refs[0]
+        sums = SumScatter(n, me, parts, lefts, rights, *take(4))
     if gathers:
         gather = RowGather(n, me, parts, gathered, *take(2))
     rows = totals.shape[1] if products else gathered.shape[0] // n
@@ -257,7 +333,7 @@
     def finish_part(part):
         def body(block):
             at = pl.multiple_of(part * part_rows + block, BLOCK)
-            total = totals[me, pl.ds(at, BLOCK), :] if products else None
+            total = totals[me, pl.ds(at, BLOCK), :].astype(jnp.float32) if products else None
             sent_rows = finish(at, total, more, results)
             if gathers:
                 gathered[pl.ds(pl.multiple_of(me * rows + at, BLOCK), BLOCK), :] = sent_rows
@@ -269,40 +345,51 @@
         if result.shape[0] == 8:
             result[...] = jnp.zeros_like(result)
     if products:
-        for hop in range(n - 1):
-            sums.products(hop)
-            sums.open(0, hop)
-        for part in range(1, parts):
-            for hop in range(n - 1):
-                sums.open(part, hop)
-        sums.product(me)
+        sums.begin()
+    if filler:
+        filler.open(lefts)
     for part in range(parts):
         for hop in range(n - 1):
-            if products:
-                sums.pass_on(part, hop)
+            if filler:
+                filler.step()
+            if products and hop < n - 2:
+                sums.pass_on(part, hop + 1)
+            if products and hop == n - 2:
+                sums.last(part)
             if gathers and part > 0:
                 gather.step(part - 1, hop)
-        if products:
-            sums.last(part)
         finish_part(part)
         if gathers:
             gather.start(part)
     if gathers:
         for hop in range(n - 1):
+            if filler:
+                filler.step()
             gather.step(parts - 1, hop)
         gather.drain()
+    if filler:
+        filler.close()
     if products:
         sums.drain()
 
 
-def line_exchange(name, collective_id, pairs, extras, outs, rows, width, finish, gathers, parts):
+def line_exchange(
+    name, collective_id, pairs, extras, outs, rows, width, finish, gathers, parts, side=()
+):
     n = lax.axis_size("tensor")
     scratch = scatter_scratch(n, parts, rows, width) if pairs else []
     if gathers:
         scratch = scratch + gather_scratch(n, parts)
         outs = outs + [jax.ShapeDtypeStruct((n * rows, width), jnp.bfloat16)]
     operands = [pair[0] for pair in pairs] + [pair[1] for pair in pairs] + list(extras)
-    specs = whole_part(len(operands))
+    specs = whole_part(len(operands)) + [pl.BlockSpec(memory_space=pl.ANY)] * len(side)
+    own_outs = len(outs) - gathers
+    out_specs = whole_part(len(outs))
+    operands = operands + list(side)
+    if side:
+        outs = outs + [jax.ShapeDtypeStruct((side[0].shape[0], width), jnp.bfloat16)]
+        out_specs = out_specs + [pl.BlockSpec(memory_space=pl.ANY)]
+        scratch = scratch + side_scratch(width, side[0].shape[1])
     for k, (left, right, which) in enumerate(pairs):
         specs[len(pairs) + k] = pl.BlockSpec(
             (None, *right.shape[1:]), lambda i, which=which: (which, 0, 0), pipeline_mode=pl.Buffered(1)
@@ -310,12 +397,12 @@
     depth = sum(pair[0].shape[1] for pair in pairs)
     return pl.pallas_call(
         functools.partial(
-            line_kernel, n, parts, len(pairs), len(extras), len(outs) - gathers, gathers, finish
+            line_kernel, n, parts, len(pairs), len(extras), own_outs, gathers, len(side) > 0, finish
         ),
         grid=(1,),
         out_shape=outs,
         in_specs=specs,
-        out_specs=whole_part(len(outs)),
+        out_specs=out_specs,
         scratch_shapes=scratch,
         compiler_params=pltpu.CompilerParams(
             collective_id=collective_id, has_side_effects=True, vmem_limit_bytes=60 * 2**20
@@ -452,22 +539,10 @@
 
 
 def attention_forward_kernel(
-    n, first_in, weights, cos_ref, sine_ref, starts_ref, own_rows,
-    queries, key_rows, values, attended, log_totals, gathered, turned_values, sent, got
+    first_in, weights, cos_ref, sine_ref, starts_ref,
+    queries, key_rows, values, attended, log_totals, turned_values
 ):
-    me = lax.axis_index("tensor")
-    rows = own_rows.shape[0]
     length, width = queries.shape
-    greet(n, me)
-    gather = RowGather(n, me, 1, gathered, sent, got)
-    blocks_of(
-        rows,
-        lambda at: gathered.__setitem__(
-            (pl.ds(pl.multiple_of(me * rows + at, BLOCK), BLOCK), slice(None)),
-            own_rows[pl.ds(at, BLOCK), :],
-        ),
-    )
-    gather.start(0)
 
     @pl.loop(0, length // QUERIES)
     def _(block):
@@ -510,13 +585,8 @@
                 log_totals[2 * pair + head, :, at] = peak + jnp.log(total)
             attended[at, lanes] = jnp.concatenate(both, axis=0).T.astype(jnp.bfloat16)
 
-    for hop in range(n - 1):
-        gather.step(0, hop)
-    gather.drain()
-
-
-def attention_forward(first_in, weights, cos_tile, sine_tile, starts, own_rows):
-    n = lax.axis_size("tensor")
+
+def attention_forward(first_in, weights, cos_tile, sine_tile, starts):
     length, depth = first_in.shape
     width = weights.shape[2]
     narrow = jax.ShapeDtypeStruct((length, width), jnp.bfloat16)
@@ -526,34 +596,29 @@
         narrow,
         narrow,
         jax.ShapeDtypeStruct((width // HEAD_DIM, 1, length), jnp.float32),
-        jax.ShapeDtypeStruct((length, depth), jnp.bfloat16),
     ]
-    specs = whole_part(6)
+    specs = whole_part(5)
     specs[1] = pl.BlockSpec((3, depth, width), lambda i: (0, 0, 0), pipeline_mode=pl.Buffered(1))
     return pl.pallas_call(
-        functools.partial(attention_forward_kernel, n),
+        attention_forward_kernel,
         grid=(1,),
         out_shape=outs,
         in_specs=specs,
         out_specs=whole_part(len(outs)),
-        scratch_shapes=[pltpu.VMEM((PAIR, length), jnp.bfloat16)] + gather_scratch(n, 1),
-        compiler_params=pltpu.CompilerParams(
-            collective_id=5, has_side_effects=True, vmem_limit_bytes=60 * 2**20
-        ),
+        scratch_shapes=[pltpu.VMEM((PAIR, length), jnp.bfloat16)],
+        compiler_params=pltpu.CompilerParams(vmem_limit_bytes=60 * 2**20),
         cost_estimate=pl.CostEstimate(
-            flops=6 * length * depth * width, bytes_accessed=200 * 2**20, transcendentals=0
+            flops=6 * length * depth * width, bytes_accessed=100 * 2**20, transcendentals=0
         ),
         name="attention_forward",
-    )(first_in, weights, cos_tile, sine_tile, starts, own_rows)
+    )(first_in, weights, cos_tile, sine_tile, starts)
 
 
 def attention_back_kernel(
-    n, d_attn, out_weight, queries, key_rows, values, attended, log_totals, cos_ref, sine_ref,
-    starts_ref, middle, hidden, down_weight, query_raw, key_raw, value_raw, layer_out,
-    d_attended, turned_keys, key_sum, value_sum, held, held_sems,
-    totals, run_right, run_left, sent, got
+    d_attn, out_weight, queries, key_rows, values, attended, log_totals, cos_ref, sine_ref,
+    starts_ref, query_raw, key_raw, value_raw,
+    d_attended, turned_keys, key_sum, value_sum, held, held_sems
 ):
-    me = lax.axis_index("tensor")
     length, width = queries.shape
 
     def fetch(block):
@@ -562,13 +627,6 @@
         )
 
     fetch(0).start()
-    greet(n, me)
-    sums = SumScatter(n, me, 1, [hidden], [down_weight], totals, (run_right, run_left), sent, got)
-    for hop in range(n - 1):
-        sums.products(hop)
-        sums.open(0, hop)
-    sums.product(me)
-
     for block in range(length // QUERIES):
         fetch(block).wait()
         if (block + 1) * QUERIES < length:
@@ -577,7 +635,8 @@
             held[block % 2], out_weight[0], preferred_element_type=jnp.float32
         ).astype(jnp.bfloat16)
 
-    def back_pair(pair):
+    @pl.loop(0, width // PAIR)
+    def _(pair):
         lanes = pl.ds(pl.multiple_of(pair * PAIR, PAIR), PAIR)
         turned_keys[...] = key_rows[:, lanes].astype(jnp.float32).T.astype(jnp.bfloat16)
         key_sum[...] = jnp.zeros_like(key_sum)
@@ -618,42 +677,24 @@
         key_raw[:, lanes] = turned(key_sum[...], cos_ref[...], -sine_ref[...]).astype(jnp.bfloat16)
         value_raw[:, lanes] = value_sum[...].astype(jnp.bfloat16)
 
-    pairs = width // PAIR
-    pl.loop(0, pairs // 2)(back_pair)
-    sums.pass_on(0, 0)
-    pl.loop(pairs // 2, pairs)(back_pair)
-    for hop in range(1, n - 1):
-        sums.pass_on(0, hop)
-    sums.last(0)
-
-    def body(at):
-        rows = pl.ds(at, BLOCK)
-        layer_out[rows, :] = (middle[rows, :] + totals[me, rows, :]).astype(jnp.bfloat16)
-
-    blocks_of(middle.shape[0], body)
-    sums.drain()
-
 
 def attention_back(
-    d_attn, attn_low, queries, key_rows, values, attended, log_totals, cos_tile, sine_tile, starts,
-    middle, hidden, mlp_low
+    d_attn, attn_low, queries, key_rows, values, attended, log_totals, cos_tile, sine_tile, starts
 ):
-    n = lax.axis_size("tensor")
     length, depth = d_attn.shape
-    width, units = queries.shape[1], hidden.shape[1]
-    rows = middle.shape[0]
+    width = queries.shape[1]
     narrow = jax.ShapeDtypeStruct((length, width), jnp.bfloat16)
-    specs = whole_part(13)
-    once = pl.Buffered(1)
+    specs = whole_part(10)
     specs[0] = pl.BlockSpec(memory_space=pl.ANY)
-    specs[1] = pl.BlockSpec((1, depth, width), lambda i: (3, 0, 0), pipeline_mode=once)
-    specs[12] = pl.BlockSpec((None, depth, units), lambda i: (2, 0, 0), pipeline_mode=once)
+    specs[1] = pl.BlockSpec(
+        (1, depth, width), lambda i: (3, 0, 0), pipeline_mode=pl.Buffered(1)
+    )
     return pl.pallas_call(
-        functools.partial(attention_back_kernel, n),
+        attention_back_kernel,
         grid=(1,),
-        out_shape=[narrow, narrow, narrow, jax.ShapeDtypeStruct((rows, depth), jnp.bfloat16)],
+        out_shape=[narrow, narrow, narrow],
         in_specs=specs,
-        out_specs=whole_part(4),
+        out_specs=whole_part(3),
         scratch_shapes=[
             pltpu.VMEM((length, width), jnp.bfloat16),
             pltpu.VMEM((PAIR, length), jnp.bfloat16),
@@ -661,20 +702,15 @@
             pltpu.VMEM((length, PAIR), jnp.float32),
             pltpu.VMEM((2, QUERIES, depth), jnp.bfloat16),
             pltpu.SemaphoreType.DMA((2,)),
-        ]
-        + scatter_scratch(n, 1, rows, depth, jnp.bfloat16),
-        compiler_params=pltpu.CompilerParams(
-            collective_id=6, has_side_effects=True, vmem_limit_bytes=60 * 2**20
-        ),
+        ],
+        compiler_params=pltpu.CompilerParams(vmem_limit_bytes=60 * 2**20),
         cost_estimate=pl.CostEstimate(
-            flops=2 * length * depth * (width + units),
-            bytes_accessed=200 * 2**20,
-            transcendentals=0,
+            flops=2 * length * depth * width, bytes_accessed=120 * 2**20, transcendentals=0
         ),
         name="attention_back",
     )(
         d_attn, attn_low, queries, key_rows, values, attended, log_totals, cos_tile, sine_tile,
-        starts, middle, hidden, mlp_low
+        starts
     )
 
 
@@ -816,8 +852,9 @@
     )
     attn_low = lax.all_gather(attn_weight.astype(jnp.bfloat16), "dp", axis=1, tiled=True)
 
-    queries, key_rows, values, attended, log_totals, grad_out = attention_forward(
-        first_in, attn_low, cos_tile, sine_tile, starts, cotangent
+    grad_out = lax.all_gather(cotangent, "tensor", axis=0, tiled=True)
+    queries, key_rows, values, attended, log_totals = attention_forward(
+        first_in, attn_low, cos_tile, sine_tile, starts
     )
     middle, second_in = exchange(
         "attention_out",
@@ -832,11 +869,8 @@
     mlp_low = lax.all_gather(mlp_weight.astype(jnp.bfloat16), "dp", axis=1, tiled=True)
     hidden, d_gate, d_up, mlp_sums = mlp_middle(second_in, grad_out, mlp_low)
 
-    def to_owner(partial):
-        return lax.psum_scatter(partial, "dp", scatter_dimension=1, tiled=True).astype(jnp.float32)
-
-    mlp_grad = to_owner(mlp_sums)
-    d_middle, gain_two, d_attn = exchange(
+    mlp_owned = lax.psum_scatter(mlp_sums, "dp", scatter_dimension=1, tiled=True)
+    d_middle, gain_two, d_attn, out_sums = exchange(
         "mlp_back",
         3,
         [(d_gate, mlp_low, 0), (d_up, mlp_low, 1)],
@@ -845,26 +879,20 @@
         finish=second_back,
         gathers=True,
         parts=2,
-    )
-    query_raw, key_raw, value_raw, layer_out = attention_back(
-        d_attn,
-        attn_low,
-        queries,
-        key_rows,
-        values,
-        attended,
-        log_totals,
-        cos_tile,
-        sine_tile,
-        starts,
-        middle,
-        hidden,
-        mlp_low,
-    )
-    attn_sums, mlp_grad = lax.optimization_barrier(
-        (attention_grads(first_in, query_raw, key_raw, value_raw, d_attn, attended), mlp_grad)
-    )
-    attn_grad = to_owner(attn_sums)
+        side=(hidden, mlp_low),
+    )
+    out_sums, mlp_owned = lax.optimization_barrier((out_sums, mlp_owned))
+    out_rows = lax.psum_scatter(out_sums, "tensor", scatter_dimension=0, tiled=True)
+    query_raw, key_raw, value_raw = attention_back(
+        d_attn, attn_low, queries, key_rows, values, attended, log_totals, cos_tile, sine_tile,
+        starts
+    )
+    attn_sums, out_rows = lax.optimization_barrier(
+        (attention_grads(first_in, query_raw, key_raw, value_raw, d_attn, attended), out_rows)
+    )
+    attn_owned = lax.psum_scatter(attn_sums, "dp", scatter_dimension=1, tiled=True)
+    layer_out = (middle + out_rows.astype(jnp.float32)).astype(jnp.bfloat16)
+    mlp_grad, attn_grad = mlp_owned.astype(jnp.float32), attn_owned.astype(jnp.float32)
     grad_in, gain_one = exchange(
         "input_back",
         4,

time: 825 us -> 768 us (0.931)
  Pallas kernels: 757 us -> 664 us
  waiting for transfers between devices: 0.11 us -> 40 us
    pallas_call x2, Pallas kernels: 169 us -> 55.6 us  [the longest x1 29.1 us: attention_forward(): pl.pallas_call(attention_forward_kernel, grid=(1,), out_shape=outs, in_sp...]
    reduce_scatter x2 -> x3, waiting for transfers between devices: 0.02 us -> 39.2 us  [the longest x1 31.8 us: local(): lax.psum_scatter(out_sums, 'tensor', scatter_dimension=0, tiled=True)]
    pallas_call x4, Pallas kernels: 474 us -> 492 us  [line_exchange(): pl.pallas_call(functools.partial(line_kernel, n, parts, len(pairs), len(e...]
  transfers between devices with their start and end apart: 4 -> 6, of which waited for: 0 -> 2; matrix products, arithmetic and copies ran while one was open for 3% -> 4% of each run, Pallas kernels for 83% -> 77%
where the time goes in v4:
time: 768 us; the launch traced here: 760 us
  Pallas kernels  664 us (86%)
  waiting for transfers between devices  40 us (5%)
  other arithmetic  37.1 us (5%)
  between operations  14.8 us (2%)
    pallas_call x4, Pallas kernels, line_exchange(): pl.pallas_call(functools.partial(line_kernel, n, parts, len(pairs), len(e...  492 us
    pallas_call x1, Pallas kernels, mlp_middle(): pl.pallas_call(mlp_kernel, grid=(units // tile,), out_shape=[wide, wide,...  79.7 us
    reduce_scatter x1, waiting for transfers between devices, local(): lax.psum_scatter(out_sums, 'tensor', scatter_dimension=0, tiled=True)  31.8 us
    pallas_call x1, Pallas kernels, attention_forward(): pl.pallas_call(attention_forward_kernel, grid=(1,), out_shape=outs, in_sp...  29.1 us
    pallas_call x1, Pallas kernels, attention_back(): pl.pallas_call(attention_back_kernel, grid=(1,), out_shape=[narrow, narro...  26.5 us
    sub x3, other arithmetic, adam_update(): weight - step_rate * (first_new / fix_one / (jnp.sqrt(second_new / fix_tw...  22.6 us
    pallas_call x1, Pallas kernels, attention_grads(): pl.pallas_call(grads_kernel, grid=(4,), out_shape=jax.ShapeDtypeStruct((4...  20.3 us
    pallas_call x1, Pallas kernels, sum_everywhere(): pl.pallas_call(functools.partial(everywhere_kernel, sizes), out_shape=jax...  16.6 us
  transfers between devices with their start and end apart: 6, of which 2 were waited for; matrix products, arithmetic and copies ran while one was open for 4% of the time, Pallas kernels for 77%

profile of v4, /device:TPU:0, one launch (start us, length us, event | category | flops | bytes accessed | tf_op | source)
XLA Modules:
  0.0 760.2 jit_solution(12933376724462107404)
XLA Ops:
  7.2 2.7 convert_element_type.28
  10.0 0.7 all-gather.6.cloned.1.call-update
  10.8 4.9 convert_element_type.31
  16.0 123.0 %first_norm.1.first_in = bf16[1024,2048]{1,0:T(8,128)(2,1)} custom-call(bf16[256,2048]{1,0:T(8,128)(2,1)} %refs_6_.3, f32[2,2048]{1,0:T(2,128)} %refs_8_.1), custom_call_target="tpu_custom_call" | custom-call | flops 4194304 | bytes 209715200 | tf_op jit(solution)/shard_map/first_norm/pallas_call | solution.py:398
  139.2 1.9 fusion.2
  141.1 1.9 pad_maximum_fusion
  143.6 29.1 %attention_forward.1 = (bf16[1024,512]{1,0:T(8,128)(2,1)}, bf16[1024,512]{1,0:T(8,128)(2,1)}, bf16[1024,512]{1,0:T(8,128)(2,1)}, bf16[1024,512]{1,0:T(8,128)(2,1)}, f32[8,1,1024]{2,1,0:T(1,128)}) custom-call(bf16[1024,2048]{1,0:T(8,128)(2,1)} %first_norm.1.first_in, ...), custom_call_target="tpu_custom_call" | custom-call | flops 6442450944 | bytes 104857600 | tf_op jit(solution)/shard_map/attention_forward/pallas_call | solution.py:602
  172.7 132.7 %attention_out.1 = (f32[256,2048]{1,0:T(8,128)}, bf16[1024,2048]{1,0:T(8,128)(2,1)}) custom-call(bf16[1024,512]{1,0:T(8,128)(2,1)} %get-tuple-element.38.refs_0_.attended, bf16[4,2048,512]{2,1,0:T(8,128)(2,1)} %all-gather.4.cloned.1.call-done.weights.refs_1_.out_weight.refs_3_.refs_4_.refs_5_, bf16[256,2048]{1,0:T(8,128)(2,1)} %refs_6_.3, f32[2,2048]{1,0:T(2,128)} %refs_8_.1), custom_call_target="tpu_custom_call" | custom-call | flops 2147483648 | bytes 209715200 | tf_op jit(solution)/shard_map/attention_out/pallas_call | solution.py:398
  305.4 79.7 %mlp_middle.1 = (bf16[1024,2048]{1,0:T(8,128)(2,1)}, bf16[1024,2048]{1,0:T(8,128)(2,1)}, bf16[1024,2048]{1,0:T(8,128)(2,1)}, bf16[3,2048,2048]{2,1,0:T(8,128)(2,1)}) custom-call(bf16[1024,2048]{1,0:T(8,128)(2,1)} %get-tuple-element.40.second_in, bf16[1024,2048]{1,0:T(8,128)(2,1)} %all-gather.6.cloned.1.call-done.cotangent, ...), custom_call_target="tpu_custom_call" | custom-call | flops 51539607552 | bytes 62914560 | tf_op jit(solution)/shard_map/mlp_middle/pallas_call | solution.py:763
  385.2 152.1 %mlp_back.1 = (f32[256,2048]{1,0:T(8,128)}, f32[8,2048]{1,0:T(8,128)}, bf16[1024,2048]{1,0:T(8,128)(2,1)}, bf16[1024,2048]{1,0:T(8,128)(2,1)}) custom-call(bf16[1024,2048]{1,0:T(8,128)(2,1)} %get-tuple-element.41.refs_0_, bf16[1024,2048]{1,0:T(8,128)(2,1)} %get-tuple-element.42.refs_1_, ...), custom_call_target="tpu_custom_call" | custom-call | flops 17179869184 | bytes 209715200 | tf_op jit(solution)/shard_map/mlp_back/pallas_call | solution.py:398
  537.4 7.4 reduce-scatter.4.cloned.1.call-done
  545.0 26.5 %attention_back.1 = (bf16[1024,512]{1,0:T(8,128)(2,1)}, bf16[1024,512]{1,0:T(8,128)(2,1)}, bf16[1024,512]{1,0:T(8,128)(2,1)}) custom-call(bf16[1024,2048]{1,0:T(8,128)(2,1)} %get-tuple-element.44.d_attn, bf16[4,2048,512]{2,1,0:T(8,128)(2,1)} %all-gather.4.cloned.1.call-done.weights.refs_1_.out_weight.refs_3_.refs_4_.refs_5_, ...), custom_call_target="tpu_custom_call" | custom-call | flops 2147483648 | bytes 125829120 | tf_op jit(solution)/shard_map/attention_back/pallas_call | solution.py:692
  571.6 20.3 %attention_grads.1 = bf16[4,2048,512]{2,1,0:T(8,128)(2,1)} custom-call(bf16[1024,2048]{1,0:T(8,128)(2,1)} %first_norm.1.first_in, bf16[1024,512]{1,0:T(8,128)(2,1)} %get-tuple-element.49.query_raw.refs_0_, bf16[1024,512]{1,0:T(8,128)(2,1)} %get-tuple-element.50.key_raw.refs_1_, bf16[1024,512]{1,0:T(8,128)(2,1)} %get-tuple-element.51.value_raw.refs_2_, ...), custom_call_target="tpu_custom_call" | custom-call | flops 8589934592 | bytes 20971520 | tf_op jit(solution)/shard_map/attention_grads/pallas_call | solution.py:797
  591.9 31.8 %reduce-scatter.6.cloned.1.call-done = bf16[256,2048]{1,0:T(8,128)(2,1)} async-done(((bf16[1024,2048]{1,0:T(8,128)(2,1)}), bf16[256,2048]{1,0:T(8,128)(2,1)}) %reduce-scatter.6.cloned.1.call-update) | async-done | bytes 1048592 | tf_op jit(solution)/shard_map/reduce_scatter | solution.py:885
  623.7 84.4 %input_back.1 = (f32[256,2048]{1,0:T(8,128)}, f32[8,2048]{1,0:T(8,128)}) custom-call(bf16[1024,512]{1,0:T(8,128)(2,1)} %get-tuple-element.49.query_raw.refs_0_, bf16[1024,512]{1,0:T(8,128)(2,1)} %get-tuple-element.50.key_raw.refs_1_, bf16[1024,512]{1,0:T(8,128)(2,1)} %get-tuple-element.51.value_raw.refs_2_, ...), custom_call_target="tpu_custom_call" | custom-call | flops 6442450944 | bytes 209715200 | tf_op jit(solution)/shard_map/input_back/pallas_call | solution.py:398
  708.1 0.9 reduce_sum.41
  709.7 16.6 %gain_sum.1 = f32[8,512]{1,0:T(8,128)} custom-call(f32[8,512]{1,0:T(8,128)} %reshape.80.field), custom_call_target="tpu_custom_call" | custom-call | tf_op jit(solution)/shard_map/gain_sum/pallas_call | solution.py:451
  726.2 0.7 reshape.81
  727.0 0.7 multiply_subtract_fusion.2
  727.7 15.2 %multiply_subtract_fusion = (f32[3,256,2048]{2,1,0:T(8,128)}, f32[3,256,2048]{2,1,0:T(8,128)}, f32[3,256,2048]{2,1,0:T(8,128)}, f32[3,256,2048]{2,1,0:T(8,128)}) fusion(f32[3,256,2048]{2,1,0:T(8,128)} %param.18, f32[3,256,2048]{2,1,0:T(8,128)} %param.24, f32[3,256,2048]{2,1,0:T(8,128)} %param.21, bf16[3,256,2048]{2,1,0:T(8,128)(2,1)S(1)} %copy-done.2), kind=kLoop, calls=%fused_computation.2 | loop fusion | flops 25165824 | bytes 47185920 | tf_op jit(solution)/shard_map/sub | solution.py:821
  742.9 1.3 add_convert_fusion
  744.2 0.6 copy-done
  744.9 6.7 multiply_subtract_fusion.1
  751.6 1.3 copy.29
  (48 shorter events, 2.3 us)
Async XLA Ops:
  7.2 136.4 %all-gather.4.cloned.1.call-start = ((), (), s32[]{:S(2)}) async-start(), calls=%async_computation.3 | async-start | bytes 9437184 | tf_op jit(solution)/shard_map/all_gather | solution.py:853
  9.9 295.5 %all-gather.6.cloned.1.call-start = ((), (), s32[]{:S(2)}) async-start(), calls=%async_computation.4 | async-start | bytes 5242880 | tf_op jit(solution)/shard_map/all_gather | solution.py:855
  10.7 5.1 copy-start.11
  10.7 294.7 %all-gather.8.cloned.1.call-start = ((), (), s32[]{:S(2)}) async-start(), calls=%async_computation.5 | async-start | bytes 28311552 | tf_op jit(solution)/shard_map/all_gather | solution.py:869
  15.7 529.0 %reduce-scatter.4.cloned.1.call-start = ((), (), s32[]{:S(2)}) async-start(), calls=%async_computation.6 | async-start | bytes 28311552 | tf_op jit(solution)/shard_map/reduce_scatter | solution.py:872
  385.2 238.5 %reduce-scatter.6.cloned.1.call-start = ((), (), s32[]{:S(2)}) async-start(), calls=%async_computation.7 | async-start | bytes 5242880 | tf_op jit(solution)/shard_map/reduce_scatter | solution.py:885
  544.8 199.5 %reduce-scatter.8.cloned.1.call-start = ((), (), s32[]{:S(2)}) async-start(), calls=%async_computation.8 | async-start | bytes 9437184 | tf_op jit(solution)/shard_map/reduce_scatter | solution.py:893
  623.7 85.3 %copy-start.7 = (f32[8,2048]{1,0:T(8,128)S(1)}, f32[8,2048]{1,0:T(8,128)}, u32[]{:S(2)}) copy-start(f32[8,2048]{1,0:T(8,128)} %get-tuple-element.59) | copy-start | bytes 196612
  623.7 103.3 %copy-start.5 = (f32[2,2048]{1,0:T(2,128)S(1)}, f32[2,2048]{1,0:T(2,128)}, u32[]{:S(2)}) copy-start(f32[2,2048]{1,0:T(2,128)} %refs_8_.1) | copy-start | bytes 49156
  623.7 103.3 %copy-start.8 = (f32[2,2048]{1,0:T(2,128)S(1)}, f32[2,2048]{1,0:T(2,128)}, u32[]{:S(2)}) copy-start(f32[2,2048]{1,0:T(2,128)} %param.22) | copy-start | bytes 49156
  623.7 103.3 %copy-start.9 = (f32[2,2048]{1,0:T(2,128)S(1)}, f32[2,2048]{1,0:T(2,128)}, u32[]{:S(2)}) copy-start(f32[2,2048]{1,0:T(2,128)} %param.19) | copy-start | bytes 49156
  623.7 104.0 %copy-start.2 = (bf16[3,256,2048]{2,1,0:T(8,128)(2,1)S(1)}, bf16[3,256,2048]{2,1,0:T(8,128)(2,1)}, u32[]{:S(2)}) copy-start(bf16[3,256,2048]{2,1,0:T(8,128)(2,1)} %reduce-scatter.4.cloned.1.call-done) | copy-start | bytes 9437188
  727.0 15.9 %copy-start.6 = (f32[2,2048]{1,0:T(2,128)}, f32[2,2048]{1,0:T(2,128)S(1)}, u32[]{:S(2)}) copy-start(f32[2,2048]{1,0:T(2,128)S(1)} %reshape.81) | copy-start | bytes 49156
  727.7 15.2 %copy-start.1 = (f32[256,2048]{1,0:T(8,128)S(1)}, f32[256,2048]{1,0:T(8,128)}, u32[]{:S(2)}) copy-start(f32[256,2048]{1,0:T(8,128)} %get-tuple-element.39.refs_4_) | copy-start | bytes 6291460
  727.7 15.2 %copy-start.4 = (bf16[256,2048]{1,0:T(8,128)(2,1)S(1)}, bf16[256,2048]{1,0:T(8,128)(2,1)}, u32[]{:S(2)}) copy-start(bf16[256,2048]{1,0:T(8,128)(2,1)} %reduce-scatter.6.cloned.1.call-done) | copy-start | bytes 3145732
  742.9 2.0 copy-start
  742.9 2.0 copy-start.10
  744.9 6.7 copy-start.3
Sparse Core Ops, SparseCore 0:
  10.5 57.0 all-gather.3
  69.2 93.8 all-gather.5
  165.6 127.9 all-gather.7
  385.3 159.4 reduce-scatter.3
  546.9 76.7 reduce-scatter.5
  627.4 71.7 reduce-scatter.7

commit v5 on v4

--- a/solution.py
+++ b/solution.py
@@ -54,15 +54,23 @@
     return [pl.BlockSpec(memory_space=pltpu.VMEM)] * count
 
 
-def greet(n, me):
+def mate_of():
+    place = lax.axis_index("dp")
+    return place + 1 - 2 * (place % 2)
+
+
+def greet(n, me, mate=False):
     barrier = pltpu.get_barrier_semaphore()
+    if mate:
+        pl.semaphore_signal(barrier, inc=1, device_id={"dp": mate_of()}, device_id_type=MESH)
     for there, step in ((me > 0, -1), (me < n - 1, 1)):
 
         @pl.when(there)
         def _():
             pl.semaphore_signal(barrier, inc=1, device_id={"tensor": me + step}, device_id_type=MESH)
 
-    pl.semaphore_wait(barrier, (me > 0).astype(jnp.int32) + (me < n - 1).astype(jnp.int32))
+    count = (me > 0).astype(jnp.int32) + (me < n - 1).astype(jnp.int32)
+    pl.semaphore_wait(barrier, count + 1 if mate else count)
 
 
 def blocks_of(count, body):
@@ -169,7 +177,8 @@
             for way, dest in ((0, self.n - 1 - hop), (1, hop)):
                 needed = (dest > self.me, dest < self.me)[way]
                 run = self.run
-                pl.when(needed)(lambda: self.product(dest))
+                if self.lefts:
+                    pl.when(needed)(lambda: self.product(dest))
 
                 @pl.when(needed & jnp.logical_not(self.fed[way]))
                 def _():
@@ -184,7 +193,8 @@
                         blocks_of(self.rows // self.parts, body)
                         self.copy(way, part, hop).start()
 
-        self.product(self.me)
+        if self.lefts:
+            self.product(self.me)
 
     def arrivals(self, count):
         for way, behind in ((0, self.me), (1, self.n - 1 - self.me)):
@@ -473,13 +483,6 @@
     return (field * inverse_scale(field) * gains[0:1, :]).astype(jnp.bfloat16)
 
 
-def second_norm(at, total, more, results):
-    layer_in, gains = more
-    field = layer_in[pl.ds(at, BLOCK), :].astype(jnp.float32) + total
-    results[0][pl.ds(at, BLOCK), :] = field
-    return (field * inverse_scale(field) * gains[1:2, :]).astype(jnp.bfloat16)
-
-
 def norm_back(field, gradient, gain_row, gain_out):
     inv_scale = inverse_scale(field)
     normed = field * inv_scale
@@ -539,15 +542,43 @@
 
 
 def attention_forward_kernel(
-    first_in, weights, cos_ref, sine_ref, starts_ref,
-    queries, key_rows, values, attended, log_totals, turned_values
+    n, parts, first_in, weights, cos_ref, sine_ref, starts_ref, own_rows, layer_in, gains,
+    queries, key_rows, values, attended, log_totals, cot_rows, middle, second_in,
+    turned_values, held, held_sems, cot_sent, cot_got, rows_sent, rows_got, turn, totals, run,
+    sums_sent, sums_got
 ):
+    me = lax.axis_index("tensor")
+    second_core = lax.axis_index("dp") % 2 == 1
+    rows = own_rows.shape[0]
+    part_rows = rows // parts
     length, width = queries.shape
 
-    @pl.loop(0, length // QUERIES)
-    def _(block):
-        at = pl.ds(pl.multiple_of(block * QUERIES, QUERIES), QUERIES)
-        source = first_in[at, :]
+    def fetch(block):
+        return pltpu.make_async_copy(
+            first_in.at[pl.ds(block * QUERIES, QUERIES), :], held.at[block % 2], held_sems.at[block % 2]
+        )
+
+    fetch(0).start()
+    greet(n, me, True)
+    cot_gather = RowGather(n, me, 1, cot_rows, cot_sent, cot_got)
+    gather = RowGather(n, me, parts, second_in, rows_sent, rows_got)
+    sums = SumScatter(
+        n, me, parts, [attended], [weights.at[3]], totals, run, sums_sent, sums_got
+    )
+
+    def place_own(at):
+        place = pl.ds(pl.multiple_of(me * rows + at, BLOCK), BLOCK)
+        cot_rows[place, :] = own_rows[pl.ds(at, BLOCK), :]
+
+    blocks_of(rows, place_own)
+    cot_gather.start(0)
+
+    for block in range(length // QUERIES):
+        fetch(block).wait()
+        if (block + 1) * QUERIES < length:
+            fetch(block + 1).start()
+        at = pl.ds(block * QUERIES, QUERIES)
+        source = held[block % 2]
         cos_tile, sine_tile = cos_ref[at, :], sine_ref[at, :]
         for which, target in enumerate((queries, key_rows, values)):
             field = jnp.dot(source, weights[which], preferred_element_type=jnp.float32)
@@ -559,8 +590,7 @@
                     tile = tile.astype(jnp.bfloat16) * HEAD_DIM ** (-0.5)
                 target[at, pair * PAIR : (pair + 1) * PAIR] = tile.astype(jnp.bfloat16)
 
-    @pl.loop(0, width // PAIR)
-    def _(pair):
+    def attend(pair):
         lanes = pl.ds(pl.multiple_of(pair * PAIR, PAIR), PAIR)
         turned_values[...] = values[:, lanes].astype(jnp.float32).T.astype(jnp.bfloat16)
         for block in range(length // QUERIES):
@@ -585,48 +615,118 @@
                 log_totals[2 * pair + head, :, at] = peak + jnp.log(total)
             attended[at, lanes] = jnp.concatenate(both, axis=0).T.astype(jnp.bfloat16)
 
-
-def attention_forward(first_in, weights, cos_tile, sine_tile, starts):
+    pairs = width // PAIR
+    pl.loop(0, pairs - 1)(attend)
+    cot_gather.step(0, 0)
+    pl.loop(pairs - 1, pairs)(attend)
+
+    @pl.when(second_core)
+    def _():
+        for hop in range(1, n - 1):
+            cot_gather.step(0, hop)
+        pl.semaphore_wait(turn, 1)
+
+    sums.begin()
+
+    def finish_part(part):
+        def body(block):
+            at = pl.multiple_of(part * part_rows + block, BLOCK)
+            here = pl.ds(at, BLOCK)
+            total = totals[me, here, :].astype(jnp.float32)
+            field = layer_in[here, :].astype(jnp.float32) + total
+            middle[here, :] = field
+            place = pl.ds(pl.multiple_of(me * rows + at, BLOCK), BLOCK)
+            second_in[place, :] = (field * inverse_scale(field) * gains[1:2, :]).astype(jnp.bfloat16)
+
+        blocks_of(part_rows, body)
+
+    for part in range(parts):
+        for hop in range(1, n):
+            if part == 0 and hop < n - 1:
+                pl.when(jnp.logical_not(second_core))(lambda: cot_gather.step(0, hop))
+            if hop < n - 1:
+                sums.pass_on(part, hop)
+            else:
+                sums.last(part)
+            if part > 0:
+                gather.step(part - 1, hop - 1)
+        finish_part(part)
+        gather.start(part)
+
+    @pl.when(jnp.logical_not(second_core))
+    def _():
+        pl.semaphore_signal(turn, inc=1, device_id={"dp": mate_of()}, device_id_type=MESH)
+
+    for hop in range(n - 1):
+        gather.step(parts - 1, hop)
+    cot_gather.drain()
+    gather.drain()
+    sums.drain()
+
+
+def attention_forward(first_in, weights, cos_tile, sine_tile, starts, own_rows, layer_in, gains):
+    n = lax.axis_size("tensor")
+    parts = 2
     length, depth = first_in.shape
-    width = weights.shape[2]
+    rows, width = own_rows.shape[0], weights.shape[2]
     narrow = jax.ShapeDtypeStruct((length, width), jnp.bfloat16)
+    wide = jax.ShapeDtypeStruct((length, depth), jnp.bfloat16)
     outs = [
         narrow,
         narrow,
         narrow,
         narrow,
         jax.ShapeDtypeStruct((width // HEAD_DIM, 1, length), jnp.float32),
+        wide,
+        jax.ShapeDtypeStruct((rows, depth), jnp.float32),
+        wide,
     ]
-    specs = whole_part(5)
-    specs[1] = pl.BlockSpec((3, depth, width), lambda i: (0, 0, 0), pipeline_mode=pl.Buffered(1))
+    specs = whole_part(8)
+    specs[0] = pl.BlockSpec(memory_space=pl.ANY)
     return pl.pallas_call(
-        attention_forward_kernel,
-        grid=(1,),
+        functools.partial(attention_forward_kernel, n, parts),
         out_shape=outs,
         in_specs=specs,
         out_specs=whole_part(len(outs)),
-        scratch_shapes=[pltpu.VMEM((PAIR, length), jnp.bfloat16)],
-        compiler_params=pltpu.CompilerParams(vmem_limit_bytes=60 * 2**20),
+        scratch_shapes=[
+            pltpu.VMEM((PAIR, length), jnp.bfloat16),
+            pltpu.VMEM((2, QUERIES, depth), jnp.bfloat16),
+            pltpu.SemaphoreType.DMA((2,)),
+        ]
+        + gather_scratch(n, 1)
+        + gather_scratch(n, parts)
+        + [pltpu.SemaphoreType.REGULAR]
+        + scatter_scratch(n, parts, rows, depth),
+        compiler_params=pltpu.CompilerParams(
+            collective_id=5, has_side_effects=True, vmem_limit_bytes=60 * 2**20
+        ),
         cost_estimate=pl.CostEstimate(
-            flops=6 * length * depth * width, bytes_accessed=100 * 2**20, transcendentals=0
+            flops=8 * length * depth * width, bytes_accessed=400 * 2**20, transcendentals=0
         ),
         name="attention_forward",
-    )(first_in, weights, cos_tile, sine_tile, starts)
+    )(first_in, weights, cos_tile, sine_tile, starts, own_rows, layer_in, gains)
 
 
 def attention_back_kernel(
-    d_attn, out_weight, queries, key_rows, values, attended, log_totals, cos_ref, sine_ref,
-    starts_ref, query_raw, key_raw, value_raw,
-    d_attended, turned_keys, key_sum, value_sum, held, held_sems
+    n, d_attn, out_weight, queries, key_rows, values, attended, log_totals, cos_ref, sine_ref,
+    starts_ref, middle, out_sums, query_raw, key_raw, value_raw, layer_out,
+    d_attended, turned_keys, key_sum, value_sum, held, held_sems, totals, run, sent, got
 ):
+    me = lax.axis_index("tensor")
     length, width = queries.shape
+    sums = SumScatter(n, me, 1, [], [], totals, run, sent, got)
 
     def fetch(block):
         return pltpu.make_async_copy(
             d_attn.at[pl.ds(block * QUERIES, QUERIES), :], held.at[block % 2], held_sems.at[block % 2]
         )
 
+    ready = pltpu.make_async_copy(out_sums, totals, held_sems.at[2])
+    ready.start()
     fetch(0).start()
+    greet(n, me)
+    ready.wait()
+    sums.begin()
     for block in range(length // QUERIES):
         fetch(block).wait()
         if (block + 1) * QUERIES < length:
@@ -635,8 +735,7 @@
             held[block % 2], out_weight[0], preferred_element_type=jnp.float32
         ).astype(jnp.bfloat16)
 
-    @pl.loop(0, width // PAIR)
-    def _(pair):
+    def back_pair(pair):
         lanes = pl.ds(pl.multiple_of(pair * PAIR, PAIR), PAIR)
         turned_keys[...] = key_rows[:, lanes].astype(jnp.float32).T.astype(jnp.bfloat16)
         key_sum[...] = jnp.zeros_like(key_sum)
@@ -677,40 +776,60 @@
         key_raw[:, lanes] = turned(key_sum[...], cos_ref[...], -sine_ref[...]).astype(jnp.bfloat16)
         value_raw[:, lanes] = value_sum[...].astype(jnp.bfloat16)
 
+    pairs = width // PAIR
+    for count in range(1, n):
+        pl.loop(pairs * (count - 1) // (n - 1), pairs * count // (n - 1))(back_pair)
+        if count < n - 1:
+            sums.pass_on(0, count)
+    sums.last(0)
+
+    def body(at):
+        rows = pl.ds(at, BLOCK)
+        total = middle[rows, :] + totals[me, rows, :].astype(jnp.float32)
+        layer_out[rows, :] = total.astype(jnp.bfloat16)
+
+    blocks_of(middle.shape[0], body)
+    sums.drain()
+
 
 def attention_back(
-    d_attn, attn_low, queries, key_rows, values, attended, log_totals, cos_tile, sine_tile, starts
+    d_attn, attn_low, queries, key_rows, values, attended, log_totals, cos_tile, sine_tile, starts,
+    middle, out_sums
 ):
+    n = lax.axis_size("tensor")
     length, depth = d_attn.shape
-    width = queries.shape[1]
+    width, rows = queries.shape[1], middle.shape[0]
     narrow = jax.ShapeDtypeStruct((length, width), jnp.bfloat16)
-    specs = whole_part(10)
-    specs[0] = pl.BlockSpec(memory_space=pl.ANY)
-    specs[1] = pl.BlockSpec(
-        (1, depth, width), lambda i: (3, 0, 0), pipeline_mode=pl.Buffered(1)
-    )
+    specs = whole_part(12)
+    specs[0] = specs[11] = pl.BlockSpec(memory_space=pl.ANY)
+    specs[1] = pl.BlockSpec((1, depth, width), lambda i: (3, 0, 0), pipeline_mode=pl.Buffered(1))
+    scratch = scatter_scratch(n, 1, rows, depth)
+    scratch[0] = pltpu.VMEM((n, rows, depth), jnp.bfloat16)
     return pl.pallas_call(
-        attention_back_kernel,
+        functools.partial(attention_back_kernel, n),
         grid=(1,),
-        out_shape=[narrow, narrow, narrow],
+        out_shape=[narrow, narrow, narrow, jax.ShapeDtypeStruct((rows, depth), jnp.bfloat16)],
         in_specs=specs,
-        out_specs=whole_part(3),
+        out_specs=whole_part(4),
         scratch_shapes=[
             pltpu.VMEM((length, width), jnp.bfloat16),
             pltpu.VMEM((PAIR, length), jnp.bfloat16),
             pltpu.VMEM((length, PAIR), jnp.float32),
             pltpu.VMEM((length, PAIR), jnp.float32),
             pltpu.VMEM((2, QUERIES, depth), jnp.bfloat16),
-            pltpu.SemaphoreType.DMA((2,)),
-        ],
-        compiler_params=pltpu.CompilerParams(vmem_limit_bytes=60 * 2**20),
+            pltpu.SemaphoreType.DMA((3,)),
+        ]
+        + scratch,
+        compiler_params=pltpu.CompilerParams(
+            collective_id=6, has_side_effects=True, vmem_limit_bytes=60 * 2**20
+        ),
         cost_estimate=pl.CostEstimate(
-            flops=2 * length * depth * width, bytes_accessed=120 * 2**20, transcendentals=0
+            flops=2 * length * depth * width, bytes_accessed=200 * 2**20, transcendentals=0
         ),
         name="attention_back",
     )(
         d_attn, attn_low, queries, key_rows, values, attended, log_totals, cos_tile, sine_tile,
-        starts
+        starts, middle, out_sums.reshape(n, rows, depth)
     )
 
 
@@ -852,19 +971,10 @@
     )
     attn_low = lax.all_gather(attn_weight.astype(jnp.bfloat16), "dp", axis=1, tiled=True)
 
-    grad_out = lax.all_gather(cotangent, "tensor", axis=0, tiled=True)
-    queries, key_rows, values, attended, log_totals = attention_forward(
-        first_in, attn_low, cos_tile, sine_tile, starts
-    )
-    middle, second_in = exchange(
-        "attention_out",
-        2,
-        [(attended, attn_low, 3)],
-        [inputs, norm_gains],
-        [rows_f32],
-        finish=second_norm,
-        gathers=True,
-        parts=2,
+    (
+        queries, key_rows, values, attended, log_totals, grad_out, middle, second_in
+    ) = attention_forward(
+        first_in, attn_low, cos_tile, sine_tile, starts, cotangent, inputs, norm_gains
     )
     mlp_low = lax.all_gather(mlp_weight.astype(jnp.bfloat16), "dp", axis=1, tiled=True)
     hidden, d_gate, d_up, mlp_sums = mlp_middle(second_in, grad_out, mlp_low)
@@ -881,17 +991,14 @@
         parts=2,
         side=(hidden, mlp_low),
     )
-    out_sums, mlp_owned = lax.optimization_barrier((out_sums, mlp_owned))
-    out_rows = lax.psum_scatter(out_sums, "tensor", scatter_dimension=0, tiled=True)
-    query_raw, key_raw, value_raw = attention_back(
+    query_raw, key_raw, value_raw, layer_out = attention_back(
         d_attn, attn_low, queries, key_rows, values, attended, log_totals, cos_tile, sine_tile,
-        starts
-    )
-    attn_sums, out_rows = lax.optimization_barrier(
-        (attention_grads(first_in, query_raw, key_raw, value_raw, d_attn, attended), out_rows)
+        starts, middle, out_sums
+    )
+    attn_sums, mlp_owned = lax.optimization_barrier(
+        (attention_grads(first_in, query_raw, key_raw, value_raw, d_attn, attended), mlp_owned)
     )
     attn_owned = lax.psum_scatter(attn_sums, "dp", scatter_dimension=1, tiled=True)
-    layer_out = (middle + out_rows.astype(jnp.float32)).astype(jnp.bfloat16)
     mlp_grad, attn_grad = mlp_owned.astype(jnp.float32), attn_owned.astype(jnp.float32)
     grad_in, gain_one = exchange(
         "input_back",

time: 768 us -> 693 us (0.902)
  waiting for transfers between devices: 40 us -> 0.43 us
  Pallas kernels: 664 us -> 635 us
    pallas_call x4 -> x3, Pallas kernels: 492 us -> 277 us  [line_exchange(): pl.pallas_call(functools.partial(line_kernel, n, parts, len(pairs), len(e...]
    pallas_call x2, Pallas kernels: 55.6 us -> 205 us  [the longest x1 148 us: attention_forward(): pl.pallas_call(functools.partial(attention_forward_kernel, n, parts), out...]
    pallas_call x1, Pallas kernels: 16.6 us -> 52.8 us  [sum_everywhere(): pl.pallas_call(functools.partial(everywhere_kernel, sizes), out_shape=jax...]
    reduce_scatter x1 -> x0, waiting for transfers between devices: 31.8 us -> none  [local(): lax.psum_scatter(out_sums, 'tensor', scatter_dimension=0, tiled=True)]
  transfers between devices with their start and end apart: 6 -> 4, of which waited for: 2 -> 1; matrix products, arithmetic and copies ran while one was open for 4% -> 4% of each run, Pallas kernels for 77% -> 81%
where the time goes in v5:
time: 693 us; the launch traced here: 690 us
  Pallas kernels  635 us (92%)
  other arithmetic  36.2 us (5%)
  between operations  14.3 us (2%)
    pallas_call x3, Pallas kernels, line_exchange(): pl.pallas_call(functools.partial(line_kernel, n, parts, len(pairs), len(e...  277 us
    pallas_call x1, Pallas kernels, attention_forward(): pl.pallas_call(functools.partial(attention_forward_kernel, n, parts), out...  148 us
    pallas_call x1, Pallas kernels, mlp_middle(): pl.pallas_call(mlp_kernel, grid=(units // tile,), out_shape=[wide, wide,...  79.6 us
    pallas_call x1, Pallas kernels, attention_back(): pl.pallas_call(functools.partial(attention_back_kernel, n), grid=(1,), ou...  57.1 us
    pallas_call x1, Pallas kernels, sum_everywhere(): pl.pallas_call(functools.partial(everywhere_kernel, sizes), out_shape=jax...  52.8 us
    sub x3, other arithmetic, adam_update(): weight - step_rate * (first_new / fix_one / (jnp.sqrt(second_new / fix_tw...  23 us
    pallas_call x1, Pallas kernels, attention_grads(): pl.pallas_call(grads_kernel, grid=(4,), out_shape=jax.ShapeDtypeStruct((4...  20.5 us
  transfers between devices with their start and end apart: 4, of which 1 were waited for; matrix products, arithmetic and copies ran while one was open for 4% of the time, Pallas kernels for 81%

profile of v5, /device:TPU:0, one launch (start us, length us, event | category | flops | bytes accessed | tf_op | source)
XLA Modules:
  0.0 689.6 jit_solution(3895707448738302535)
XLA Ops:
  7.2 2.7 convert_element_type.22
  10.0 4.9 convert_element_type.25
  15.0 0.2 reduce-window.4
  15.2 78.3 %first_norm.1.first_in = bf16[1024,2048]{1,0:T(8,128)(2,1)} custom-call(bf16[256,2048]{1,0:T(8,128)(2,1)} %refs_6_.3, f32[2,2048]{1,0:T(2,128)} %refs_8_.1), custom_call_target="tpu_custom_call" | custom-call | flops 4194304 | bytes 209715200 | tf_op jit(solution)/shard_map/first_norm/pallas_call | solution.py:408
  93.5 0.1 convert_reduce_fusion
  93.7 1.9 fusion.2
  95.6 1.8 pad_maximum_fusion
  97.4 0.6 subtract_subtract_fusion.starts_ref
  98.0 147.8 %attention_forward.1 = (bf16[1024,512]{1,0:T(8,128)(2,1)}, bf16[1024,512]{1,0:T(8,128)(2,1)}, bf16[1024,512]{1,0:T(8,128)(2,1)}, bf16[1024,512]{1,0:T(8,128)(2,1...) custom-call(bf16[1024,2048]{1,0:T(8,128)(2,1)} %first_norm.1.first_in,, ...), custom_call_target="tpu_custom_call" | custom-call | flops 8589934592 | bytes 419430400 | tf_op jit(solution)/shard_map/attention_forward/pallas_call | solution.py:686
  245.8 79.6 %mlp_middle.1 = (bf16[1024,2048]{1,0:T(8,128)(2,1)}, bf16[1024,2048]{1,0:T(8,128)(2,1)}, bf16[1024,2048]{1,0:T(8,128)(2,1)}, bf16[3,2048,2048]{2,1,0:T(8,128)(2,1)}) custom-call(bf16[1024,2048]{1,0:T(8,128)(2,1)} %get-tuple-element.38.second_in, bf16[1024,2048]{1,0:T(8,128)(2,1)} %get-tuple-element.39.cotangent, ...), custom_call_target="tpu_custom_call" | custom-call | flops 51539607552 | bytes 62914560 | tf_op jit(solution)/shard_map/mlp_middle/pallas_call | solution.py:882
  325.5 135.4 %mlp_back.1 = (f32[256,2048]{1,0:T(8,128)}, f32[8,2048]{1,0:T(8,128)}, bf16[1024,2048]{1,0:T(8,128)(2,1)}, bf16[1024,2048]{1,0:T(8,128)(2,1)}) custom-call(bf16[1024,2048]{1,0:T(8,128)(2,1)} %get-tuple-element.40.refs_0_, bf16[1024,2048]{1,0:T(8,128)(2,1)} %get-tuple-element.41.refs_1_, ...), custom_call_target="tpu_custom_call" | custom-call | flops 17179869184 | bytes 209715200 | tf_op jit(solution)/shard_map/mlp_back/pallas_call | solution.py:408
  460.9 57.1 %attention_back.1 = (bf16[1024,512]{1,0:T(8,128)(2,1)}, bf16[1024,512]{1,0:T(8,128)(2,1)}, bf16[1024,512]{1,0:T(8,128)(2,1)}, bf16[256,2048]{1,0:T(8,128)(2,1)}) custom-call(bf16[1024,2048]{1,0:T(8,128)(2,1)} %get-tuple-element.44.d_attn, bf16[4,2048,512]{2,1,0:T(8,128)(2,1)} %all-gather.3.cloned.1.call-done.weights.out_weight.refs_3_.refs_4_.refs_5_, ...), custom_call_target="tpu_custom_call" | custom-call | flops 2147483648 | bytes 209715200 | tf_op jit(solution)/shard_map/attention_back/pallas_call | solution.py:808
  518.1 20.5 %attention_grads.1 = bf16[4,2048,512]{2,1,0:T(8,128)(2,1)} custom-call(bf16[1024,2048]{1,0:T(8,128)(2,1)} %first_norm.1.first_in, bf16[1024,512]{1,0:T(8,128)(2,1)} %get-tuple-element.52.refs_0_.query_raw, bf16[1024,512]{1,0:T(8,128)(2,1)} %get-tuple-element.53.refs_1_.key_raw, bf16[1024,512]{1,0:T(8,128)(2,1)} %get-tuple-element.54.refs_2_.value_raw, ...), custom_call_target="tpu_custom_call" | custom-call | flops 8589934592 | bytes 20971520 | tf_op jit(solution)/shard_map/attention_grads/pallas_call | solution.py:916
  538.6 0.3 reduce-scatter.3.cloned.1.call-done
  539.0 63.4 %input_back.1 = (f32[256,2048]{1,0:T(8,128)}, f32[8,2048]{1,0:T(8,128)}) custom-call(bf16[1024,512]{1,0:T(8,128)(2,1)} %get-tuple-element.52.refs_0_.query_raw, bf16[1024,512]{1,0:T(8,128)(2,1)} %get-tuple-element.53.refs_1_.key_raw, bf16[1024,512]{1,0:T(8,128)(2,1)} %get-tuple-element.54.refs_2_.value_raw, ...), custom_call_target="tpu_custom_call" | custom-call | flops 6442450944 | bytes 209715200 | tf_op jit(solution)/shard_map/input_back/pallas_call | solution.py:408
  602.4 0.9 reduce_sum.41
  603.3 0.6 reshape.84.field
  603.9 52.8 %gain_sum.1 = f32[8,512]{1,0:T(8,128)} custom-call(f32[8,512]{1,0:T(8,128)} %reshape.84.field), custom_call_target="tpu_custom_call" | custom-call | tf_op jit(solution)/shard_map/gain_sum/pallas_call | solution.py:461
  656.7 0.7 reshape.85
  657.5 0.7 multiply_subtract_fusion.2
  658.2 15.6 %multiply_subtract_fusion = (f32[3,256,2048]{2,1,0:T(8,128)}, f32[3,256,2048]{2,1,0:T(8,128)}, f32[3,256,2048]{2,1,0:T(8,128)}, f32[3,256,2048]{2,1,0:T(8,128)}) fusion(f32[3,256,2048]{2,1,0:T(8,128)} %param.18, f32[3,256,2048]{2,1,0:T(8,128)} %param.24, f32[3,256,2048]{2,1,0:T(8,128)} %param.21, bf16[3,256,2048]{2,1,0:T(8,128)(2,1)} %reduce-scatter.3.cloned.1.call-done), kind=kLoop, calls=%fused_computation.2 | loop fusion | flops 25165824 | bytes 47185920 | tf_op jit(solution)/shard_map/sub | solution.py:940
  673.8 6.7 multiply_subtract_fusion.1
  680.5 1.0 copy.30
  681.5 1.3 copy.31
  (37 shorter events, 0.5 us)
Async XLA Ops:
  7.2 90.9 %all-gather.3.cloned.1.call-start = ((), (), s32[]{:S(2)}) async-start(), calls=%async_computation.2 | async-start | bytes 9437184 | tf_op jit(solution)/shard_map/all_gather | solution.py:972
  9.9 5.1 copy-start.9
  10.0 235.9 %all-gather.5.cloned.1.call-start = ((), (), s32[]{:S(2)}) async-start(), calls=%async_computation.3 | async-start | bytes 28311552 | tf_op jit(solution)/shard_map/all_gather | solution.py:979
  15.0 523.9 %reduce-scatter.3.cloned.1.call-start = ((), (), s32[]{:S(2)}) async-start(), calls=%async_computation.4 | async-start | bytes 28311552 | tf_op jit(solution)/shard_map/reduce_scatter | solution.py:982
  325.5 348.3 %reduce-scatter.5.cloned.1.call-start = ((), (), s32[]{:S(2)}) async-start(), calls=%async_computation.5 | async-start | bytes 9437184 | tf_op jit(solution)/shard_map/reduce_scatter | solution.py:1001
  538.9 64.3 %copy-start.5 = (f32[8,2048]{1,0:T(8,128)S(1)}, f32[8,2048]{1,0:T(8,128)}, u32[]{:S(2)}) copy-start(f32[8,2048]{1,0:T(8,128)} %get-tuple-element.58) | copy-start | bytes 196612
  538.9 118.5 %copy-start.3 = (f32[2,2048]{1,0:T(2,128)S(1)}, f32[2,2048]{1,0:T(2,128)}, u32[]{:S(2)}) copy-start(f32[2,2048]{1,0:T(2,128)} %refs_8_.1) | copy-start | bytes 49156
  539.0 118.5 %copy-start.6 = (f32[2,2048]{1,0:T(2,128)S(1)}, f32[2,2048]{1,0:T(2,128)}, u32[]{:S(2)}) copy-start(f32[2,2048]{1,0:T(2,128)} %param.22) | copy-start | bytes 49156
  539.0 118.5 %copy-start.7 = (f32[2,2048]{1,0:T(2,128)S(1)}, f32[2,2048]{1,0:T(2,128)}, u32[]{:S(2)}) copy-start(f32[2,2048]{1,0:T(2,128)} %param.19) | copy-start | bytes 49156
  657.5 16.3 %copy-start.4 = (f32[2,2048]{1,0:T(2,128)}, f32[2,2048]{1,0:T(2,128)S(1)}, u32[]{:S(2)}) copy-start(f32[2,2048]{1,0:T(2,128)S(1)} %reshape.85) | copy-start | bytes 49156
  658.2 15.6 %copy-start = (f32[4,256,512]{2,1,0:T(8,128)S(1)}, f32[4,256,512]{2,1,0:T(8,128)}, u32[]{:S(2)}) copy-start(f32[4,256,512]{2,1,0:T(8,128)} %param.17) | copy-start | bytes 6291460
  658.2 15.6 %copy-start.8 = (f32[4]{0:T(128)S(1)}, f32[4]{0:T(128)}, u32[]{:S(2)}) copy-start(f32[4]{0:T(128)} %constant.12) | copy-start | bytes 52
  673.8 6.8 copy-start.2
  673.8 7.7 %copy-start.1 = (f32[256,2048]{1,0:T(8,128)S(1)}, f32[256,2048]{1,0:T(8,128)}, u32[]{:S(2)}) copy-start(f32[256,2048]{1,0:T(8,128)} %get-tuple-element.93) | copy-start | bytes 6291460
Sparse Core Ops, SparseCore 0:
  10.5 57.0 all-gather.2
  70.1 125.3 all-gather.4
  325.6 213.2 reduce-scatter.2
  542.2 115.7 reduce-scatter.4

commit v6 on v5

--- a/solution.py
+++ b/solution.py
@@ -122,7 +122,8 @@
                 pl.when(self.has_left)(lambda: self.copy(1, part, hop + 1, owner).start())
 
     def drain(self):
-        for part in range(self.parts):
+        @pl.loop(0, self.parts)
+        def _(part):
             for hop in range(self.n - 1):
                 pl.when(self.has_right & (hop <= self.me))(
                     lambda: self.copy(0, part, hop, self.me - hop).wait_send()
@@ -173,24 +174,25 @@
         return part * (self.n + 1) + (hop, self.n - hop)[way]
 
     def begin(self):
+        part_rows = self.rows // self.parts
         for hop in range(self.n - 1):
             for way, dest in ((0, self.n - 1 - hop), (1, hop)):
                 needed = (dest > self.me, dest < self.me)[way]
-                run = self.run
                 if self.lefts:
                     pl.when(needed)(lambda: self.product(dest))
 
                 @pl.when(needed & jnp.logical_not(self.fed[way]))
                 def _():
-                    for part in range(self.parts):
-                        first = part * (self.rows // self.parts)
+                    @pl.loop(0, self.parts)
+                    def _(part):
                         slot = self.place(way, part, hop)
 
                         def body(at):
-                            own = self.totals[dest, pl.ds(first + at, BLOCK), :]
-                            run[slot, pl.ds(at, BLOCK), :] = own.astype(jnp.bfloat16)
-
-                        blocks_of(self.rows // self.parts, body)
+                            first = pl.multiple_of(part * part_rows + at, BLOCK)
+                            own = self.totals[dest, pl.ds(first, BLOCK), :]
+                            self.run[slot, pl.ds(at, BLOCK), :] = own.astype(jnp.bfloat16)
+
+                        blocks_of(part_rows, body)
                         self.copy(way, part, hop).start()
 
         if self.lefts:
@@ -211,7 +213,8 @@
                 self.copy(way, part, hop).wait_recv()
 
                 def body(at):
-                    own = self.totals[dest, pl.ds(first + at, BLOCK), :].astype(jnp.float32)
+                    here = pl.ds(pl.multiple_of(first + at, BLOCK), BLOCK)
+                    own = self.totals[dest, here, :].astype(jnp.float32)
                     came = run[slot, pl.ds(at, BLOCK), :].astype(jnp.float32)
                     run[slot, pl.ds(at, BLOCK), :] = (own + came).astype(jnp.bfloat16)
 
@@ -228,7 +231,7 @@
                 self.copy(way, part, hop).wait_recv()
 
                 def body(at):
-                    own = pl.ds(first + at, BLOCK)
+                    own = pl.ds(pl.multiple_of(first + at, BLOCK), BLOCK)
                     came = run[slot, pl.ds(at, BLOCK), :].astype(jnp.float32)
                     total = self.totals[self.me, own, :].astype(jnp.float32) + came
                     self.totals[self.me, own, :] = total.astype(self.totals.dtype)
@@ -236,7 +239,8 @@
                 blocks_of(self.rows // self.parts, body)
 
     def drain(self):
-        for part in range(self.parts):
+        @pl.loop(0, self.parts)
+        def _(part):
             for hop in range(self.n - 1):
                 pl.when(self.n - 1 - hop > self.me)(lambda: self.copy(0, part, hop).wait_send())
                 pl.when(hop < self.me)(lambda: self.copy(1, part, hop).wait_send())
@@ -358,24 +362,26 @@
         sums.begin()
     if filler:
         filler.open(lefts)
-    for part in range(parts):
-        for hop in range(n - 1):
-            if filler:
-                filler.step()
-            if products and hop < n - 2:
-                sums.pass_on(part, hop + 1)
-            if products and hop == n - 2:
-                sums.last(part)
-            if gathers and part > 0:
-                gather.step(part - 1, hop)
+    def complete(part):
+        if products:
+            sums.last(part)
         finish_part(part)
         if gathers:
             gather.start(part)
+
+    if products:
+        for count in range(1, n - 1):
+            if filler:
+                filler.step()
+            pl.loop(0, parts)(lambda part: sums.pass_on(part, count))
+        if filler:
+            filler.step()
+    pl.loop(0, parts)(complete)
     if gathers:
         for hop in range(n - 1):
             if filler:
                 filler.step()
-            gather.step(parts - 1, hop)
+            pl.loop(0, parts)(lambda part: gather.step(part, hop))
         gather.drain()
     if filler:
         filler.close()
@@ -640,25 +646,24 @@
 
         blocks_of(part_rows, body)
 
-    for part in range(parts):
-        for hop in range(1, n):
-            if part == 0 and hop < n - 1:
-                pl.when(jnp.logical_not(second_core))(lambda: cot_gather.step(0, hop))
-            if hop < n - 1:
-                sums.pass_on(part, hop)
-            else:
-                sums.last(part)
-            if part > 0:
-                gather.step(part - 1, hop - 1)
+    def complete(part):
+        sums.last(part)
         finish_part(part)
         gather.start(part)
+
+    for count in range(1, n - 1):
+        pl.loop(0, parts)(lambda part: sums.pass_on(part, count))
+        if count < n - 2:
+            pl.when(jnp.logical_not(second_core))(lambda: cot_gather.step(0, count))
+    pl.loop(0, parts)(complete)
 
     @pl.when(jnp.logical_not(second_core))
     def _():
         pl.semaphore_signal(turn, inc=1, device_id={"dp": mate_of()}, device_id_type=MESH)
+        cot_gather.step(0, n - 2)
 
     for hop in range(n - 1):
-        gather.step(parts - 1, hop)
+        pl.loop(0, parts)(lambda part: gather.step(part, hop))
     cot_gather.drain()
     gather.drain()
     sums.drain()
@@ -666,7 +671,7 @@
 
 def attention_forward(first_in, weights, cos_tile, sine_tile, starts, own_rows, layer_in, gains):
     n = lax.axis_size("tensor")
-    parts = 2
+    parts = 4
     length, depth = first_in.shape
     rows, width = own_rows.shape[0], weights.shape[2]
     narrow = jax.ShapeDtypeStruct((length, width), jnp.bfloat16)
@@ -714,7 +719,8 @@
 ):
     me = lax.axis_index("tensor")
     length, width = queries.shape
-    sums = SumScatter(n, me, 1, [], [], totals, run, sent, got)
+    parts = 4
+    sums = SumScatter(n, me, parts, [], [], totals, run, sent, got)
 
     def fetch(block):
         return pltpu.make_async_copy(
@@ -780,8 +786,8 @@
     for count in range(1, n):
         pl.loop(pairs * (count - 1) // (n - 1), pairs * count // (n - 1))(back_pair)
         if count < n - 1:
-            sums.pass_on(0, count)
-    sums.last(0)
+            pl.loop(0, parts)(lambda part: sums.pass_on(part, count))
+    pl.loop(0, parts)(sums.last)
 
     def body(at):
         rows = pl.ds(at, BLOCK)
@@ -803,7 +809,7 @@
     specs = whole_part(12)
     specs[0] = specs[11] = pl.BlockSpec(memory_space=pl.ANY)
     specs[1] = pl.BlockSpec((1, depth, width), lambda i: (3, 0, 0), pipeline_mode=pl.Buffered(1))
-    scratch = scatter_scratch(n, 1, rows, depth)
+    scratch = scatter_scratch(n, 4, rows, depth)
     scratch[0] = pltpu.VMEM((n, rows, depth), jnp.bfloat16)
     return pl.pallas_call(
         functools.partial(attention_back_kernel, n),
@@ -967,7 +973,7 @@
     gain_f32 = jax.ShapeDtypeStruct((8, width), jnp.float32)
     exchange = functools.partial(line_exchange, rows=row_count, width=width)
     (first_in,) = exchange(
-        "first_norm", 1, [], [inputs, norm_gains], [], finish=first_norm, gathers=True, parts=1
+        "first_norm", 1, [], [inputs, norm_gains], [], finish=first_norm, gathers=True, parts=4
     )
     attn_low = lax.all_gather(attn_weight.astype(jnp.bfloat16), "dp", axis=1, tiled=True)
 
@@ -988,7 +994,7 @@
         [rows_f32, gain_f32],
         finish=second_back,
         gathers=True,
-        parts=2,
+        parts=4,
         side=(hidden, mlp_low),
     )
     query_raw, key_raw, value_raw, layer_out = attention_back(
@@ -1008,7 +1014,7 @@
         [rows_f32, gain_f32],
         finish=first_back,
         gathers=False,
-        parts=1,
+        parts=4,
     )
     gain_parts = jnp.stack([jnp.sum(gain_one, axis=0), jnp.sum(gain_two, axis=0)])
     gain_grad = sum_everywhere(gain_parts.reshape(8, -1)).reshape(norm_gains.shape)

time: 693 us -> 640 us (0.924)
  Pallas kernels: 635 us -> 578 us
    pallas_call x3, Pallas kernels: 277 us -> 246 us  [line_exchange(): pl.pallas_call(functools.partial(line_kernel, n, parts, len(pairs), len(e...]
    pallas_call x1, Pallas kernels: 57.1 us -> 46.1 us  [attention_back(): pl.pallas_call(functools.partial(attention_back_kernel, n), grid=(1,), ou...]
    pallas_call x1, Pallas kernels: 52.8 us -> 44.7 us  [sum_everywhere(): pl.pallas_call(functools.partial(everywhere_kernel, sizes), out_shape=jax...]
    pallas_call x1, Pallas kernels: 148 us -> 141 us  [attention_forward(): pl.pallas_call(functools.partial(attention_forward_kernel, n, parts), out...]
  transfers between devices with their start and end apart: 4 -> 4, of which waited for: 1 -> 1; matrix products, arithmetic and copies ran while one was open for 4% -> 4% of each run, Pallas kernels for 81% -> 78%
where the time goes in v6:
time: 640 us; the launch traced here: 637 us
  Pallas kernels  578 us (90%)
  other arithmetic  36.3 us (6%)
  between operations  14.3 us (2%)
    pallas_call x3, Pallas kernels, line_exchange(): pl.pallas_call(functools.partial(line_kernel, n, parts, len(pairs), len(e...  246 us
    pallas_call x1, Pallas kernels, attention_forward(): pl.pallas_call(functools.partial(attention_forward_kernel, n, parts), out...  141 us
    pallas_call x1, Pallas kernels, mlp_middle(): pl.pallas_call(mlp_kernel, grid=(units // tile,), out_shape=[wide, wide,...  79.6 us
    pallas_call x1, Pallas kernels, attention_back(): pl.pallas_call(functools.partial(attention_back_kernel, n), grid=(1,), ou...  46.1 us
    pallas_call x1, Pallas kernels, sum_everywhere(): pl.pallas_call(functools.partial(everywhere_kernel, sizes), out_shape=jax...  44.7 us
    sub x3, other arithmetic, adam_update(): weight - step_rate * (first_new / fix_one / (jnp.sqrt(second_new / fix_tw...  23 us
    pallas_call x1, Pallas kernels, attention_grads(): pl.pallas_call(grads_kernel, grid=(4,), out_shape=jax.ShapeDtypeStruct((4...  20.5 us
  transfers between devices with their start and end apart: 4, of which 1 were waited for; matrix products, arithmetic and copies ran while one was open for 4% of the time, Pallas kernels for 78%

profile of v6, /device:TPU:0, one launch (start us, length us, event | category | flops | bytes accessed | tf_op | source)
XLA Modules:
  0.0 636.6 jit_solution(1141194445322234097)
XLA Ops:
  7.2 2.7 convert_element_type.22
  10.0 4.9 convert_element_type.25
  15.0 0.2 reduce-window.4
  15.2 76.3 %first_norm.1.first_in = bf16[1024,2048]{1,0:T(8,128)(2,1)} custom-call(bf16[256,2048]{1,0:T(8,128)(2,1)} %refs_6_.3, f32[2,2048]{1,0:T(2,128)} %refs_8_.1), custom_call_target="tpu_custom_call" | custom-call | flops 4194304 | bytes 209715200 | tf_op jit(solution)/shard_map/first_norm/pallas_call | solution.py:414
  91.5 0.1 convert_reduce_fusion
  91.7 1.9 fusion.2
  93.6 1.8 pad_maximum_fusion
  95.5 0.6 subtract_subtract_fusion.starts_ref
  96.1 140.6 %attention_forward.1 = (bf16[1024,512]{1,0:T(8,128)(2,1)}, bf16[1024,512]{1,0:T(8,128)(2,1)}, bf16[1024,512]{1,0:T(8,128)(2,1)}, bf16[1024,512]{1,0:T(8,128)(2,1...) custom-call(bf16[1024,2048]{1,0:T(8,128)(2,1)} %first_norm.1.first_in,, ...), custom_call_target="tpu_custom_call" | custom-call | flops 8589934592 | bytes 419430400 | tf_op jit(solution)/shard_map/attention_forward/pallas_call | solution.py:691
  236.8 79.6 %mlp_middle.1 = (bf16[1024,2048]{1,0:T(8,128)(2,1)}, bf16[1024,2048]{1,0:T(8,128)(2,1)}, bf16[1024,2048]{1,0:T(8,128)(2,1)}, bf16[3,2048,2048]{2,1,0:T(8,128)(2,1)}) custom-call(bf16[1024,2048]{1,0:T(8,128)(2,1)} %get-tuple-element.38.second_in, bf16[1024,2048]{1,0:T(8,128)(2,1)} %get-tuple-element.39.cotangent, ...), custom_call_target="tpu_custom_call" | custom-call | flops 51539607552 | bytes 62914560 | tf_op jit(solution)/shard_map/mlp_middle/pallas_call | solution.py:888
  316.5 117.8 %mlp_back.1 = (f32[256,2048]{1,0:T(8,128)}, f32[8,2048]{1,0:T(8,128)}, bf16[1024,2048]{1,0:T(8,128)(2,1)}, bf16[1024,2048]{1,0:T(8,128)(2,1)}) custom-call(bf16[1024,2048]{1,0:T(8,128)(2,1)} %get-tuple-element.40.refs_0_, bf16[1024,2048]{1,0:T(8,128)(2,1)} %get-tuple-element.41.refs_1_, ...), custom_call_target="tpu_custom_call" | custom-call | flops 17179869184 | bytes 209715200 | tf_op jit(solution)/shard_map/mlp_back/pallas_call | solution.py:414
  434.3 46.1 %attention_back.1 = (bf16[1024,512]{1,0:T(8,128)(2,1)}, bf16[1024,512]{1,0:T(8,128)(2,1)}, bf16[1024,512]{1,0:T(8,128)(2,1)}, bf16[256,2048]{1,0:T(8,128)(2,1)}) custom-call(bf16[1024,2048]{1,0:T(8,128)(2,1)} %get-tuple-element.44.d_attn, bf16[4,2048,512]{2,1,0:T(8,128)(2,1)} %all-gather.3.cloned.1.call-done.weights.out_weight.refs_3_.refs_4_.refs_5_, ...), custom_call_target="tpu_custom_call" | custom-call | flops 2147483648 | bytes 209715200 | tf_op jit(solution)/shard_map/attention_back/pallas_call | solution.py:814
  480.4 20.5 %attention_grads.1 = bf16[4,2048,512]{2,1,0:T(8,128)(2,1)} custom-call(bf16[1024,2048]{1,0:T(8,128)(2,1)} %first_norm.1.first_in, bf16[1024,512]{1,0:T(8,128)(2,1)} %get-tuple-element.52.refs_0_.query_raw, bf16[1024,512]{1,0:T(8,128)(2,1)} %get-tuple-element.53.refs_1_.key_raw, bf16[1024,512]{1,0:T(8,128)(2,1)} %get-tuple-element.54.refs_2_.value_raw, ...), custom_call_target="tpu_custom_call" | custom-call | flops 8589934592 | bytes 20971520 | tf_op jit(solution)/shard_map/attention_grads/pallas_call | solution.py:922
  500.9 4.0 reduce-scatter.3.cloned.1.call-done
  505.1 52.3 %input_back.1 = (f32[256,2048]{1,0:T(8,128)}, f32[8,2048]{1,0:T(8,128)}) custom-call(bf16[1024,512]{1,0:T(8,128)(2,1)} %get-tuple-element.52.refs_0_.query_raw, bf16[1024,512]{1,0:T(8,128)(2,1)} %get-tuple-element.53.refs_1_.key_raw, bf16[1024,512]{1,0:T(8,128)(2,1)} %get-tuple-element.54.refs_2_.value_raw, ...), custom_call_target="tpu_custom_call" | custom-call | flops 6442450944 | bytes 209715200 | tf_op jit(solution)/shard_map/input_back/pallas_call | solution.py:414
  557.4 0.9 reduce_sum.41
  558.3 0.6 reshape.84.field
  559.0 44.7 %gain_sum.1 = f32[8,512]{1,0:T(8,128)} custom-call(f32[8,512]{1,0:T(8,128)} %reshape.84.field), custom_call_target="tpu_custom_call" | custom-call | tf_op jit(solution)/shard_map/gain_sum/pallas_call | solution.py:467
  603.7 0.7 reshape.85
  604.4 0.7 multiply_subtract_fusion.2
  605.1 15.6 %multiply_subtract_fusion = (f32[3,256,2048]{2,1,0:T(8,128)}, f32[3,256,2048]{2,1,0:T(8,128)}, f32[3,256,2048]{2,1,0:T(8,128)}, f32[3,256,2048]{2,1,0:T(8,128)}) fusion(f32[3,256,2048]{2,1,0:T(8,128)} %param.18, f32[3,256,2048]{2,1,0:T(8,128)} %param.24, f32[3,256,2048]{2,1,0:T(8,128)} %param.21, bf16[3,256,2048]{2,1,0:T(8,128)(2,1)} %reduce-scatter.3.cloned.1.call-done), kind=kLoop, calls=%fused_computation.2 | loop fusion | flops 25165824 | bytes 47185920 | tf_op jit(solution)/shard_map/sub | solution.py:946
  620.8 6.7 %multiply_subtract_fusion.1 = (f32[4,256,512]{2,1,0:T(8,128)}, f32[4,256,512]{2,1,0:T(8,128)}, f32[4,256,512]{2,1,0:T(8,128)}, f32[4,256,512]{2,1,0:T(8,128)}) fusion(f32[4,256,512]{2,1,0:T(8,128)S(1)} %copy-done, f32[4]{0:T(128)S(1)} %copy-done.8, f32[4,256,512]{2,1,0:T(8,128)} %param.23, f32[4,256,512]{2,1,0:T(8,128)} %param.20, ...), kind=kLoop, calls=%fused_computation.6 | loop fusion | flops 8388608 | bytes 15728656 | tf_op jit(solution)/shard_map/sub | solution.py:946
  627.5 1.0 copy.30
  628.5 1.3 copy.31
  (37 shorter events, 0.5 us)
Async XLA Ops:
  7.2 88.9 %all-gather.3.cloned.1.call-start = ((), (), s32[]{:S(2)}) async-start(), calls=%async_computation.2 | async-start | bytes 9437184 | tf_op jit(solution)/shard_map/all_gather | solution.py:978
  9.9 5.1 copy-start.9
  10.0 226.8 %all-gather.5.cloned.1.call-start = ((), (), s32[]{:S(2)}) async-start(), calls=%async_computation.3 | async-start | bytes 28311552 | tf_op jit(solution)/shard_map/all_gather | solution.py:985
  15.0 490.0 %reduce-scatter.3.cloned.1.call-start = ((), (), s32[]{:S(2)}) async-start(), calls=%async_computation.4 | async-start | bytes 28311552 | tf_op jit(solution)/shard_map/reduce_scatter | solution.py:988
  316.4 304.3 %reduce-scatter.5.cloned.1.call-start = ((), (), s32[]{:S(2)}) async-start(), calls=%async_computation.5 | async-start | bytes 9437184 | tf_op jit(solution)/shard_map/reduce_scatter | solution.py:1007
  505.0 53.3 %copy-start.5 = (f32[8,2048]{1,0:T(8,128)S(1)}, f32[8,2048]{1,0:T(8,128)}, u32[]{:S(2)}) copy-start(f32[8,2048]{1,0:T(8,128)} %get-tuple-element.58) | copy-start | bytes 196612
  505.0 99.4 %copy-start.3 = (f32[2,2048]{1,0:T(2,128)S(1)}, f32[2,2048]{1,0:T(2,128)}, u32[]{:S(2)}) copy-start(f32[2,2048]{1,0:T(2,128)} %refs_8_.1) | copy-start | bytes 49156
  505.0 99.4 %copy-start.6 = (f32[2,2048]{1,0:T(2,128)S(1)}, f32[2,2048]{1,0:T(2,128)}, u32[]{:S(2)}) copy-start(f32[2,2048]{1,0:T(2,128)} %param.22) | copy-start | bytes 49156
  505.0 99.4 %copy-start.7 = (f32[2,2048]{1,0:T(2,128)S(1)}, f32[2,2048]{1,0:T(2,128)}, u32[]{:S(2)}) copy-start(f32[2,2048]{1,0:T(2,128)} %param.19) | copy-start | bytes 49156
  604.4 16.3 %copy-start.4 = (f32[2,2048]{1,0:T(2,128)}, f32[2,2048]{1,0:T(2,128)S(1)}, u32[]{:S(2)}) copy-start(f32[2,2048]{1,0:T(2,128)S(1)} %reshape.85) | copy-start | bytes 49156
  605.1 15.6 %copy-start = (f32[4,256,512]{2,1,0:T(8,128)S(1)}, f32[4,256,512]{2,1,0:T(8,128)}, u32[]{:S(2)}) copy-start(f32[4,256,512]{2,1,0:T(8,128)} %param.17) | copy-start | bytes 6291460
  605.1 15.6 %copy-start.8 = (f32[4]{0:T(128)S(1)}, f32[4]{0:T(128)}, u32[]{:S(2)}) copy-start(f32[4]{0:T(128)} %constant.12) | copy-start | bytes 52
  620.7 6.8 %copy-start.2 = (bf16[256,2048]{1,0:T(8,128)(2,1)S(1)}, bf16[256,2048]{1,0:T(8,128)(2,1)}, u32[]{:S(2)}) copy-start(bf16[256,2048]{1,0:T(8,128)(2,1)} %get-tuple-element.92) | copy-start | bytes 3145732
  620.8 7.7 %copy-start.1 = (f32[256,2048]{1,0:T(8,128)S(1)}, f32[256,2048]{1,0:T(8,128)}, u32[]{:S(2)}) copy-start(f32[256,2048]{1,0:T(8,128)} %get-tuple-element.93) | copy-start | bytes 6291460
Sparse Core Ops, SparseCore 0:
  10.5 57.0 all-gather.2
  70.1 125.3 all-gather.4
  316.5 188.4 reduce-scatter.2
  508.3 96.1 reduce-scatter.4

commit v7 on v6

--- a/solution.py
+++ b/solution.py
@@ -59,10 +59,12 @@
     return place + 1 - 2 * (place % 2)
 
 
-def greet(n, me, mate=False):
+def signal_mate(semaphore):
+    pl.semaphore_signal(semaphore, inc=1, device_id={"dp": mate_of()}, device_id_type=MESH)
+
+
+def greet(n, me, here=None):
     barrier = pltpu.get_barrier_semaphore()
-    if mate:
-        pl.semaphore_signal(barrier, inc=1, device_id={"dp": mate_of()}, device_id_type=MESH)
     for there, step in ((me > 0, -1), (me < n - 1, 1)):
 
         @pl.when(there)
@@ -70,7 +72,13 @@
             pl.semaphore_signal(barrier, inc=1, device_id={"tensor": me + step}, device_id_type=MESH)
 
     count = (me > 0).astype(jnp.int32) + (me < n - 1).astype(jnp.int32)
-    pl.semaphore_wait(barrier, count + 1 if mate else count)
+    if here is not None:
+        second_core = lax.axis_index("dp") % 2
+        pl.when(second_core == 0)(lambda: signal_mate(barrier))
+        count = count + second_core
+    pl.semaphore_wait(barrier, count)
+    if here is not None:
+        pl.when(second_core == 1)(lambda: signal_mate(here))
 
 
 def blocks_of(count, body):
@@ -327,7 +335,7 @@
     ]
 
 
-def line_kernel(n, parts, products, extras, outs, gathers, side, finish, *refs):
+def line_kernel(n, parts, products, extras, outs, gathers, side, turn_hop, finish, *refs):
     refs = list(refs)
     take = lambda count: [refs.pop(0) for _ in range(count)]
     lefts, rights, more = take(products), take(products), take(extras)
@@ -354,7 +362,12 @@
 
         blocks_of(part_rows, body)
 
-    greet(n, me)
+    second_core = lax.axis_index("dp") % 2 == 1
+    if turn_hop is None:
+        greet(n, me)
+    else:
+        turns = take(1)[0]
+        greet(n, me, turns.at[1])
     for result in results:
         if result.shape[0] == 8:
             result[...] = jnp.zeros_like(result)
@@ -376,12 +389,21 @@
             pl.loop(0, parts)(lambda part: sums.pass_on(part, count))
         if filler:
             filler.step()
+    if turn_hop is not None:
+        pl.when(second_core)(lambda: pl.semaphore_wait(turns.at[0], 1))
     pl.loop(0, parts)(complete)
     if gathers:
         for hop in range(n - 1):
             if filler:
                 filler.step()
             pl.loop(0, parts)(lambda part: gather.step(part, hop))
+            if hop == turn_hop:
+
+                @pl.when(jnp.logical_not(second_core))
+                def _():
+                    pl.semaphore_wait(turns.at[1], 1)
+                    signal_mate(turns.at[0])
+
         gather.drain()
     if filler:
         filler.close()
@@ -390,7 +412,7 @@
 
 
 def line_exchange(
-    name, collective_id, pairs, extras, outs, rows, width, finish, gathers, parts, side=()
+    name, collective_id, pairs, extras, outs, rows, width, finish, gathers, parts, side=(), turn_hop=None
 ):
     n = lax.axis_size("tensor")
     scratch = scatter_scratch(n, parts, rows, width) if pairs else []
@@ -406,14 +428,15 @@
         outs = outs + [jax.ShapeDtypeStruct((side[0].shape[0], width), jnp.bfloat16)]
         out_specs = out_specs + [pl.BlockSpec(memory_space=pl.ANY)]
         scratch = scratch + side_scratch(width, side[0].shape[1])
+    if turn_hop is not None:
+        scratch = scratch + [pltpu.SemaphoreType.REGULAR((2,))]
     for k, (left, right, which) in enumerate(pairs):
         specs[len(pairs) + k] = pl.BlockSpec(
             (None, *right.shape[1:]), lambda i, which=which: (which, 0, 0), pipeline_mode=pl.Buffered(1)
         )
-    depth = sum(pair[0].shape[1] for pair in pairs)
     return pl.pallas_call(
         functools.partial(
-            line_kernel, n, parts, len(pairs), len(extras), own_outs, gathers, len(side) > 0, finish
+            line_kernel, n, parts, len(pairs), len(extras), own_outs, gathers, len(side) > 0, turn_hop, finish
         ),
         grid=(1,),
         out_shape=outs,
@@ -424,9 +447,7 @@
             collective_id=collective_id, has_side_effects=True, vmem_limit_bytes=60 * 2**20
         ),
         cost_estimate=pl.CostEstimate(
-            flops=2 * n * rows * width * max(depth, 1),
-            bytes_accessed=200 * 2**20,
-            transcendentals=0,
+            flops=2 * n * rows * width, bytes_accessed=rows * width, transcendentals=0
         ),
         name=name,
     )(*operands)
@@ -550,7 +571,7 @@
 def attention_forward_kernel(
     n, parts, first_in, weights, cos_ref, sine_ref, starts_ref, own_rows, layer_in, gains,
     queries, key_rows, values, attended, log_totals, cot_rows, middle, second_in,
-    turned_values, held, held_sems, cot_sent, cot_got, rows_sent, rows_got, turn, totals, run,
+    turned_values, held, held_sems, cot_sent, cot_got, rows_sent, rows_got, turns, totals, run,
     sums_sent, sums_got
 ):
     me = lax.axis_index("tensor")
@@ -565,7 +586,7 @@
         )
 
     fetch(0).start()
-    greet(n, me, True)
+    greet(n, me, turns.at[1])
     cot_gather = RowGather(n, me, 1, cot_rows, cot_sent, cot_got)
     gather = RowGather(n, me, parts, second_in, rows_sent, rows_got)
     sums = SumScatter(
@@ -630,7 +651,7 @@
     def _():
         for hop in range(1, n - 1):
             cot_gather.step(0, hop)
-        pl.semaphore_wait(turn, 1)
+        pl.semaphore_wait(turns.at[0], 1)
 
     sums.begin()
 
@@ -659,7 +680,8 @@
 
     @pl.when(jnp.logical_not(second_core))
     def _():
-        pl.semaphore_signal(turn, inc=1, device_id={"dp": mate_of()}, device_id_type=MESH)
+        pl.semaphore_wait(turns.at[1], 1)
+        signal_mate(turns.at[0])
         cot_gather.step(0, n - 2)
 
     for hop in range(n - 1):
@@ -700,7 +722,7 @@
         ]
         + gather_scratch(n, 1)
         + gather_scratch(n, parts)
-        + [pltpu.SemaphoreType.REGULAR]
+        + [pltpu.SemaphoreType.REGULAR((2,))]
         + scatter_scratch(n, parts, rows, depth),
         compiler_params=pltpu.CompilerParams(
             collective_id=5, has_side_effects=True, vmem_limit_bytes=60 * 2**20
@@ -714,18 +736,39 @@
 
 def attention_back_kernel(
     n, d_attn, out_weight, queries, key_rows, values, attended, log_totals, cos_ref, sine_ref,
-    starts_ref, middle, out_sums, query_raw, key_raw, value_raw, layer_out,
-    d_attended, turned_keys, key_sum, value_sum, held, held_sems, totals, run, sent, got
+    starts_ref, middle, out_sums, first_in, query_raw, key_raw, value_raw, layer_out, grads,
+    d_attended, turned_keys, key_sum, value_sum, held, held_sems, turned_rows, staged, staged_sems,
+    totals, run, sent, got
 ):
     me = lax.axis_index("tensor")
     length, width = queries.shape
     parts = 4
     sums = SumScatter(n, me, parts, [], [], totals, run, sent, got)
 
+    blocks = length // QUERIES
+
     def fetch(block):
+        source = d_attn if block < blocks else first_in
         return pltpu.make_async_copy(
-            d_attn.at[pl.ds(block * QUERIES, QUERIES), :], held.at[block % 2], held_sems.at[block % 2]
+            source.at[pl.ds(block % blocks * QUERIES, QUERIES), :],
+            held.at[block % 2],
+            held_sems.at[block % 2],
         )
+
+    def store(which):
+        return pltpu.make_async_copy(
+            staged.at[which % 2], grads.at[which], staged_sems.at[which % 2]
+        )
+
+    def weight_grad(which, right):
+        @pl.loop(0, turned_rows.shape[0] // 512)
+        def _(block):
+            at = pl.ds(pl.multiple_of(block * 512, 512), 512)
+            staged[which % 2, at, :] = jnp.dot(
+                turned_rows[at, :], right[...], preferred_element_type=jnp.float32
+            ).astype(jnp.bfloat16)
+
+        store(which).start()
 
     ready = pltpu.make_async_copy(out_sums, totals, held_sems.at[2])
     ready.start()
@@ -733,13 +776,21 @@
     greet(n, me)
     ready.wait()
     sums.begin()
-    for block in range(length // QUERIES):
+    for block in range(2 * blocks):
         fetch(block).wait()
-        if (block + 1) * QUERIES < length:
+        if block + 1 < 2 * blocks:
             fetch(block + 1).start()
-        d_attended[block * QUERIES : (block + 1) * QUERIES, :] = jnp.dot(
-            held[block % 2], out_weight[0], preferred_element_type=jnp.float32
-        ).astype(jnp.bfloat16)
+        here = slice(block % blocks * QUERIES, (block % blocks + 1) * QUERIES)
+        source = held[block % 2]
+        if block < blocks:
+            d_attended[here, :] = jnp.dot(
+                source, out_weight[0], preferred_element_type=jnp.float32
+            ).astype(jnp.bfloat16)
+        for k in range(source.shape[1] // TILE):
+            columns = slice(k * TILE, (k + 1) * TILE)
+            turned_rows[columns, here] = source[:, columns].astype(jnp.float32).T.astype(jnp.bfloat16)
+        if block + 1 == blocks:
+            weight_grad(3, attended)
 
     def back_pair(pair):
         lanes = pl.ds(pl.multiple_of(pair * PAIR, PAIR), PAIR)
@@ -783,10 +834,16 @@
         value_raw[:, lanes] = value_sum[...].astype(jnp.bfloat16)
 
     pairs = width // PAIR
-    for count in range(1, n):
-        pl.loop(pairs * (count - 1) // (n - 1), pairs * count // (n - 1))(back_pair)
-        if count < n - 1:
-            pl.loop(0, parts)(lambda part: sums.pass_on(part, count))
+    pl.loop(0, pairs // 2)(back_pair)
+    pl.loop(0, parts)(lambda part: sums.pass_on(part, 1))
+    pl.loop(pairs // 2, pairs)(back_pair)
+    for count in range(2, n - 1):
+        pl.loop(0, parts)(lambda part: sums.pass_on(part, count))
+    weight_grad(0, query_raw)
+    store(3).wait()
+    weight_grad(1, key_raw)
+    store(0).wait()
+    weight_grad(2, value_raw)
     pl.loop(0, parts)(sums.last)
 
     def body(at):
@@ -795,28 +852,36 @@
         layer_out[rows, :] = total.astype(jnp.bfloat16)
 
     blocks_of(middle.shape[0], body)
+    store(1).wait()
+    store(2).wait()
     sums.drain()
 
 
 def attention_back(
     d_attn, attn_low, queries, key_rows, values, attended, log_totals, cos_tile, sine_tile, starts,
-    middle, out_sums
+    middle, out_sums, first_in
 ):
     n = lax.axis_size("tensor")
     length, depth = d_attn.shape
     width, rows = queries.shape[1], middle.shape[0]
     narrow = jax.ShapeDtypeStruct((length, width), jnp.bfloat16)
-    specs = whole_part(12)
-    specs[0] = specs[11] = pl.BlockSpec(memory_space=pl.ANY)
+    specs = whole_part(13)
+    specs[0] = specs[11] = specs[12] = pl.BlockSpec(memory_space=pl.ANY)
     specs[1] = pl.BlockSpec((1, depth, width), lambda i: (3, 0, 0), pipeline_mode=pl.Buffered(1))
     scratch = scatter_scratch(n, 4, rows, depth)
     scratch[0] = pltpu.VMEM((n, rows, depth), jnp.bfloat16)
     return pl.pallas_call(
         functools.partial(attention_back_kernel, n),
         grid=(1,),
-        out_shape=[narrow, narrow, narrow, jax.ShapeDtypeStruct((rows, depth), jnp.bfloat16)],
+        out_shape=[
+            narrow,
+            narrow,
+            narrow,
+            jax.ShapeDtypeStruct((rows, depth), jnp.bfloat16),
+            jax.ShapeDtypeStruct((4, depth, width), jnp.bfloat16),
+        ],
         in_specs=specs,
-        out_specs=whole_part(4),
+        out_specs=whole_part(4) + [pl.BlockSpec(memory_space=pl.ANY)],
         scratch_shapes=[
             pltpu.VMEM((length, width), jnp.bfloat16),
             pltpu.VMEM((PAIR, length), jnp.bfloat16),
@@ -824,18 +889,21 @@
             pltpu.VMEM((length, PAIR), jnp.float32),
             pltpu.VMEM((2, QUERIES, depth), jnp.bfloat16),
             pltpu.SemaphoreType.DMA((3,)),
+            pltpu.VMEM((depth, length), jnp.bfloat16),
+            pltpu.VMEM((2, depth, width), jnp.bfloat16),
+            pltpu.SemaphoreType.DMA((2,)),
         ]
         + scratch,
         compiler_params=pltpu.CompilerParams(
             collective_id=6, has_side_effects=True, vmem_limit_bytes=60 * 2**20
         ),
         cost_estimate=pl.CostEstimate(
-            flops=2 * length * depth * width, bytes_accessed=200 * 2**20, transcendentals=0
+            flops=2 * length * depth, bytes_accessed=length * depth, transcendentals=0
         ),
         name="attention_back",
     )(
         d_attn, attn_low, queries, key_rows, values, attended, log_totals, cos_tile, sine_tile,
-        starts, middle, out_sums.reshape(n, rows, depth)
+        starts, middle, out_sums.reshape(n, rows, depth), first_in
     )
 
 
@@ -898,40 +966,6 @@
         ),
         name="mlp_middle",
     )(second_in, cotangent, weights)
-
-
-def grads_kernel(first_in, query_raw, key_raw, value_raw, d_attn, attended, grads, turned_rows):
-    which = pl.program_id(0)
-    pl.when(which == 0)(lambda: turn_into(turned_rows, first_in))
-    pl.when(which == 3)(lambda: turn_into(turned_rows, d_attn))
-    for k, right in enumerate((query_raw, key_raw, value_raw, attended)):
-
-        @pl.when(which == k)
-        def _():
-            @pl.loop(0, turned_rows.shape[0] // 512)
-            def _(block):
-                at = pl.ds(pl.multiple_of(block * 512, 512), 512)
-                grads[at, :] = jnp.dot(
-                    turned_rows[at, :], right[...], preferred_element_type=jnp.float32
-                ).astype(jnp.bfloat16)
-
-
-def attention_grads(first_in, query_raw, key_raw, value_raw, d_attn, attended):
-    length, depth = first_in.shape
-    width = attended.shape[1]
-    return pl.pallas_call(
-        grads_kernel,
-        grid=(4,),
-        out_shape=jax.ShapeDtypeStruct((4, depth, width), jnp.bfloat16),
-        in_specs=whole_part(6),
-        out_specs=pl.BlockSpec((None, depth, width), lambda j: (j, 0, 0)),
-        scratch_shapes=[pltpu.VMEM((depth, length), jnp.bfloat16)],
-        compiler_params=pltpu.CompilerParams(vmem_limit_bytes=60 * 2**20),
-        cost_estimate=pl.CostEstimate(
-            flops=8 * length * depth * width, bytes_accessed=20 * 2**20, transcendentals=0
-        ),
-        name="attention_grads",
-    )(first_in, query_raw, key_raw, value_raw, d_attn, attended)
 
 
 def attn_rates():
@@ -973,7 +1007,8 @@
     gain_f32 = jax.ShapeDtypeStruct((8, width), jnp.float32)
     exchange = functools.partial(line_exchange, rows=row_count, width=width)
     (first_in,) = exchange(
-        "first_norm", 1, [], [inputs, norm_gains], [], finish=first_norm, gathers=True, parts=4
+        "first_norm", 1, [], [inputs, norm_gains], [], finish=first_norm, gathers=True, parts=4,
+        turn_hop=lax.axis_size("tensor") // 2 - 1,
     )
     attn_low = lax.all_gather(attn_weight.astype(jnp.bfloat16), "dp", axis=1, tiled=True)
 
@@ -997,15 +1032,12 @@
         parts=4,
         side=(hidden, mlp_low),
     )
-    query_raw, key_raw, value_raw, layer_out = attention_back(
+    query_raw, key_raw, value_raw, layer_out, attn_sums = attention_back(
         d_attn, attn_low, queries, key_rows, values, attended, log_totals, cos_tile, sine_tile,
-        starts, middle, out_sums
-    )
-    attn_sums, mlp_owned = lax.optimization_barrier(
-        (attention_grads(first_in, query_raw, key_raw, value_raw, d_attn, attended), mlp_owned)
+        starts, middle, out_sums, first_in
     )
     attn_owned = lax.psum_scatter(attn_sums, "dp", scatter_dimension=1, tiled=True)
-    mlp_grad, attn_grad = mlp_owned.astype(jnp.float32), attn_owned.astype(jnp.float32)
+    mlp_grad = mlp_owned.astype(jnp.float32)
     grad_in, gain_one = exchange(
         "input_back",
         4,
@@ -1021,11 +1053,13 @@
     gain_first_new, gain_second_new, gain_new = adam_update(
         norm_gains, gain_grad, gain_first, gain_second, GAIN_RATE
     )
+    mlp_first_new, mlp_second_new, mlp_new = adam_update(
+        mlp_weight, mlp_grad, mlp_first, mlp_second, 0.5 * D ** (-0.5)
+    )
+    attn_owned, mlp_new = lax.optimization_barrier((attn_owned, mlp_new))
+    attn_grad = attn_owned.astype(jnp.float32)
     attn_first_new, attn_second_new, attn_new = adam_update(
         attn_weight, attn_grad, attn_first, attn_second, attn_rates()
-    )
-    mlp_first_new, mlp_second_new, mlp_new = adam_update(
-        mlp_weight, mlp_grad, mlp_first, mlp_second, 0.5 * D ** (-0.5)
     )
     return (
         layer_out,

time: 640 us -> 616 us (0.963)
  Pallas kernels: 578 us -> 557 us
    pallas_call x1 -> x0, Pallas kernels: 20.5 us -> none  [attention_grads(): pl.pallas_call(grads_kernel, grid=(4,), out_shape=jax.ShapeDtypeStruct((4...]
    pallas_call x3, Pallas kernels: 246 us -> 230 us  [line_exchange(): pl.pallas_call(functools.partial(line_kernel, n, parts, len(pairs), len(e...]
    pallas_call x1, Pallas kernels: 141 us -> 149 us  [attention_forward(): pl.pallas_call(functools.partial(attention_forward_kernel, n, parts), out...]
  transfers between devices with their start and end apart: 4 -> 4, of which waited for: 1 -> 0; matrix products, arithmetic and copies ran while one was open for 4% -> 5% of each run, Pallas kernels for 78% -> 78%
where the time goes in v7:
time: 616 us; the launch traced here: 612 us
  Pallas kernels  557 us (90%)
  other arithmetic  36.3 us (6%)
  between operations  14.2 us (2%)
    pallas_call x3, Pallas kernels, line_exchange(): pl.pallas_call(functools.partial(line_kernel, n, parts, len(pairs), len(e...  230 us
    pallas_call x1, Pallas kernels, attention_forward(): pl.pallas_call(functools.partial(attention_forward_kernel, n, parts), out...  149 us
    pallas_call x1, Pallas kernels, mlp_middle(): pl.pallas_call(mlp_kernel, grid=(units // tile,), out_shape=[wide, wide,...  79.6 us
    pallas_call x1, Pallas kernels, attention_back(): pl.pallas_call(functools.partial(attention_back_kernel, n), grid=(1,), ou...  50.6 us
    pallas_call x1, Pallas kernels, sum_everywhere(): pl.pallas_call(functools.partial(everywhere_kernel, sizes), out_shape=jax...  48.2 us
    sub x3, other arithmetic, adam_update(): weight - step_rate * (first_new / fix_one / (jnp.sqrt(second_new / fix_tw...  23.1 us
  transfers between devices with their start and end apart: 4, of which 0 were waited for; matrix products, arithmetic and copies ran while one was open for 5% of the time, Pallas kernels for 78%

profile of v7, /device:TPU:0, one launch (start us, length us, event | category | flops | bytes accessed | tf_op | source)
XLA Modules:
  0.0 611.8 jit_solution(16765124497388090492)
XLA Ops:
  7.2 2.7 convert_element_type.22
  10.0 4.9 convert_element_type.25
  15.0 0.0 reduce-scatter.5.cloned.1.call-start
  15.0 0.2 reduce-window.4
  15.2 51.7 %first_norm.1.first_in = bf16[1024,2048]{1,0:T(8,128)(2,1)} custom-call(bf16[256,2048]{1,0:T(8,128)(2,1)} %refs_6_.3, f32[2,2048]{1,0:T(2,128)} %refs_8_.1), custom_call_target="tpu_custom_call" | custom-call | flops 4194304 | bytes 524288 | tf_op jit(solution)/shard_map/first_norm/pallas_call | solution.py:437
  66.9 0.1 convert_reduce_fusion
  67.0 0.1 select_reduce_fusion
  67.1 1.9 fusion.2
  69.0 1.8 pad_maximum_fusion
  70.9 0.6 subtract_subtract_fusion.starts_ref
  71.5 148.9 %attention_forward.1 = (bf16[1024,512]{1,0:T(8,128)(2,1)}, bf16[1024,512]{1,0:T(8,128)(2,1)}, bf16[1024,512]{1,0:T(8,128)(2,1)}, bf16[1024,512]{1,0:T(8,128)(2,1...) custom-call(bf16[1024,2048]{1,0:T(8,128)(2,1)} %first_norm.1.first_in,, ...), custom_call_target="tpu_custom_call" | custom-call | flops 8589934592 | bytes 419430400 | tf_op jit(solution)/shard_map/attention_forward/pallas_call | solution.py:713
  220.4 79.6 %mlp_middle.1 = (bf16[1024,2048]{1,0:T(8,128)(2,1)}, bf16[1024,2048]{1,0:T(8,128)(2,1)}, bf16[1024,2048]{1,0:T(8,128)(2,1)}, bf16[3,2048,2048]{2,1,0:T(8,128)(2,1)}) custom-call(bf16[1024,2048]{1,0:T(8,128)(2,1)} %get-tuple-element.39.second_in, bf16[1024,2048]{1,0:T(8,128)(2,1)} %get-tuple-element.40.cotangent, ...), custom_call_target="tpu_custom_call" | custom-call | flops 51539607552 | bytes 62914560 | tf_op jit(solution)/shard_map/mlp_middle/pallas_call | solution.py:956
  300.1 112.6 %mlp_back.1 = (f32[256,2048]{1,0:T(8,128)}, f32[8,2048]{1,0:T(8,128)}, bf16[1024,2048]{1,0:T(8,128)(2,1)}, bf16[1024,2048]{1,0:T(8,128)(2,1)}) custom-call(bf16[1024,2048]{1,0:T(8,128)(2,1)} %get-tuple-element.41.refs_0_, bf16[1024,2048]{1,0:T(8,128)(2,1)} %get-tuple-element.42.refs_1_, ...), custom_call_target="tpu_custom_call" | custom-call | flops 4194304 | bytes 524288 | tf_op jit(solution)/shard_map/mlp_back/pallas_call | solution.py:437
  412.7 50.6 %attention_back.1 = (bf16[1024,512]{1,0:T(8,128)(2,1)}, bf16[1024,512]{1,0:T(8,128)(2,1)}, bf16[1024,512]{1,0:T(8,128)(2,1)}, bf16[256,2048]{1,0:T(8,128)(2,1)}, bf16[4,2048,512]{2,1,0:T(8,128)(2,1)}) custom-call(bf16[1024,2048]{1,0:T(8,128)(2,1)} %get-tuple-element.45.d_attn, ...), custom_call_target="tpu_custom_call" | custom-call | flops 4194304 | bytes 2097152 | tf_op jit(solution)/shard_map/attention_back/pallas_call | solution.py:873
  463.4 65.7 %input_back.1 = (f32[256,2048]{1,0:T(8,128)}, f32[8,2048]{1,0:T(8,128)}) custom-call(bf16[1024,512]{1,0:T(8,128)(2,1)} %get-tuple-element.53.refs_0_, bf16[1024,512]{1,0:T(8,128)(2,1)} %get-tuple-element.54.refs_1_, bf16[1024,512]{1,0:T(8,128)(2,1)} %get-tuple-element.55.refs_2_, ...), custom_call_target="tpu_custom_call" | custom-call | flops 4194304 | bytes 524288 | tf_op jit(solution)/shard_map/input_back/pallas_call | solution.py:437
  529.0 0.9 reduce_sum.41
  530.0 0.6 reshape.84.field
  530.6 48.2 %gain_sum.1 = f32[8,512]{1,0:T(8,128)} custom-call(f32[8,512]{1,0:T(8,128)} %reshape.84.field), custom_call_target="tpu_custom_call" | custom-call | tf_op jit(solution)/shard_map/gain_sum/pallas_call | solution.py:488
  578.8 0.7 reshape.85
  579.6 0.7 multiply_subtract_fusion.2
  580.3 15.7 %multiply_subtract_fusion = (f32[3,256,2048]{2,1,0:T(8,128)}, f32[3,256,2048]{2,1,0:T(8,128)}, f32[3,256,2048]{2,1,0:T(8,128)}, f32[3,256,2048]{2,1,0:T(8,128)}) fusion(f32[3,256,2048]{2,1,0:T(8,128)} %param.18, f32[3,256,2048]{2,1,0:T(8,128)} %param.21, f32[3,256,2048]{2,1,0:T(8,128)} %param.24, bf16[3,256,2048]{2,1,0:T(8,128)(2,1)} %reduce-scatter.5.cloned.1.call-done), kind=kLoop, calls=%fused_computation.2 | loop fusion | flops 25165824 | bytes 47185920 | tf_op jit(solution)/shard_map/sub | solution.py:980
  596.0 6.7 %multiply_subtract_fusion.1 = (f32[4,256,512]{2,1,0:T(8,128)}, f32[4,256,512]{2,1,0:T(8,128)}, f32[4,256,512]{2,1,0:T(8,128)}, f32[4,256,512]{2,1,0:T(8,128)}) fusion(f32[4,256,512]{2,1,0:T(8,128)S(1)} %copy-done, f32[4]{0:T(128)S(1)} %copy-done.8, f32[4,256,512]{2,1,0:T(8,128)} %param.23, f32[4,256,512]{2,1,0:T(8,128)} %param.20, ...), kind=kLoop, calls=%fused_computation.6 | loop fusion | flops 8388608 | bytes 15728656 | tf_op jit(solution)/shard_map/sub | solution.py:980
  602.8 1.0 copy.30
  603.7 1.3 copy.31
  (36 shorter events, 0.3 us)
Async XLA Ops:
  7.2 64.3 %all-gather.3.cloned.1.call-start = ((), (), s32[]{:S(2)}) async-start(), calls=%async_computation.2 | async-start | bytes 9437184 | tf_op jit(solution)/shard_map/all_gather | solution.py:1013
  9.9 5.1 copy-start.9
  10.0 210.4 %all-gather.5.cloned.1.call-start = ((), (), s32[]{:S(2)}) async-start(), calls=%async_computation.3 | async-start | bytes 28311552 | tf_op jit(solution)/shard_map/all_gather | solution.py:1020
  15.0 565.3 %reduce-scatter.5.cloned.1.call-start = ((), (), s32[]{:S(2)}) async-start(), calls=%async_computation.5 | async-start | bytes 28311552 | tf_op jit(solution)/shard_map/reduce_scatter | solution.py:1023
  300.0 296.0 %reduce-scatter.3.cloned.1.call-start = ((), (), s32[]{:S(2)}) async-start(), calls=%async_computation.4 | async-start | bytes 9437184 | tf_op jit(solution)/shard_map/reduce_scatter | solution.py:1039
  463.3 66.6 %copy-start.5 = (f32[8,2048]{1,0:T(8,128)S(1)}, f32[8,2048]{1,0:T(8,128)}, u32[]{:S(2)}) copy-start(f32[8,2048]{1,0:T(8,128)} %get-tuple-element.59) | copy-start | bytes 196612
  463.3 116.2 %copy-start.3 = (f32[2,2048]{1,0:T(2,128)S(1)}, f32[2,2048]{1,0:T(2,128)}, u32[]{:S(2)}) copy-start(f32[2,2048]{1,0:T(2,128)} %refs_8_.1) | copy-start | bytes 49156
  463.3 116.2 %copy-start.6 = (f32[2,2048]{1,0:T(2,128)S(1)}, f32[2,2048]{1,0:T(2,128)}, u32[]{:S(2)}) copy-start(f32[2,2048]{1,0:T(2,128)} %param.22) | copy-start | bytes 49156
  463.3 116.2 %copy-start.7 = (f32[2,2048]{1,0:T(2,128)S(1)}, f32[2,2048]{1,0:T(2,128)}, u32[]{:S(2)}) copy-start(f32[2,2048]{1,0:T(2,128)} %param.19) | copy-start | bytes 49156
  579.6 16.4 %copy-start.4 = (f32[2,2048]{1,0:T(2,128)}, f32[2,2048]{1,0:T(2,128)S(1)}, u32[]{:S(2)}) copy-start(f32[2,2048]{1,0:T(2,128)S(1)} %reshape.85) | copy-start | bytes 49156
  580.3 15.7 %copy-start = (f32[4,256,512]{2,1,0:T(8,128)S(1)}, f32[4,256,512]{2,1,0:T(8,128)}, u32[]{:S(2)}) copy-start(f32[4,256,512]{2,1,0:T(8,128)} %param.17) | copy-start | bytes 6291460
  580.3 15.7 %copy-start.8 = (f32[4]{0:T(128)S(1)}, f32[4]{0:T(128)}, u32[]{:S(2)}) copy-start(f32[4]{0:T(128)} %constant.12) | copy-start | bytes 52
  596.0 6.7 %copy-start.2 = (bf16[256,2048]{1,0:T(8,128)(2,1)S(1)}, bf16[256,2048]{1,0:T(8,128)(2,1)}, u32[]{:S(2)}) copy-start(bf16[256,2048]{1,0:T(8,128)(2,1)} %get-tuple-element.94) | copy-start | bytes 3145732
  596.0 7.7 %copy-start.1 = (f32[256,2048]{1,0:T(8,128)S(1)}, f32[256,2048]{1,0:T(8,128)}, u32[]{:S(2)}) copy-start(f32[256,2048]{1,0:T(8,128)} %get-tuple-element.95) | copy-start | bytes 6291460
Sparse Core Ops, SparseCore 0:
  10.5 57.0 all-gather.2
  70.1 125.3 all-gather.4
  300.2 198.2 reduce-scatter.4
  501.7 81.3 reduce-scatter.2

commit v8 on v7

--- a/solution.py
+++ b/solution.py
@@ -186,11 +186,12 @@
         for hop in range(self.n - 1):
             for way, dest in ((0, self.n - 1 - hop), (1, hop)):
                 needed = (dest > self.me, dest < self.me)[way]
-                if self.lefts:
-                    pl.when(needed)(lambda: self.product(dest))
 
                 @pl.when(needed & jnp.logical_not(self.fed[way]))
                 def _():
+                    if self.lefts:
+                        self.product(dest)
+
                     @pl.loop(0, self.parts)
                     def _(part):
                         slot = self.place(way, part, hop)
@@ -203,8 +204,12 @@
                         blocks_of(part_rows, body)
                         self.copy(way, part, hop).start()
 
-        if self.lefts:
+    def prepare(self, count):
+        if count == self.n - 1:
             self.product(self.me)
+        else:
+            for way, hop, dest, there in self.arrivals(count):
+                pl.when(there)(lambda: self.product(dest))
 
     def arrivals(self, count):
         for way, behind in ((0, self.me), (1, self.n - 1 - self.me)):
@@ -384,9 +389,9 @@
 
     if products:
         for count in range(1, n - 1):
-            if filler:
-                filler.step()
+            sums.prepare(count)
             pl.loop(0, parts)(lambda part: sums.pass_on(part, count))
+        sums.prepare(n - 1)
         if filler:
             filler.step()
     if turn_hop is not None:
@@ -586,7 +591,7 @@
         )
 
     fetch(0).start()
-    greet(n, me, turns.at[1])
+    greet(n, me)
     cot_gather = RowGather(n, me, 1, cot_rows, cot_sent, cot_got)
     gather = RowGather(n, me, parts, second_in, rows_sent, rows_got)
     sums = SumScatter(
@@ -651,7 +656,6 @@
     def _():
         for hop in range(1, n - 1):
             cot_gather.step(0, hop)
-        pl.semaphore_wait(turns.at[0], 1)
 
     sums.begin()
 
@@ -673,16 +677,14 @@
         gather.start(part)
 
     for count in range(1, n - 1):
+        sums.prepare(count)
         pl.loop(0, parts)(lambda part: sums.pass_on(part, count))
         if count < n - 2:
             pl.when(jnp.logical_not(second_core))(lambda: cot_gather.step(0, count))
+    sums.prepare(n - 1)
     pl.loop(0, parts)(complete)
 
-    @pl.when(jnp.logical_not(second_core))
-    def _():
-        pl.semaphore_wait(turns.at[1], 1)
-        signal_mate(turns.at[0])
-        cot_gather.step(0, n - 2)
+    pl.when(jnp.logical_not(second_core))(lambda: cot_gather.step(0, n - 2))
 
     for hop in range(n - 1):
         pl.loop(0, parts)(lambda part: gather.step(part, hop))

time: 616 us -> 609 us (0.989)
  Pallas kernels: 557 us -> 550 us
    pallas_call x3, Pallas kernels: 230 us -> 218 us  [line_exchange(): pl.pallas_call(functools.partial(line_kernel, n, parts, len(pairs), len(e...]
    pallas_call x1, Pallas kernels: 48.2 us -> 55.1 us  [sum_everywhere(): pl.pallas_call(functools.partial(everywhere_kernel, sizes), out_shape=jax...]
where the time goes in v8:
time: 609 us; the launch traced here: 605 us
  Pallas kernels  550 us (90%)
  other arithmetic  36.3 us (6%)
  between operations  14.3 us (2%)
    pallas_call x3, Pallas kernels, line_exchange(): pl.pallas_call(functools.partial(line_kernel, n, parts, len(pairs), len(e...  218 us
    pallas_call x1, Pallas kernels, attention_forward(): pl.pallas_call(functools.partial(attention_forward_kernel, n, parts), out...  147 us
    pallas_call x1, Pallas kernels, mlp_middle(): pl.pallas_call(mlp_kernel, grid=(units // tile,), out_shape=[wide, wide,...  79.6 us
    pallas_call x1, Pallas kernels, sum_everywhere(): pl.pallas_call(functools.partial(everywhere_kernel, sizes), out_shape=jax...  55.1 us
    pallas_call x1, Pallas kernels, attention_back(): pl.pallas_call(functools.partial(attention_back_kernel, n), grid=(1,), ou...  50.8 us
    sub x3, other arithmetic, adam_update(): weight - step_rate * (first_new / fix_one / (jnp.sqrt(second_new / fix_tw...  23.1 us
  transfers between devices with their start and end apart: 4, of which 0 were waited for; matrix products, arithmetic and copies ran while one was open for 5% of the time, Pallas kernels for 78%

profile of v8, /device:TPU:0, one launch (start us, length us, event | category | flops | bytes accessed | tf_op | source)
XLA Modules:
  0.0 604.7 jit_solution(15863916595708156525)
XLA Ops:
  7.2 2.7 convert_element_type.22
  10.0 4.9 convert_element_type.25
  15.0 0.2 reduce-window.4
  15.2 51.7 %first_norm.1.first_in = bf16[1024,2048]{1,0:T(8,128)(2,1)} custom-call(bf16[256,2048]{1,0:T(8,128)(2,1)} %refs_6_.3, f32[2,2048]{1,0:T(2,128)} %refs_8_.1), custom_call_target="tpu_custom_call" | custom-call | flops 4194304 | bytes 524288 | tf_op jit(solution)/shard_map/first_norm/pallas_call | solution.py:442
  66.9 0.1 convert_reduce_fusion
  67.0 0.1 select_reduce_fusion
  67.1 1.9 fusion.2
  69.0 1.8 pad_maximum_fusion
  70.9 0.6 subtract_subtract_fusion.starts_ref
  71.5 147.0 %attention_forward.1 = (bf16[1024,512]{1,0:T(8,128)(2,1)}, bf16[1024,512]{1,0:T(8,128)(2,1)}, bf16[1024,512]{1,0:T(8,128)(2,1)}, bf16[1024,512]{1,0:T(8,128)(2,1...) custom-call(bf16[1024,2048]{1,0:T(8,128)(2,1)} %first_norm.1.first_in,, ...), custom_call_target="tpu_custom_call" | custom-call | flops 8589934592 | bytes 419430400 | tf_op jit(solution)/shard_map/attention_forward/pallas_call | solution.py:715
  218.5 79.6 %mlp_middle.1 = (bf16[1024,2048]{1,0:T(8,128)(2,1)}, bf16[1024,2048]{1,0:T(8,128)(2,1)}, bf16[1024,2048]{1,0:T(8,128)(2,1)}, bf16[3,2048,2048]{2,1,0:T(8,128)(2,1)}) custom-call(bf16[1024,2048]{1,0:T(8,128)(2,1)} %get-tuple-element.39.second_in, bf16[1024,2048]{1,0:T(8,128)(2,1)} %get-tuple-element.40.cotangent, ...), custom_call_target="tpu_custom_call" | custom-call | flops 51539607552 | bytes 62914560 | tf_op jit(solution)/shard_map/mlp_middle/pallas_call | solution.py:958
  298.1 0.0 reduce-scatter.3.cloned.1.call-start
  298.2 101.3 %mlp_back.1 = (f32[256,2048]{1,0:T(8,128)}, f32[8,2048]{1,0:T(8,128)}, bf16[1024,2048]{1,0:T(8,128)(2,1)}, bf16[1024,2048]{1,0:T(8,128)(2,1)}) custom-call(bf16[1024,2048]{1,0:T(8,128)(2,1)} %get-tuple-element.41.refs_0_, bf16[1024,2048]{1,0:T(8,128)(2,1)} %get-tuple-element.42.refs_1_, ...), custom_call_target="tpu_custom_call" | custom-call | flops 4194304 | bytes 524288 | tf_op jit(solution)/shard_map/mlp_back/pallas_call | solution.py:442
  399.4 50.8 %attention_back.1 = (bf16[1024,512]{1,0:T(8,128)(2,1)}, bf16[1024,512]{1,0:T(8,128)(2,1)}, bf16[1024,512]{1,0:T(8,128)(2,1)}, bf16[256,2048]{1,0:T(8,128)(2,1)}, bf16[4,2048,512]{2,1,0:T(8,128)(2,1)}) custom-call(bf16[1024,2048]{1,0:T(8,128)(2,1)} %get-tuple-element.45.d_attn, ...), custom_call_target="tpu_custom_call" | custom-call | flops 4194304 | bytes 2097152 | tf_op jit(solution)/shard_map/attention_back/pallas_call | solution.py:875
  450.3 64.7 %input_back.1 = (f32[256,2048]{1,0:T(8,128)}, f32[8,2048]{1,0:T(8,128)}) custom-call(bf16[1024,512]{1,0:T(8,128)(2,1)} %get-tuple-element.53.refs_0_, bf16[1024,512]{1,0:T(8,128)(2,1)} %get-tuple-element.54.refs_1_, bf16[1024,512]{1,0:T(8,128)(2,1)} %get-tuple-element.55.refs_2_, ...), custom_call_target="tpu_custom_call" | custom-call | flops 4194304 | bytes 524288 | tf_op jit(solution)/shard_map/input_back/pallas_call | solution.py:442
  515.0 0.9 reduce_sum.41
  516.0 0.6 reshape.84.field
  516.6 55.1 %gain_sum.1 = f32[8,512]{1,0:T(8,128)} custom-call(f32[8,512]{1,0:T(8,128)} %reshape.84.field), custom_call_target="tpu_custom_call" | custom-call | tf_op jit(solution)/shard_map/gain_sum/pallas_call | solution.py:493
  571.7 0.7 reshape.85
  572.4 0.7 multiply_subtract_fusion.2
  573.1 15.7 %multiply_subtract_fusion = (f32[3,256,2048]{2,1,0:T(8,128)}, f32[3,256,2048]{2,1,0:T(8,128)}, f32[3,256,2048]{2,1,0:T(8,128)}, f32[3,256,2048]{2,1,0:T(8,128)}) fusion(f32[3,256,2048]{2,1,0:T(8,128)} %param.18, f32[3,256,2048]{2,1,0:T(8,128)} %param.21, f32[3,256,2048]{2,1,0:T(8,128)} %param.24, bf16[3,256,2048]{2,1,0:T(8,128)(2,1)} %reduce-scatter.5.cloned.1.call-done), kind=kLoop, calls=%fused_computation.2 | loop fusion | flops 25165824 | bytes 47185920 | tf_op jit(solution)/shard_map/sub | solution.py:982
  588.9 6.7 %multiply_subtract_fusion.1 = (f32[4,256,512]{2,1,0:T(8,128)}, f32[4,256,512]{2,1,0:T(8,128)}, f32[4,256,512]{2,1,0:T(8,128)}, f32[4,256,512]{2,1,0:T(8,128)}) fusion(f32[4,256,512]{2,1,0:T(8,128)S(1)} %copy-done, f32[4]{0:T(128)S(1)} %copy-done.8, f32[4,256,512]{2,1,0:T(8,128)} %param.23, f32[4,256,512]{2,1,0:T(8,128)} %param.20, ...), kind=kLoop, calls=%fused_computation.6 | loop fusion | flops 8388608 | bytes 15728656 | tf_op jit(solution)/shard_map/sub | solution.py:982
  595.6 1.0 copy.30
  596.6 1.3 copy.31
  (36 shorter events, 0.3 us)
Async XLA Ops:
  7.2 64.3 %all-gather.3.cloned.1.call-start = ((), (), s32[]{:S(2)}) async-start(), calls=%async_computation.2 | async-start | bytes 9437184 | tf_op jit(solution)/shard_map/all_gather | solution.py:1015
  9.9 5.1 copy-start.9
  10.0 208.5 %all-gather.5.cloned.1.call-start = ((), (), s32[]{:S(2)}) async-start(), calls=%async_computation.3 | async-start | bytes 28311552 | tf_op jit(solution)/shard_map/all_gather | solution.py:1022
  15.0 558.2 %reduce-scatter.5.cloned.1.call-start = ((), (), s32[]{:S(2)}) async-start(), calls=%async_computation.5 | async-start | bytes 28311552 | tf_op jit(solution)/shard_map/reduce_scatter | solution.py:1025
  298.1 290.7 %reduce-scatter.3.cloned.1.call-start = ((), (), s32[]{:S(2)}) async-start(), calls=%async_computation.4 | async-start | bytes 9437184 | tf_op jit(solution)/shard_map/reduce_scatter | solution.py:1041
  450.2 65.7 %copy-start.5 = (f32[8,2048]{1,0:T(8,128)S(1)}, f32[8,2048]{1,0:T(8,128)}, u32[]{:S(2)}) copy-start(f32[8,2048]{1,0:T(8,128)} %get-tuple-element.59) | copy-start | bytes 196612
  450.2 122.2 %copy-start.3 = (f32[2,2048]{1,0:T(2,128)S(1)}, f32[2,2048]{1,0:T(2,128)}, u32[]{:S(2)}) copy-start(f32[2,2048]{1,0:T(2,128)} %refs_8_.1) | copy-start | bytes 49156
  450.3 122.2 %copy-start.6 = (f32[2,2048]{1,0:T(2,128)S(1)}, f32[2,2048]{1,0:T(2,128)}, u32[]{:S(2)}) copy-start(f32[2,2048]{1,0:T(2,128)} %param.22) | copy-start | bytes 49156
  450.3 122.2 %copy-start.7 = (f32[2,2048]{1,0:T(2,128)S(1)}, f32[2,2048]{1,0:T(2,128)}, u32[]{:S(2)}) copy-start(f32[2,2048]{1,0:T(2,128)} %param.19) | copy-start | bytes 49156
  572.4 16.4 %copy-start.4 = (f32[2,2048]{1,0:T(2,128)}, f32[2,2048]{1,0:T(2,128)S(1)}, u32[]{:S(2)}) copy-start(f32[2,2048]{1,0:T(2,128)S(1)} %reshape.85) | copy-start | bytes 49156
  573.1 15.7 %copy-start = (f32[4,256,512]{2,1,0:T(8,128)S(1)}, f32[4,256,512]{2,1,0:T(8,128)}, u32[]{:S(2)}) copy-start(f32[4,256,512]{2,1,0:T(8,128)} %param.17) | copy-start | bytes 6291460
  573.1 15.7 %copy-start.8 = (f32[4]{0:T(128)S(1)}, f32[4]{0:T(128)}, u32[]{:S(2)}) copy-start(f32[4]{0:T(128)} %constant.12) | copy-start | bytes 52
  588.9 6.7 %copy-start.2 = (bf16[256,2048]{1,0:T(8,128)(2,1)S(1)}, bf16[256,2048]{1,0:T(8,128)(2,1)}, u32[]{:S(2)}) copy-start(bf16[256,2048]{1,0:T(8,128)(2,1)} %get-tuple-element.94) | copy-start | bytes 3145732
  588.9 7.7 %copy-start.1 = (f32[256,2048]{1,0:T(8,128)S(1)}, f32[256,2048]{1,0:T(8,128)}, u32[]{:S(2)}) copy-start(f32[256,2048]{1,0:T(8,128)} %get-tuple-element.95) | copy-start | bytes 6291460
Sparse Core Ops, SparseCore 0:
  10.5 57.0 all-gather.2
  70.1 125.3 all-gather.4
  298.2 199.9 reduce-scatter.4
  501.5 76.5 reduce-scatter.2

commit v9 on v8

--- a/solution.py
+++ b/solution.py
@@ -838,9 +838,12 @@
     pairs = width // PAIR
     pl.loop(0, pairs // 2)(back_pair)
     pl.loop(0, parts)(lambda part: sums.pass_on(part, 1))
-    pl.loop(pairs // 2, pairs)(back_pair)
+    late = max(pairs // 2 + 1, 3 * pairs // 4)
+    pl.loop(pairs // 2, late)(back_pair)
     for count in range(2, n - 1):
         pl.loop(0, parts)(lambda part: sums.pass_on(part, count))
+    if late < pairs:
+        pl.loop(late, pairs)(back_pair)
     weight_grad(0, query_raw)
     store(3).wait()
     weight_grad(1, key_raw)

time: 609 us -> 612 us (level)
  no operation moved by 1% of the time
where the time goes in v9:
time: 612 us; the launch traced here: 608 us
  Pallas kernels  554 us (91%)
  other arithmetic  36.3 us (6%)
  between operations  14.3 us (2%)
    pallas_call x3, Pallas kernels, line_exchange(): pl.pallas_call(functools.partial(line_kernel, n, parts, len(pairs), len(e...  222 us
    pallas_call x1, Pallas kernels, attention_forward(): pl.pallas_call(functools.partial(attention_forward_kernel, n, parts), out...  147 us
    pallas_call x1, Pallas kernels, mlp_middle(): pl.pallas_call(mlp_kernel, grid=(units // tile,), out_shape=[wide, wide,...  79.6 us
    pallas_call x1, Pallas kernels, sum_everywhere(): pl.pallas_call(functools.partial(everywhere_kernel, sizes), out_shape=jax...  55 us
    pallas_call x1, Pallas kernels, attention_back(): pl.pallas_call(functools.partial(attention_back_kernel, n), grid=(1,), ou...  49.9 us
    sub x3, other arithmetic, adam_update(): weight - step_rate * (first_new / fix_one / (jnp.sqrt(second_new / fix_tw...  23.1 us
  transfers between devices with their start and end apart: 4, of which 0 were waited for; matrix products, arithmetic and copies ran while one was open for 5% of the time, Pallas kernels for 78%

profile of v9, /device:TPU:0, one launch (start us, length us, event | category | flops | bytes accessed | tf_op | source)
XLA Modules:
  0.0 608.1 jit_solution(8455995533204931259)
XLA Ops:
  7.2 2.7 convert_element_type.22
  10.0 4.9 convert_element_type.25
  15.0 0.0 reduce-scatter.5.cloned.1.call-start
  15.0 0.2 reduce-window.4
  15.2 51.7 %first_norm.1.first_in = bf16[1024,2048]{1,0:T(8,128)(2,1)} custom-call(bf16[256,2048]{1,0:T(8,128)(2,1)} %refs_6_.3, f32[2,2048]{1,0:T(2,128)} %refs_8_.1), custom_call_target="tpu_custom_call" | custom-call | flops 4194304 | bytes 524288 | tf_op jit(solution)/shard_map/first_norm/pallas_call | solution.py:442
  66.9 0.1 convert_reduce_fusion
  67.0 0.1 select_reduce_fusion
  67.1 1.9 fusion.2
  69.0 1.8 pad_maximum_fusion
  70.9 0.6 subtract_subtract_fusion.starts_ref
  71.5 147.2 %attention_forward.1 = (bf16[1024,512]{1,0:T(8,128)(2,1)}, bf16[1024,512]{1,0:T(8,128)(2,1)}, bf16[1024,512]{1,0:T(8,128)(2,1)}, bf16[1024,512]{1,0:T(8,128)(2,1...) custom-call(bf16[1024,2048]{1,0:T(8,128)(2,1)} %first_norm.1.first_in,, ...), custom_call_target="tpu_custom_call" | custom-call | flops 8589934592 | bytes 419430400 | tf_op jit(solution)/shard_map/attention_forward/pallas_call | solution.py:715
  218.8 79.6 %mlp_middle.1 = (bf16[1024,2048]{1,0:T(8,128)(2,1)}, bf16[1024,2048]{1,0:T(8,128)(2,1)}, bf16[1024,2048]{1,0:T(8,128)(2,1)}, bf16[3,2048,2048]{2,1,0:T(8,128)(2,1)}) custom-call(bf16[1024,2048]{1,0:T(8,128)(2,1)} %get-tuple-element.39.second_in, bf16[1024,2048]{1,0:T(8,128)(2,1)} %get-tuple-element.40.cotangent, ...), custom_call_target="tpu_custom_call" | custom-call | flops 51539607552 | bytes 62914560 | tf_op jit(solution)/shard_map/mlp_middle/pallas_call | solution.py:961
  298.5 101.5 %mlp_back.1 = (f32[256,2048]{1,0:T(8,128)}, f32[8,2048]{1,0:T(8,128)}, bf16[1024,2048]{1,0:T(8,128)(2,1)}, bf16[1024,2048]{1,0:T(8,128)(2,1)}) custom-call(bf16[1024,2048]{1,0:T(8,128)(2,1)} %get-tuple-element.41.refs_0_, bf16[1024,2048]{1,0:T(8,128)(2,1)} %get-tuple-element.42.refs_1_, ...), custom_call_target="tpu_custom_call" | custom-call | flops 4194304 | bytes 524288 | tf_op jit(solution)/shard_map/mlp_back/pallas_call | solution.py:442
  400.0 49.9 %attention_back.1 = (bf16[1024,512]{1,0:T(8,128)(2,1)}, bf16[1024,512]{1,0:T(8,128)(2,1)}, bf16[1024,512]{1,0:T(8,128)(2,1)}, bf16[256,2048]{1,0:T(8,128)(2,1)}, bf16[4,2048,512]{2,1,0:T(8,128)(2,1)}) custom-call(bf16[1024,2048]{1,0:T(8,128)(2,1)} %get-tuple-element.45.d_attn, ...), custom_call_target="tpu_custom_call" | custom-call | flops 4194304 | bytes 2097152 | tf_op jit(solution)/shard_map/attention_back/pallas_call | solution.py:878
  449.9 68.6 %input_back.1 = (f32[256,2048]{1,0:T(8,128)}, f32[8,2048]{1,0:T(8,128)}) custom-call(bf16[1024,512]{1,0:T(8,128)(2,1)} %get-tuple-element.53.refs_0_, bf16[1024,512]{1,0:T(8,128)(2,1)} %get-tuple-element.54.refs_1_, bf16[1024,512]{1,0:T(8,128)(2,1)} %get-tuple-element.55.refs_2_, ...), custom_call_target="tpu_custom_call" | custom-call | flops 4194304 | bytes 524288 | tf_op jit(solution)/shard_map/input_back/pallas_call | solution.py:442
  518.5 0.9 reduce_sum.41
  519.5 0.6 reshape.84.field
  520.1 55.0 %gain_sum.1 = f32[8,512]{1,0:T(8,128)} custom-call(f32[8,512]{1,0:T(8,128)} %reshape.84.field), custom_call_target="tpu_custom_call" | custom-call | tf_op jit(solution)/shard_map/gain_sum/pallas_call | solution.py:493
  575.1 0.7 reshape.85
  575.9 0.7 multiply_subtract_fusion.2
  576.6 15.7 %multiply_subtract_fusion = (f32[3,256,2048]{2,1,0:T(8,128)}, f32[3,256,2048]{2,1,0:T(8,128)}, f32[3,256,2048]{2,1,0:T(8,128)}, f32[3,256,2048]{2,1,0:T(8,128)}) fusion(f32[3,256,2048]{2,1,0:T(8,128)} %param.18, f32[3,256,2048]{2,1,0:T(8,128)} %param.21, f32[3,256,2048]{2,1,0:T(8,128)} %param.24, bf16[3,256,2048]{2,1,0:T(8,128)(2,1)} %reduce-scatter.5.cloned.1.call-done), kind=kLoop, calls=%fused_computation.2 | loop fusion | flops 25165824 | bytes 47185920 | tf_op jit(solution)/shard_map/sub | solution.py:985
  592.3 6.7 %multiply_subtract_fusion.1 = (f32[4,256,512]{2,1,0:T(8,128)}, f32[4,256,512]{2,1,0:T(8,128)}, f32[4,256,512]{2,1,0:T(8,128)}, f32[4,256,512]{2,1,0:T(8,128)}) fusion(f32[4,256,512]{2,1,0:T(8,128)S(1)} %copy-done, f32[4]{0:T(128)S(1)} %copy-done.8, f32[4,256,512]{2,1,0:T(8,128)} %param.23, f32[4,256,512]{2,1,0:T(8,128)} %param.20, ...), kind=kLoop, calls=%fused_computation.6 | loop fusion | flops 8388608 | bytes 15728656 | tf_op jit(solution)/shard_map/sub | solution.py:985
  599.1 1.0 copy.30
  600.0 1.3 copy.31
  (36 shorter events, 0.3 us)
Async XLA Ops:
  7.2 64.3 %all-gather.3.cloned.1.call-start = ((), (), s32[]{:S(2)}) async-start(), calls=%async_computation.2 | async-start | bytes 9437184 | tf_op jit(solution)/shard_map/all_gather | solution.py:1018
  9.9 5.1 copy-start.9
  10.0 208.8 %all-gather.5.cloned.1.call-start = ((), (), s32[]{:S(2)}) async-start(), calls=%async_computation.3 | async-start | bytes 28311552 | tf_op jit(solution)/shard_map/all_gather | solution.py:1025
  15.0 561.6 %reduce-scatter.5.cloned.1.call-start = ((), (), s32[]{:S(2)}) async-start(), calls=%async_computation.5 | async-start | bytes 28311552 | tf_op jit(solution)/shard_map/reduce_scatter | solution.py:1028
  298.4 293.9 %reduce-scatter.3.cloned.1.call-start = ((), (), s32[]{:S(2)}) async-start(), calls=%async_computation.4 | async-start | bytes 9437184 | tf_op jit(solution)/shard_map/reduce_scatter | solution.py:1044
  449.9 69.5 %copy-start.5 = (f32[8,2048]{1,0:T(8,128)S(1)}, f32[8,2048]{1,0:T(8,128)}, u32[]{:S(2)}) copy-start(f32[8,2048]{1,0:T(8,128)} %get-tuple-element.59) | copy-start | bytes 196612
  449.9 126.0 %copy-start.3 = (f32[2,2048]{1,0:T(2,128)S(1)}, f32[2,2048]{1,0:T(2,128)}, u32[]{:S(2)}) copy-start(f32[2,2048]{1,0:T(2,128)} %refs_8_.1) | copy-start | bytes 49156
  449.9 126.0 %copy-start.6 = (f32[2,2048]{1,0:T(2,128)S(1)}, f32[2,2048]{1,0:T(2,128)}, u32[]{:S(2)}) copy-start(f32[2,2048]{1,0:T(2,128)} %param.22) | copy-start | bytes 49156
  449.9 125.9 %copy-start.7 = (f32[2,2048]{1,0:T(2,128)S(1)}, f32[2,2048]{1,0:T(2,128)}, u32[]{:S(2)}) copy-start(f32[2,2048]{1,0:T(2,128)} %param.19) | copy-start | bytes 49156
  575.9 16.4 %copy-start.4 = (f32[2,2048]{1,0:T(2,128)}, f32[2,2048]{1,0:T(2,128)S(1)}, u32[]{:S(2)}) copy-start(f32[2,2048]{1,0:T(2,128)S(1)} %reshape.85) | copy-start | bytes 49156
  576.6 15.7 %copy-start = (f32[4,256,512]{2,1,0:T(8,128)S(1)}, f32[4,256,512]{2,1,0:T(8,128)}, u32[]{:S(2)}) copy-start(f32[4,256,512]{2,1,0:T(8,128)} %param.17) | copy-start | bytes 6291460
  576.6 15.7 %copy-start.8 = (f32[4]{0:T(128)S(1)}, f32[4]{0:T(128)}, u32[]{:S(2)}) copy-start(f32[4]{0:T(128)} %constant.12) | copy-start | bytes 52
  592.3 6.7 %copy-start.2 = (bf16[256,2048]{1,0:T(8,128)(2,1)S(1)}, bf16[256,2048]{1,0:T(8,128)(2,1)}, u32[]{:S(2)}) copy-start(bf16[256,2048]{1,0:T(8,128)(2,1)} %get-tuple-element.94) | copy-start | bytes 3145732
  592.3 7.7 %copy-start.1 = (f32[256,2048]{1,0:T(8,128)S(1)}, f32[256,2048]{1,0:T(8,128)}, u32[]{:S(2)}) copy-start(f32[256,2048]{1,0:T(8,128)} %get-tuple-element.95) | copy-start | bytes 6291460
Sparse Core Ops, SparseCore 0:
  10.5 57.0 all-gather.2
  70.1 125.3 all-gather.4
  298.5 199.7 reduce-scatter.4
  501.6 80.0 reduce-scatter.2
